TPU v7x, 32 devices: a whole 2x2x4 slice. The times are simulated.
32 devices in a mesh: dp: 16 (over z, y, x), fsdp: 2 (over core).
Axes of the slice: x: 2, y: 2, z: 4, core: 2. Of those that a mesh axis runs over, the one named last changes fastest.
Arguments:
- tokens_in: bfloat16 [32, 576, 768], P(('dp', 'fsdp')), may hold values from -6 to 6
- cotangent: bfloat16 [32, 576, 768], P(('dp', 'fsdp')), may hold values from -6 to 6
- segments: int32 [32, 576], P(('dp', 'fsdp')), may hold values from 0 to 3, as said below
- tile_sides: int32 [32, 576], P(('dp', 'fsdp')), may hold values from 1 to 15, as said below
- valid_slots: int32 [32, 576], P(('dp', 'fsdp')), may hold values from 0 to 1, as said below
- owners: int32 [32], replicated, may hold values from 0 to 31, as said below
- master_qkv: float32 [768, 2304], P(('dp', 'fsdp')), may hold values from -0.21875 to 0.21875
- master_out: float32 [768, 768], P(('dp', 'fsdp')), may hold values from -0.625 to 0.625
- master_up: float32 [768, 3072], P(('dp', 'fsdp')), may hold values from -0.21875 to 0.21875
- master_down: float32 [3072, 768], P(('dp', 'fsdp')), may hold values from -0.109375 to 0.109375
- master_vec: float32 [7680], P(('dp', 'fsdp'))
- first_qkv: float32 [768, 2304], P(('dp', 'fsdp')), may hold values from -56 to 56
- first_out: float32 [768, 768], P(('dp', 'fsdp')), may hold values from -40 to 40
- first_up: float32 [768, 3072], P(('dp', 'fsdp')), may hold values from -28 to 28
- first_down: float32 [3072, 768], P(('dp', 'fsdp')), may hold values from -64 to 64
- first_vec: float32 [7680], P(('dp', 'fsdp')), may hold values from -48 to 48
- second_qkv: float32 [768, 2304], P(('dp', 'fsdp')), may hold values from 7.3728 to 29.4912
- second_out: float32 [768, 768], P(('dp', 'fsdp')), may hold values from 3.6864 to 14.7456
- second_up: float32 [768, 3072], P(('dp', 'fsdp')), may hold values from 1.8432 to 7.3728
- second_down: float32 [3072, 768], P(('dp', 'fsdp')), may hold values from 11.9808 to 47.9232
- second_vec: float32 [7680], P(('dp', 'fsdp')), may hold values from 4.608 to 18.432
Outputs:
- block_out: bfloat16 [32, 576, 768], P(('dp', 'fsdp'))
- tokens_grad: float32 [32, 576, 768], P(('dp', 'fsdp'))
- first_qkv_new: float32 [768, 2304], P(('dp', 'fsdp'))
- second_qkv_new: float32 [768, 2304], P(('dp', 'fsdp'))
- master_qkv_new: float32 [768, 2304], P(('dp', 'fsdp'))
- first_out_new: float32 [768, 768], P(('dp', 'fsdp'))
- second_out_new: float32 [768, 768], P(('dp', 'fsdp'))
- master_out_new: float32 [768, 768], P(('dp', 'fsdp'))
- first_up_new: float32 [768, 3072], P(('dp', 'fsdp'))
- second_up_new: float32 [768, 3072], P(('dp', 'fsdp'))
- master_up_new: float32 [768, 3072], P(('dp', 'fsdp'))
- first_down_new: float32 [3072, 768], P(('dp', 'fsdp'))
- second_down_new: float32 [3072, 768], P(('dp', 'fsdp'))
- master_down_new: float32 [3072, 768], P(('dp', 'fsdp'))
- first_vec_new: float32 [7680], P(('dp', 'fsdp'))
- second_vec_new: float32 [7680], P(('dp', 'fsdp'))
- master_vec_new: float32 [7680], P(('dp', 'fsdp'))
Inputs may be any that keep to these rules, and one draw needn't show every extreme that they name: In each row, segments never fall from slot to slot and count tiles from 0; a row holds four small tiles, two large tiles then padding, or a large tile, two small tiles then padding; padding slots form the row's last segment. `tile_sides`: every slot of a tile carries that tile's side (12 or 15); padding slots carry 1. `valid_slots`: padding slots are 0 and stand at the end of a row. `owners`: A permutation of 0 .. 31.
All inputs are finite; a program needn't handle non-finite values.
Results may differ from a plain program's by a relative error of at most 0.011.
Values may be sent and summed in bfloat16 or wider, within the bound.
No kernel may reach another device: no remote copies, remote signals or barrier semaphores. Data moves between devices by JAX's collectives and lax.ppermute only.
A program may use at most 192 MiB of HBM per device.

v0:
```python
import functools

import jax
import jax.numpy as jnp
from jax import lax
from jax.experimental import pallas as pl
from jax.experimental.pallas import tpu as pltpu
from jax.sharding import PartitionSpec as P

D = 768
HEADS = 12
FF = 3072
STEP = 10
HALF = 384
WIN = 256
CUT_ONE = 1152
CUT_TWO = 1920
CUT_THREE = 384

EPSILON = 1e-05
BETA_ONE = 0.9
BETA_TWO = 0.999
ADAM_EPS = 1e-08
RATE_MATRIX = 0.05
DECAY_MATRIX = 0.05
RATE_VECTOR = 0.3

AXES = ("dp", "fsdp")
LOW = jnp.bfloat16
WIDE = jnp.float32
VMEM_BYTES = 56 * 2**20


def nn(left, right):
    return lax.dot_general(left, right, (((1,), (0,)), ((), ())), preferred_element_type=WIDE)


def nt(left, right):
    return lax.dot_general(left, right, (((1,), (1,)), ((), ())), preferred_element_type=WIDE)


def tn(left, right):
    return lax.dot_general(left, right, (((0,), (0,)), ((), ())), preferred_element_type=WIDE)


def shape(rows, cols, kind=LOW):
    return jax.ShapeDtypeStruct((rows, cols), kind)


def later(kernel, inputs, extra):
    return lambda *refs: kernel(*refs[:inputs], *refs[inputs + extra :])


def whole_call(kernel, outs, scratch, smem, name, flops, *args, anywhere=(), after=()):
    specs = []
    for i in range(len(args)):
        space = pltpu.SMEM if i < smem else pl.ANY if i in anywhere else pltpu.VMEM
        specs.append(pl.BlockSpec(memory_space=space))
    moved = sum(a.size * a.dtype.itemsize for a in args) + sum(o.size * o.dtype.itemsize for o in outs)
    return pl.pallas_call(
        later(kernel, len(args), len(after)),
        in_specs=specs + [pl.BlockSpec(memory_space=pl.ANY)] * len(after),
        out_specs=[pl.BlockSpec(memory_space=pltpu.VMEM)] * len(outs),
        out_shape=outs,
        scratch_shapes=scratch,
        compiler_params=pltpu.CompilerParams(vmem_limit_bytes=VMEM_BYTES),
        cost_estimate=pl.CostEstimate(flops=flops, bytes_accessed=moved, transcendentals=0),
        name=name,
    )(*args, *after)


def over_rows(count, step, body, init=None):
    return lax.fori_loop(0, count // step, lambda i, c: body(pl.ds(pl.multiple_of(i * step, step), step), c), init)


def normal(values):
    centre = values - jnp.mean(values, axis=-1, keepdims=True)
    rstd = lax.rsqrt(jnp.mean(centre * centre, axis=-1, keepdims=True) + EPSILON)
    return centre * rstd, rstd


def both(own, other, lo, width):
    return jnp.concatenate([own[:, lo : lo + width], other[:, lo : lo + width]], axis=0)


def qkv_kernel(x_ref, vec_ref, order_ref, ao, ax, bo, bx, a_ref, qkv_ref, tmp):
    gain, shift = vec_ref[0:1, :], vec_ref[1:2, :]

    def norm(rows, _):
        tmp[rows, :] = (normal(x_ref[rows, :].astype(WIDE))[0] * gain + shift).astype(LOW)

    over_rows(x_ref.shape[0], 64, norm)
    a_ref[...] = nn(tmp[...], order_ref[...]).astype(LOW)
    for col in range(0, 3 * D, 384):
        own, other, lo = (ao, ax, col) if col < CUT_ONE else (bo, bx, col - CUT_ONE)
        qkv_ref[:, col : col + 384] = nn(a_ref[...], both(own, other, lo, 384)).astype(LOW)


def project(x, vec, order, one, after=()):
    n = x.shape[0]
    return whole_call(
        qkv_kernel, [shape(n, D), shape(n, 3 * D)], [pltpu.VMEM((n, D), LOW)], 0, "project",
        2 * n * D * (4 * D), x, vec, order, *one, after=after,
    )


def attend_kernel(base, spans, slopes, q_ref, k_ref, v_ref, far_ref, o_ref, p_ref, acc):
    pair = pl.program_id(0) + base
    acc[...] = jnp.zeros_like(acc)
    lane = lax.broadcasted_iota(jnp.int32, (WIN, 128), 1)
    rows = lax.broadcasted_iota(jnp.int32, (WIN, 1), 0)
    for t in range(4):
        lo, hi = spans[t, 0], spans[t, 1]

        @pl.when(hi > lo)
        def _():
            at = pl.multiple_of(spans[t, 2], 16)
            win = pl.ds(at, WIN)
            q, k, v = q_ref[win, :], k_ref[win, :], v_ref[win, :]
            inside = ((rows + at >= lo) & (rows + at < hi)).astype(WIDE)
            far = far_ref[t]
            out = None
            for e in range(2):
                keep = (lane < 64) if e == 0 else (lane >= 64)
                s = nt(q, jnp.where(keep, k, jnp.zeros_like(k))) * 0.125 - slopes[2 * pair + e] * far
                p = jnp.exp(s - jnp.max(s, axis=1, keepdims=True))
                p = (p * (inside / jnp.sum(p, axis=1, keepdims=True))).astype(LOW)
                p_ref[e, t] = p
                part = nn(p, jnp.where(keep, v, jnp.zeros_like(v)))
                out = part if out is None else out + part
            acc[win, :] += out

    o_ref[...] = acc[...].astype(LOW)


def columns(n, offset):
    return pl.BlockSpec((n, 128), lambda h, *_: (0, h + offset))


def attend(base, qkv, far, spans, slopes, after=()):
    n = qkv.shape[0]
    return pl.pallas_call(
        later(functools.partial(attend_kernel, base), 6, len(after)),
        grid_spec=pltpu.PrefetchScalarGridSpec(
            num_scalar_prefetch=2,
            grid=(3,),
            in_specs=[columns(n, base), columns(n, base + 6), columns(n, base + 12),
                      pl.BlockSpec((4, WIN, WIN), lambda h, *_: (0, 0, 0))]
            + [pl.BlockSpec(memory_space=pl.ANY)] * len(after),
            out_specs=[columns(n, 0), pl.BlockSpec((2, 4, WIN, WIN), lambda h, *_: (h, 0, 0, 0))],
            scratch_shapes=[pltpu.VMEM((n, 128), WIDE)],
        ),
        out_shape=[shape(n, HALF), jax.ShapeDtypeStruct((HEADS // 2, 4, WIN, WIN), LOW)],
        compiler_params=pltpu.CompilerParams(vmem_limit_bytes=VMEM_BYTES),
        cost_estimate=pl.CostEstimate(flops=9 * 10**9, bytes_accessed=6 * 10**6, transcendentals=0),
        name="attend",
    )(spans, slopes, qkv, qkv, qkv, far, *after)


def attend_back_kernel(spans, q_ref, k_ref, v_ref, g_ref, p_ref, dq_ref, dk_ref, dv_ref, aq, ak, av):
    for acc in (aq, ak, av):
        acc[...] = jnp.zeros_like(acc)
    lane = lax.broadcasted_iota(jnp.int32, (WIN, 128), 1)
    for t in range(4):

        @pl.when(spans[t, 1] > spans[t, 0])
        def _():
            win = pl.ds(pl.multiple_of(spans[t, 2], 16), WIN)
            q, k, v, g = q_ref[win, :], k_ref[win, :], v_ref[win, :], g_ref[win, :]
            sums = None
            for e in range(2):
                keep = (lane < 64) if e == 0 else (lane >= 64)
                qe, ke, ge = [jnp.where(keep, z, jnp.zeros_like(z)) for z in (q, k, g)]
                p = p_ref[e, t]
                wide = p.astype(WIDE)
                d = wide * nt(ge, v)
                d = ((d - wide * jnp.sum(d, axis=1, keepdims=True)) * 0.125).astype(LOW)
                parts = (nn(d, ke), tn(d, qe), tn(p, ge))
                sums = parts if sums is None else tuple(a + b for a, b in zip(sums, parts))
            for acc, part in zip((aq, ak, av), sums):
                acc[win, :] += part

    for out, acc in zip((dq_ref, dk_ref, dv_ref), (aq, ak, av)):
        out[...] = acc[...].astype(LOW)


def attend_back(base, qkv, grad, probs, spans, after=()):
    n = qkv.shape[0]
    return pl.pallas_call(
        later(attend_back_kernel, 6, len(after)),
        grid_spec=pltpu.PrefetchScalarGridSpec(
            num_scalar_prefetch=1,
            grid=(3,),
            in_specs=[columns(n, base), columns(n, base + 6), columns(n, base + 12), columns(n, base),
                      pl.BlockSpec((2, 4, WIN, WIN), lambda h, *_: (h, 0, 0, 0))]
            + [pl.BlockSpec(memory_space=pl.ANY)] * len(after),
            out_specs=[columns(n, 0)] * 3,
            scratch_shapes=[pltpu.VMEM((n, 128), WIDE)] * 3,
        ),
        out_shape=[shape(n, HALF)] * 3,
        compiler_params=pltpu.CompilerParams(vmem_limit_bytes=VMEM_BYTES),
        cost_estimate=pl.CostEstimate(flops=12 * 10**9, bytes_accessed=6 * 10**6, transcendentals=0),
        name="attend_back",
    )(spans, qkv, qkv, qkv, grad, probs, *after)


def tables(seg, side, valid):
    n = seg.shape[0]
    ids = jnp.arange(n, dtype=jnp.int32)
    tiles = jnp.arange(4, dtype=jnp.int32)
    low = jnp.sum((seg[None, :] < tiles[:, None]).astype(jnp.int32), axis=1)
    high = jnp.sum((seg[None, :] <= tiles[:, None]).astype(jnp.int32), axis=1)
    at = jnp.minimum(low // 16 * 16, n - WIN)
    spans = jnp.stack([low, high, at], axis=1)
    place = ids - jnp.sum((seg[None, :] < seg[:, None]).astype(jnp.int32), axis=1)
    packed = jnp.stack([place // side, place % side, seg, valid, ids], axis=0)
    cut = jnp.stack([lax.dynamic_slice(packed, (0, at[t]), (5, WIN)) for t in range(4)], axis=0)
    row, col = cut[:, 0].astype(WIDE), cut[:, 1].astype(WIDE)
    row = row[:, :, None] - row[:, None, :]
    col = col[:, :, None] - col[:, None, :]
    mine = cut[:, 2] == tiles[:, None]
    allowed = mine[:, :, None] & mine[:, None, :] & (
        (cut[:, 3][:, None, :] == 1) | (cut[:, 4][:, :, None] == cut[:, 4][:, None, :])
    )
    return spans, jnp.where(allowed, jnp.sqrt(row * row + col * col), 1e12)


def bell(u):
    bell_value = jnp.exp(u * u * -0.5)
    size = jnp.abs(u)
    t = 1.0 / (1.0 + 0.23164189 * size)
    poly = 0.127414796 + t * (-0.142248368 + t * (0.7107068705 + t * (-0.7265760135 + t * 0.5307027145)))
    tail = poly * t * bell_value
    share = jnp.where(u >= 0, 1.0 - tail, tail)
    return u * share, share + u * bell_value * 0.3989422804014327


def up_kernel(x_ref, o0_ref, o1_ref, vec_ref, order_ref, ao, ax, bo, bx, mixed_ref, h_ref, a_ref, gl_ref, gp_ref, tmp):
    mixed_ref[...] = (
        nn(o0_ref[...], order_ref[:HALF, :]) + nn(o1_ref[...], order_ref[HALF:, :])
    ).astype(LOW)
    for col in (0, 384):
        part = slice(col, col + 384)
        h_ref[:, part] = x_ref[:, part].astype(WIDE) + nn(mixed_ref[...], both(ao, ax, col, 384)) + vec_ref[2:3, part]
    gain, shift = vec_ref[3:4, :], vec_ref[4:5, :]

    def norm(rows, _):
        tmp[rows, :] = (normal(h_ref[rows, :])[0] * gain + shift).astype(LOW)

    over_rows(x_ref.shape[0], 64, norm)
    a_ref[...] = nn(tmp[...], order_ref[...]).astype(LOW)
    for col in range(0, FF, 384):
        lo = col + D
        own, other, lo = (ao, ax, lo) if lo < CUT_TWO else (bo, bx, lo - CUT_TWO)
        k = 5 + col // D
        u = nn(a_ref[...], both(own, other, lo, 384)) + vec_ref[k : k + 1, col % D : col % D + 384]
        value, slope = bell(u)
        gl_ref[:, col : col + 384] = value.astype(LOW)
        gp_ref[:, col : col + 384] = slope.astype(LOW)


def upward(x, o, vec, order, two, after=()):
    n = x.shape[0]
    return whole_call(
        up_kernel, [shape(n, D), shape(n, D, WIDE), shape(n, D), shape(n, FF), shape(n, FF)],
        [pltpu.VMEM((n, D), LOW)], 0, "upward", 2 * n * D * (7 * D) * 2, x, *o, vec, order, *two,
        after=after,
    )


def down_kernel(place, vec_ref, gl_ref, gp_ref, dy_ref, h_ref, w0, w1, w2, w3, out_ref, dur_ref, vg_ref, wd, sem):
    def copies(b, left, right, row):
        src, dst = [pl.ds(pl.multiple_of(z * 96, 96), 96) for z in (row, b)]
        return (
            pltpu.make_async_copy(left.at[src, :], wd.at[dst, pl.ds(0, CUT_THREE)], sem),
            pltpu.make_async_copy(right.at[src, :], wd.at[dst, pl.ds(CUT_THREE, D - CUT_THREE)], sem),
        )

    def begin(b, carry):
        p = place[b]
        pl.when(p < 16)(lambda: [z.start() for z in copies(b, w0, w2, p)] and None)
        pl.when(p >= 16)(lambda: [z.start() for z in copies(b, w1, w3, p - 16)] and None)
        return carry

    def finish(b, carry):
        for z in copies(b, w0, w2, 0):
            z.wait()
        return carry

    lax.fori_loop(0, 32, begin, 0)
    lax.fori_loop(0, 32, finish, 0)
    for col in range(0, FF, 384):
        part = slice(col, col + 384)
        du = nt(dy_ref[...], wd[part, :]) * gp_ref[:, part].astype(WIDE)
        dur_ref[:, part] = du.astype(LOW)
        k = col // D
        vg_ref[k : k + 1, col % D : col % D + 384] = jnp.sum(du, axis=0, keepdims=True)
    for col in (0, 384):
        part = slice(col, col + 384)
        out_ref[:, part] = (h_ref[:, part] + nn(gl_ref[...], wd[:, part]) + vec_ref[9:10, part]).astype(LOW)


def downward(place, vec, gl, gp, dy, h, three, after=()):
    n = h.shape[0]
    return whole_call(
        down_kernel, [shape(n, D), shape(n, FF), shape(8, D, WIDE)],
        [pltpu.VMEM((FF, D), LOW), pltpu.SemaphoreType.DMA], 1, "downward",
        2 * n * D * (8 * D), place, vec, gl, gp, dy, h, *three, anywhere=(6, 7, 8, 9), after=after,
    )


def hidden_kernel(vec_ref, order_ref, dur_ref, dy_ref, h_ref, ao, ax, bo, bx, dh_ref, dhr_ref, dor_ref, vg_ref, tmp):
    split = CUT_TWO - D
    for i, (a, b) in enumerate(((ao, bo), (ax, bx))):
        tmp[:, HALF * i : HALF * (i + 1)] = (
            nt(dur_ref[:, :split], a[:, D:]) + nt(dur_ref[:, split:], b[...])
        ).astype(LOW)
    dh_ref[...] = nt(tmp[...], order_ref[...])
    gain = vec_ref[3:4, :]

    def step(rows, sums):
        e = dh_ref[rows, :]
        dy = dy_ref[rows, :].astype(WIDE)
        n, rstd = normal(h_ref[rows, :])
        w = e * gain
        dh = dy + rstd * (w - jnp.mean(w, axis=-1, keepdims=True) - n * jnp.mean(w * n, axis=-1, keepdims=True))
        dh_ref[rows, :] = dh
        dhr_ref[rows, :] = dh.astype(LOW)
        return tuple(s + jnp.sum(z.reshape(-1, 8, D), axis=0) for s, z in zip(sums, (dh, e * n, e, dy)))

    zero = jnp.zeros((8, D), WIDE)
    sums = over_rows(h_ref.shape[0], 32, step, (zero,) * 4)
    for k, s in enumerate(sums):
        vg_ref[k : k + 1, :] = jnp.sum(s, axis=0, keepdims=True)
    for i, a in enumerate((ao, ax)):
        tmp[:, HALF * i : HALF * (i + 1)] = nt(dhr_ref[...], a[:, :D]).astype(LOW)
    dor_ref[...] = nt(tmp[...], order_ref[...]).astype(LOW)


def hidden_grad(vec, order, dur, dy, h, two, after=()):
    n = h.shape[0]
    return whole_call(
        hidden_kernel, [shape(n, D, WIDE), shape(n, D), shape(n, D), shape(8, D, WIDE)],
        [pltpu.VMEM((n, D), LOW)], 0, "hidden_grad",
        2 * n * D * (7 * D), vec, order, dur, dy, h, *two, after=after,
    )


def down_grad_kernel(place, gl_ref, dy_ref, w0, w1, w2, w3):
    for c in range(8):
        t = tn(gl_ref[:, 384 * c : 384 * (c + 1)], dy_ref[...]).astype(LOW)
        for i in range(4):
            p = place[4 * c + i]

            def put(left, right, row):
                rows = pl.ds(pl.multiple_of(row * 96, 96), 96)
                left[rows, :] = t[96 * i : 96 * (i + 1), :CUT_THREE]
                right[rows, :] = t[96 * i : 96 * (i + 1), CUT_THREE:]

            pl.when(p < 16)(lambda: put(w0, w2, p))
            pl.when(p >= 16)(lambda: put(w1, w3, p - 16))


def down_grad(place, gl, dy, after=()):
    n = dy.shape[0]
    outs = [shape(FF // 2, CUT_THREE)] * 2 + [shape(FF // 2, D - CUT_THREE)] * 2
    return whole_call(down_grad_kernel, outs, [], 1, "down_grad", 2 * n * D * FF, place, gl, dy, after=after)


def two_grad_kernel(mixed_ref, a_ref, dhr_ref, dur_ref, ao, ax, bo, bx):
    for col in range(0, D + FF, 384):
        left, right = (mixed_ref, dhr_ref[:, col : col + 384]) if col < D else (a_ref, dur_ref[:, col - D : col - D + 384])
        t = tn(left[...], right).astype(LOW)
        own, other, lo = (ao, ax, col) if col < CUT_TWO else (bo, bx, col - CUT_TWO)
        own[:, lo : lo + 384] = t[:HALF]
        other[:, lo : lo + 384] = t[HALF:]


def two_grad(mixed, a, dhr, dur, after=()):
    n = a.shape[0]
    outs = [shape(HALF, CUT_TWO)] * 2 + [shape(HALF, D + FF - CUT_TWO)] * 2
    return whole_call(two_grad_kernel, outs, [], 0, "two_grad", 2 * n * D * (D + FF), mixed, a, dhr, dur,
                      after=after)


def one_grad_kernel(a_ref, *refs):
    halves, (ao, ax, bo, bx) = refs[:6], refs[6:]
    for i, half in enumerate(halves):
        t = tn(a_ref[...], half[...]).astype(LOW)
        col = 384 * i
        own, other, lo = (ao, ax, col) if col < CUT_ONE else (bo, bx, col - CUT_ONE)
        own[:, lo : lo + 384] = t[:HALF]
        other[:, lo : lo + 384] = t[HALF:]


def one_grad(a, d, after=()):
    n = a.shape[0]
    outs = [shape(HALF, CUT_ONE)] * 2 + [shape(HALF, 3 * D - CUT_ONE)] * 2
    return whole_call(one_grad_kernel, outs, [], 0, "one_grad", 2 * n * D * 3 * D, a, *d, after=after)


def input_kernel(x_ref, vec_ref, order_ref, q0, q1, k0, k1, v0, v1, dh_ref, ao, ax, bo, bx, dx_ref, vg_ref, tmp):
    for i, (a, b) in enumerate(((ao, bo), (ax, bx))):
        parts = ((q0, a, 0), (q1, a, 384), (k0, a, 768), (k1, b, 0), (v0, b, 384), (v1, b, 768))
        tmp[:, HALF * i : HALF * (i + 1)] = sum(nt(d[...], w[:, lo : lo + 384]) for d, w, lo in parts).astype(LOW)
    dx_ref[...] = nt(tmp[...], order_ref[...])
    gain = vec_ref[0:1, :]

    def step(rows, sums):
        e = dx_ref[rows, :]
        n, rstd = normal(x_ref[rows, :].astype(WIDE))
        w = e * gain
        dx_ref[rows, :] = dh_ref[rows, :] + rstd * (
            w - jnp.mean(w, axis=-1, keepdims=True) - n * jnp.mean(w * n, axis=-1, keepdims=True)
        )
        return tuple(s + jnp.sum(z.reshape(-1, 8, D), axis=0) for s, z in zip(sums, (e * n, e)))

    zero = jnp.zeros((8, D), WIDE)
    sums = over_rows(x_ref.shape[0], 32, step, (zero,) * 2)
    for k, s in enumerate(sums):
        vg_ref[k : k + 1, :] = jnp.sum(s, axis=0, keepdims=True)


def input_grad(x, vec, order, d, dh, one, after=()):
    n = x.shape[0]
    return whole_call(
        input_kernel, [shape(n, D, WIDE), shape(8, D, WIDE)], [pltpu.VMEM((n, D), LOW)], 0, "input_grad",
        2 * n * D * 4 * D, x, vec, order, *d, dh, *one, after=after,
    )


def swap(value, bits):
    pairs = [(i, i ^ bits) for i in range(32)]
    return lax.ppermute(value, AXES, pairs)


def tie(values, *first):
    return lax.optimization_barrier((tuple(values), first))[0]


def spread(block, cut):
    near = jnp.concatenate([block] + [swap(block, 8 * k) for k in (1, 2, 3)], axis=0)
    first = yield (near,)
    rows = near.shape[0]
    (near,) = tie((near,), first)
    left, right = near[:, :cut], near[:, cut:]
    left = jnp.concatenate([left, swap(left, 2)], axis=0)
    right = jnp.concatenate([right, swap(right, 4)], axis=0)
    first = yield left, right
    left, right = tie((left, right), first)
    left = jnp.concatenate([left, swap(left, 4)], axis=0)
    far = swap(right, 2)
    right = jnp.concatenate([right[:rows], far[:rows], right[rows:], far[rows:]], axis=0)
    first = yield left, right
    left, right = tie((left, right), first)
    yield left, swap(left, 1), right, swap(right, 1)


def collect(pieces):
    got = swap(pieces[1], 1), swap(pieces[3], 1)
    yield got
    left = pieces[0].astype(WIDE) + got[0].astype(WIDE)
    right = pieces[2].astype(WIDE) + got[1].astype(WIDE)
    half = left.shape[0] // 2
    rows = half // 2
    out = jnp.concatenate([right[rows:half], right[half + rows :]], axis=0).astype(LOW)
    got = swap(left[half:].astype(LOW), 4), swap(out, 2)
    yield got
    left = left[:half] + got[0].astype(WIDE)
    right = jnp.concatenate([right[:rows], right[half : half + rows]], axis=0) + got[1].astype(WIDE)
    got = swap(left[rows:].astype(LOW), 2), swap(right[rows:].astype(LOW), 4)
    yield got
    both_sides = jnp.concatenate(
        [left[:rows] + got[0].astype(WIDE), right[:rows] + got[1].astype(WIDE)], axis=1
    )
    unit = rows // 4
    low = both_sides.astype(LOW)
    got = [swap(low[unit * k : unit * (k + 1)], 8 * k) for k in (1, 2, 3)]
    yield got
    yield (sum((z.astype(WIDE) for z in got), both_sides[:unit]),)


def collect_vec(blocks):
    for bits in (1, 4, 2):
        half = blocks.shape[0] // 2
        blocks = blocks[:half] + swap(blocks[half:], bits)
    return sum((swap(blocks[k : k + 1], 8 * k) for k in (1, 2, 3)), blocks[:1]).reshape(-1)


def cut_up(whole, cut):
    half = whole.shape[0] // 2
    return whole[:half, :cut], whole[half:, :cut], whole[:half, cut:], whole[half:, cut:]


def repeat(value, count):
    for _ in range(count):
        yield value


def spread_any(block, cut):
    return repeat(cut_up(lax.all_gather(block, AXES, axis=0, tiled=True), cut), 4)


def join(pieces):
    return jnp.concatenate(
        [jnp.concatenate(pieces[:2], axis=0), jnp.concatenate(pieces[2:], axis=0)], axis=1
    )


def collect_any(pieces):
    total = lax.psum_scatter(join(pieces), AXES, scatter_dimension=0, tiled=True).astype(WIDE)
    return repeat((total,), 5)


def rearrange(whole, order, shards):
    return jnp.take(whole.reshape(shards, -1, whole.shape[1]), order, axis=0, mode="clip").reshape(whole.shape)


def adamw(master, moment_one, moment_two, gradient, step_rate, decay_rate):
    first_new = BETA_ONE * moment_one + (1.0 - BETA_ONE) * gradient
    second_new = BETA_TWO * moment_two + (1.0 - BETA_TWO) * gradient * gradient
    first_hat = first_new / (1.0 - BETA_ONE**STEP)
    second_hat = second_new / (1.0 - BETA_TWO**STEP)
    master_new = master - step_rate * (
        first_hat / (jnp.sqrt(second_hat) + ADAM_EPS) + decay_rate * master
    )
    return (first_new, second_new, master_new)


def local(
    tokens_in, cotangent, segments, tile_sides, valid_slots, owners,
    master_qkv, master_out, master_up, master_down, master_vec,
    first_qkv, first_out, first_up, first_down, first_vec,
    second_qkv, second_out, second_up, second_down, second_vec,
):
    shards = lax.axis_size(AXES)
    near = shards == 32
    unit = D // shards
    per_row = master_vec.shape[0] // unit
    share = master_vec.shape[0]
    ids = jnp.arange(shards, dtype=jnp.int32)
    if near:
        away = owners ^ lax.axis_index(AXES).astype(jnp.int32)
        place = (away >> 3) + 4 * ((away >> 1) & 1) + 8 * ((away >> 2) & 1) + 16 * (away & 1)
        place_down = place
    else:
        place = owners
        place_down = jnp.arange(32, dtype=jnp.int32)
    inverse = jnp.sum(ids[:, None] * (place[:, None] == ids[None, :]), axis=0)
    target = (place[:, None] * unit + jnp.arange(unit, dtype=jnp.int32)[None, :]).reshape(-1)
    order = (target[:, None] == jnp.arange(D, dtype=jnp.int32)[None, :]).astype(LOW)
    gather, scatter = (spread, collect) if near else (spread_any, collect_any)

    vec_block = jnp.pad(master_vec.reshape(unit, per_row), ((0, 0), (0, 128 - per_row)))
    one = gather(jnp.concatenate([master_qkv, vec_block], axis=1).astype(LOW), CUT_ONE)
    two = gather(jnp.concatenate([master_out, master_up], axis=1).astype(LOW), CUT_TWO)
    if near:
        three = spread(master_down.astype(LOW), CUT_THREE)
    else:
        whole = lax.all_gather(master_down.astype(LOW), AXES, axis=0, tiled=True)
        three = repeat(cut_up(rearrange(whole, owners, shards), CUT_THREE), 4)
    next(one)
    two_near = next(two)
    next(one)
    three_near = next(three)
    one_second = next(one)
    two_first = two.send(one_second)
    one = next(one)

    vec_rows = jnp.concatenate([one[2][:, 3 * D - CUT_ONE :], one[3][:, 3 * D - CUT_ONE :]], axis=0)
    vec = nn(order, vec_rows)[:, :per_row].reshape(per_row, D)
    vec = jnp.pad(vec, ((0, 16 - per_row), (0, 0)))
    spans, far = tables(segments[0], tile_sides[0], valid_slots[0])
    slopes = jnp.exp2(-8.0 * (jnp.arange(HEADS, dtype=jnp.int32).astype(WIDE) + 1.0) / HEADS)
    x = tokens_in[0]
    dy = cotangent[0]
    act_one, qkv = project(x, vec, order, one, two_near)
    mixed_0, probs_0 = attend(0, qkv, far, spans, slopes, two_first + three_near)
    two_second = two.send(qkv)
    mixed_1, probs_1 = attend(3, qkv, far, spans, slopes, two_second + (mixed_0,))
    three_first = three.send(mixed_0)
    two = two.send(mixed_0)
    mixed, hidden, act_two, gelu, gelu_slope = upward(x, (mixed_0, mixed_1), vec, order, two, three_first)
    three_second = three.send(mixed_1)
    three = three.send(mixed_1)
    grad_three = down_grad(place_down, gelu, dy, three_second)
    if not near:
        whole = join(grad_three)
        back = jnp.sum(ids[:, None] * (owners[:, None] == ids[None, :]), axis=0)
        grad_three = cut_up(rearrange(whole, back, shards), CUT_THREE)
    sum_three = scatter(grad_three)
    block_out, dur, sums_up = downward(place_down, vec, gelu, gelu_slope, dy, hidden, three, tuple(grad_three))
    dh, dh_low, dmixed, sums = hidden_grad(vec, order, dur, dy, hidden, two, tuple(next(sum_three)))
    grad_two = two_grad(mixed, act_two, dh_low, dur, tuple(next(sum_three)))
    sum_two = scatter(grad_two)
    d0 = attend_back(0, qkv, dmixed, probs_0, spans, tuple(next(sum_three)) + tuple(grad_two))
    d1 = attend_back(3, qkv, dmixed, probs_1, spans, tuple(next(sum_three)) + tuple(next(sum_two)) + (d0[0],))
    d = [z for pair in zip(d0, d1) for z in pair]
    grad_one = one_grad(act_one, d, tuple(next(sum_two)))
    sum_one = scatter(grad_one)
    tokens_grad, sums_one = input_grad(
        x, vec, order, d, dh, one, tuple(next(sum_one)) + tuple(next(sum_two))
    )
    vector_grad = jnp.concatenate([sums_one[:2], sums[:3], sums_up[:4], sums[3:4]], axis=0)
    blocks = jnp.take(vector_grad.reshape(shards, share), inverse, axis=0, mode="clip")
    if near:
        sum_vec = collect_vec(blocks)
    else:
        sum_vec = lax.psum_scatter(blocks.reshape(-1), AXES, scatter_dimension=0, tiled=True)
    sum_one, sum_two, sum_three = [list(z)[-1][0] for z in (sum_one, sum_two, sum_three)]
    upd_qkv = adamw(master_qkv, first_qkv, second_qkv, sum_one, RATE_MATRIX, DECAY_MATRIX)
    upd_out = adamw(master_out, first_out, second_out, sum_two[:, :D], RATE_MATRIX, DECAY_MATRIX)
    upd_up = adamw(master_up, first_up, second_up, sum_two[:, D:], RATE_MATRIX, DECAY_MATRIX)
    upd_down = adamw(master_down, first_down, second_down, sum_three, RATE_MATRIX, DECAY_MATRIX)
    upd_vec = adamw(master_vec, first_vec, second_vec, sum_vec, RATE_VECTOR, 0.0)
    return (
        (block_out[None], tokens_grad[None]) + upd_qkv + upd_out + upd_up + upd_down + upd_vec
    )


def solution(mesh):
    rows = P(AXES, None)
    flat = P(AXES)
    deep = P(AXES, None, None)
    stored = (rows,) * 4 + (flat,)
    in_specs = (deep,) * 2 + (rows,) * 3 + (P(),) + stored * 3
    out_specs = (deep,) * 2 + (rows,) * 12 + (flat,) * 3
    return jax.shard_map(local, mesh=mesh, in_specs=in_specs, out_specs=out_specs, check_vma=False)
```

profile of v0, /device:TPU:0, one launch (start us, length us, event | category | flops | bytes accessed | tf_op | source)
XLA Modules:
  0.0 384.7 jit_solution(13571736849956014752)
XLA Ops:
  2.5 5.1 %collective-permute-start.2 = (bf16[24,2432]{1,0:T(8,128)(2,1)S(1)}, bf16[24,2432]{1,0:T(8,128)(2,1)S(1)}, u32[]{:S(2)}, u32[]{:S(2)}) collective-permute-start(bf16[24,2432]{1,0:T(8,128)(2,1)S(1)} %pad_maximum_fusion.21), channel_id=1, source_target_pairs={{0,24},{1,25},{2,26},{3,27},{4,28},{5,29},{6,30},{7,31},{8,16},{9,... | collective-permute-start | bytes 350216 | tf_op jit(solution)/shard_map/ppermute | solution.py:434
  10.1 3.8 collective-permute-start.11
  24.3 1.3 fusion.refs_2_.refs_4_.refs_1_
  25.5 1.6 sqrt_select_fusion.refs_5_
  28.0 3.7 collective-permute-start.16
  32.5 3.9 %collective-permute-done.10 = bf16[24,3840]{1,0:T(8,128)(2,1)S(1)} collective-permute-done((bf16[24,3840]{1,0:T(8,128)(2,1)S(1)}, bf16[24,3840]{1,0:T(8,128)(2,1)S(1)}, u32[]{:S(2)}, u32[]{:S(2)}) %collective-permute-start.10) | collective-permute-done | bytes 184352 | tf_op jit(solution)/shard_map/ppermute | solution.py:434
  36.5 1.5 collective-permute-start.3
  37.9 2.7 collective-permute-done.9
  40.7 1.5 collective-permute-start.4
  42.4 6.1 %collective-permute-done.4 = bf16[96,1280]{1,0:T(8,128)(2,1)S(1)} collective-permute-done((bf16[96,1280]{1,0:T(8,128)(2,1)S(1)}, bf16[96,1280]{1,0:T(8,128)(2,1)S(1)}, u32[]{:S(2)}, u32[]{:S(2)}) %collective-permute-start.4) | collective-permute-done | bytes 245792 | tf_op jit(solution)/shard_map/ppermute | solution.py:434
  48.6 1.6 collective-permute-start.5
  50.1 1.5 collective-permute-start.6
  51.7 5.2 %collective-permute-done.5 = bf16[192,1152]{1,0:T(8,128)(2,1)S(1)} collective-permute-done((bf16[192,1152]{1,0:T(8,128)(2,1)S(1)}, bf16[192,1152]{1,0:T(8,128)(2,1)S(1)}, u32[]{:S(2)}, u32[]{:S(2)}) %collective-permute-start.5) | collective-permute-done | bytes 442400 | tf_op jit(solution)/shard_map/ppermute | solution.py:434
  57.0 2.0 collective-permute-done.6
  59.2 1.6 collective-permute-start.12
  62.8 1.9 pad_maximum_fusion.10.refs_8_
  64.7 5.5 %collective-permute-done.12 = bf16[96,1920]{1,0:T(8,128)(2,1)S(1)} collective-permute-done((bf16[96,1920]{1,0:T(8,128)(2,1)S(1)}, bf16[96,1920]{1,0:T(8,128)(2,1)S(1)}, u32[]{:S(2)}, u32[]{:S(2)}) %collective-permute-start.12) | collective-permute-done | bytes 368672 | tf_op jit(solution)/shard_map/ppermute | solution.py:434
  71.2 1.9 collective-permute-done.13
  73.2 1.0 slice.375
  75.7 9.6 %project.1 = (bf16[576,768]{1,0:T(8,128)(2,1)}, bf16[576,2304]{1,0:T(8,128)(2,1)}) custom-call(bf16[576,768]{1,0:T(8,128)(2,1)} %bitcast.23, f32[16,768]{1,0:T(8,128)} %pad.10.refs_1_.refs_3_.refs_0_, bf16[768,768]{1,0:T(8,128)(2,1)} %fusion.refs_2_.refs_4_.refs_1_, bf16[384,1152]{1,0:T(8,128)(2,1)} %copy-done.11, ...), custom_call_target="tpu_custom_call" | custom-call | flops 2717908992 | bytes 9388032 | tf_op jit(solution)/shard_map/project/pallas_call | solution.py:60
  85.9 10.3 %attend.2 = (bf16[576,384]{1,0:T(8,128)(2,1)}, bf16[6,4,256,256]{3,2,1,0:T(8,128)(2,1)}) custom-call(s32[4,3]{1,0:T(4,128)} %pad_add_fusion.1.refs_0_, f32[12]{0:T(128)} %multiply_exponential_fusion.refs_1_, bf16[576,2304]{1,0:T(8,128)(2,1)} %get-tuple-element.73.refs_2_.refs_3_.refs_4_.refs_1_, ...), custom_call_target="tpu_custom_call" | custom-call | flops 8999999488 | bytes 6000000 | tf_op jit(solution)/shard_map/attend/pallas_call | solution.py:142
  97.3 1.2 collective-permute-start.17
  99.3 10.2 %collective-permute-done.21 = bf16[384,384]{1,0:T(8,128)(2,1)S(1)} collective-permute-done((bf16[384,384]{1,0:T(8,128)(2,1)S(1)}, bf16[384,384]{1,0:T(8,128)(2,1)S(1)}, u32[]{:S(2)}, u32[]{:S(2)}) %collective-permute-start.21) | collective-permute-done | bytes 294944 | tf_op jit(solution)/shard_map/ppermute | solution.py:434
  109.6 11.6 %collective-permute-done.22 = bf16[384,384]{1,0:T(8,128)(2,1)S(1)} collective-permute-done((bf16[384,384]{1,0:T(8,128)(2,1)S(1)}, bf16[384,384]{1,0:T(8,128)(2,1)S(1)}, u32[]{:S(2)}, u32[]{:S(2)}) %collective-permute-start.22) | collective-permute-done | bytes 294944 | tf_op jit(solution)/shard_map/ppermute | solution.py:434
  123.1 10.4 %attend.3 = (bf16[576,384]{1,0:T(8,128)(2,1)}, bf16[6,4,256,256]{3,2,1,0:T(8,128)(2,1)}) custom-call(s32[4,3]{1,0:T(4,128)} %pad_add_fusion.1.refs_0_, f32[12]{0:T(128)} %multiply_exponential_fusion.refs_1_, bf16[576,2304]{1,0:T(8,128)(2,1)} %get-tuple-element.73.refs_2_.refs_3_.refs_4_.refs_1_, ...), custom_call_target="tpu_custom_call" | custom-call | flops 8999999488 | bytes 6000000 | tf_op jit(solution)/shard_map/attend/pallas_call | solution.py:142
  135.0 12.9 %collective-permute-done.23 = bf16[768,384]{1,0:T(8,128)(2,1)S(1)} collective-permute-done((bf16[768,384]{1,0:T(8,128)(2,1)S(1)}, bf16[768,384]{1,0:T(8,128)(2,1)S(1)}, u32[]{:S(2)}, u32[]{:S(2)}) %collective-permute-start.23) | collective-permute-done | bytes 589856 | tf_op jit(solution)/shard_map/ppermute | solution.py:434
  149.6 18.7 %upward.1 = (bf16[576,768]{1,0:T(8,128)(2,1)}, f32[576,768]{1,0:T(8,128)}, bf16[576,768]{1,0:T(8,128)(2,1)}, bf16[576,3072]{1,0:T(8,128)(2,1)}, bf16[576,3072]{1,0:T(8,128)(2,1)}) custom-call(bf16[576,768]{1,0:T(8,128)(2,1)} %bitcast.24, bf16[576,384]{1,0:T(8,128)(2,1)} %get-tuple-element.75.refs_8_.refs_1_, bf16[576,384]{1,0:T(8,128)(2,1)} %get-tuple-element.78.refs_2_, ...), custom_call_target="tpu_custom_call" | custom-call | flops 9512681472 | bytes 19513344 | tf_op jit(solution)/shard_map/upward/pallas_call | solution.py:60
  168.3 22.1 %down_grad.1 = (bf16[1536,384]{1,0:T(8,128)(2,1)}, bf16[1536,384]{1,0:T(8,128)(2,1)}, bf16[1536,384]{1,0:T(8,128)(2,1)}, bf16[1536,384]{1,0:T(8,128)(2,1)}) custom-call(s32[32]{0:T(128)} %get-tuple-element.139.refs_0_, bf16[576,3072]{1,0:T(8,128)(2,1)} %get-tuple-element.82.refs_1_.refs_2_, bf16[576,768]{1,0:T(8,128)(2,1)} %bitcast.30, ...), custom_call_target="tpu_custom_call" | custom-call | flops 2717908992 | bytes 9142400 | tf_op jit(solution)/shard_map/down_grad/pallas_call | solution.py:60
  191.1 1.0 copy-done.58
  192.1 14.9 %downward.1 = (bf16[576,768]{1,0:T(8,128)(2,1)}, bf16[576,3072]{1,0:T(8,128)(2,1)}, f32[8,768]{1,0:T(8,128)}) custom-call(s32[32]{0:T(128)} %get-tuple-element.139.refs_0_, f32[16,768]{1,0:T(8,128)} %pad.10.refs_1_.refs_3_.refs_0_, bf16[576,3072]{1,0:T(8,128)(2,1)} %get-tuple-element.82.refs_1_.refs_2_, bf16[576,3072]{1,0:T(8,128)(2,1)} %get-tuple-element.83.refs_3_, ...), custom_call_target="tpu_custom_call" | custom-call | flops 5435817984 | bytes 18948224 | tf_op jit(solution)/shard_map/downward/pallas_call | solution.py:60
  211.4 18.2 %hidden_grad.1 = (f32[576,768]{1,0:T(8,128)}, bf16[576,768]{1,0:T(8,128)(2,1)}, bf16[576,768]{1,0:T(8,128)(2,1)}, f32[8,768]{1,0:T(8,128)}) custom-call(f32[16,768]{1,0:T(8,128)} %pad.10.refs_1_.refs_3_.refs_0_, bf16[768,768]{1,0:T(8,128)(2,1)} %fusion.refs_2_.refs_4_.refs_1_, bf16[576,3072]{1,0:T(8,128)(2,1)} %get-tuple-element.94.refs_2_.refs_3_, ...), custom_call_target="tpu_custom_call" | custom-call | flops 4756340736 | bytes 16883712 | tf_op jit(solution)/shard_map/hidden_grad/pallas_call | solution.py:60
  232.0 2.0 collective-permute-start.30
  235.9 10.2 %two_grad.1 = (bf16[384,1920]{1,0:T(8,128)(2,1)}, bf16[384,1920]{1,0:T(8,128)(2,1)}, bf16[384,1920]{1,0:T(8,128)(2,1)}, bf16[384,1920]{1,0:T(8,128)(2,1)}) custom-call(bf16[576,768]{1,0:T(8,128)(2,1)} %get-tuple-element.97.refs_0_, bf16[576,768]{1,0:T(8,128)(2,1)} %get-tuple-element.98.refs_1_, bf16[576,768]{1,0:T(8,128)(2,1)} %get-tuple-element.99.refs_2_, ...), custom_call_target="tpu_custom_call" | custom-call | flops 3397386240 | bytes 12091392 | tf_op jit(solution)/shard_map/two_grad/pallas_call | solution.py:60
  247.5 1.6 collective-permute-start.33
  249.1 3.5 collective-permute-start.34
  252.6 12.2 %attend_back.2 = (bf16[576,384]{1,0:T(8,128)(2,1)}, bf16[576,384]{1,0:T(8,128)(2,1)}, bf16[576,384]{1,0:T(8,128)(2,1)}) custom-call(s32[4,3]{1,0:T(4,128)} %pad_add_fusion.1.refs_0_, bf16[576,2304]{1,0:T(8,128)(2,1)} %get-tuple-element.73.refs_2_.refs_3_.refs_4_.refs_1_, bf16[576,2304]{1,0:T(8,128)(2,1)} %get-tuple-element.73.refs_2_.refs_3_.refs_4_.refs_1_, ...), custom_call_target="tpu_custom_call" | custom-call | flops 12000000000 | bytes 6000000 | tf_op jit(solution)/shard_map/attend_back/pallas_call | solution.py:189
  264.9 1.1 multiply_subtract_fusion
  270.9 1.0 collective-permute-start.39
  271.8 12.3 %attend_back.3 = (bf16[576,384]{1,0:T(8,128)(2,1)}, bf16[576,384]{1,0:T(8,128)(2,1)}, bf16[576,384]{1,0:T(8,128)(2,1)}) custom-call(s32[4,3]{1,0:T(4,128)} %pad_add_fusion.1.refs_0_, bf16[576,2304]{1,0:T(8,128)(2,1)} %get-tuple-element.73.refs_2_.refs_3_.refs_4_.refs_1_, bf16[576,2304]{1,0:T(8,128)(2,1)} %get-tuple-element.73.refs_2_.refs_3_.refs_4_.refs_1_, ...), custom_call_target="tpu_custom_call" | custom-call | flops 12000000000 | bytes 6000000 | tf_op jit(solution)/shard_map/attend_back/pallas_call | solution.py:189
  284.2 2.6 collective-permute-done.38.refs_7_
  289.5 1.1 collective-permute-start.43
  290.6 6.2 %collective-permute-done.42.refs_16_ = bf16[96,1920]{1,0:T(8,128)(2,1)S(1)} collective-permute-done((bf16[96,1920]{1,0:T(8,128)(2,1)S(1)}, bf16[96,1920]{1,0:T(8,128)(2,1)S(1)}, u32[]{:S(2)}, u32[]{:S(2)}) %collective-permute-start.42) | collective-permute-done | bytes 368672 | tf_op jit(solution)/shard_map/ppermute | solution.py:434
  296.9 1.5 collective-permute-done.43.refs_17_
  299.1 3.5 collective-permute-start.53
  303.6 6.7 %one_grad.1 = (bf16[384,1152]{1,0:T(8,128)(2,1)}, bf16[384,1152]{1,0:T(8,128)(2,1)}, bf16[384,1152]{1,0:T(8,128)(2,1)}, bf16[384,1152]{1,0:T(8,128)(2,1)}) custom-call(bf16[576,768]{1,0:T(8,128)(2,1)} %get-tuple-element.112.refs_0_, bf16[576,384]{1,0:T(8,128)(2,1)} %get-tuple-element.104.refs_11_.refs_1_.refs_3_, ...), custom_call_target="tpu_custom_call" | custom-call | flops 2038431744 | bytes 7077888 | tf_op jit(solution)/shard_map/one_grad/pallas_call | solution.py:60
  310.9 3.9 %collective-permute-done.52 = bf16[24,3840]{1,0:T(8,128)(2,1)S(1)} collective-permute-done((bf16[24,3840]{1,0:T(8,128)(2,1)S(1)}, bf16[24,3840]{1,0:T(8,128)(2,1)S(1)}, u32[]{:S(2)}, u32[]{:S(2)}) %collective-permute-start.52) | collective-permute-done | bytes 184352 | tf_op jit(solution)/shard_map/ppermute | solution.py:434
  315.7 1.0 multiply_subtract_fusion.1
  318.0 14.8 %input_grad.1 = (f32[576,768]{1,0:T(8,128)}, f32[8,768]{1,0:T(8,128)}) custom-call(bf16[576,768]{1,0:T(8,128)(2,1)} %bitcast.25, f32[16,768]{1,0:T(8,128)} %pad.10.refs_1_.refs_3_.refs_0_, bf16[768,768]{1,0:T(8,128)(2,1)} %fusion.refs_2_.refs_4_.refs_1_, bf16[576,384]{1,0:T(8,128)(2,1)} %get-tuple-element.104.refs_11_.refs_1_.refs_3_, ...), custom_call_target="tpu_custom_call" | custom-call | flops 2717908992 | bytes 12066816 | tf_op jit(solution)/shard_map/input_grad/pallas_call | solution.py:60
  334.3 1.4 fusion.35
  335.8 2.4 collective-permute-start.55
  338.2 1.2 collective-permute-start.46
  339.8 1.1 collective-permute-start.56
  341.1 9.5 %collective-permute-done.56 = f32[4,240]{1,0:T(4,128)S(1)} collective-permute-done((f32[4,240]{1,0:T(4,128)S(1)}, f32[4,240]{1,0:T(4,128)S(1)}, u32[]{:S(2)}, u32[]{:S(2)}) %collective-permute-start.56) | collective-permute-done | bytes 3872 | tf_op jit(solution)/shard_map/ppermute | solution.py:434
  350.6 2.8 collective-permute-start.59
  353.4 1.6 collective-permute-start.57
  356.1 1.8 collective-permute-done.58
  358.4 9.8 %collective-permute-done.44 = bf16[192,1152]{1,0:T(8,128)(2,1)S(1)} collective-permute-done((bf16[192,1152]{1,0:T(8,128)(2,1)S(1)}, bf16[192,1152]{1,0:T(8,128)(2,1)S(1)}, u32[]{:S(2)}, u32[]{:S(2)}) %collective-permute-start.44) | collective-permute-done | bytes 442400 | tf_op jit(solution)/shard_map/ppermute | solution.py:434
  368.4 1.2 collective-permute-start.45
  369.5 1.1 collective-permute-done.47
  370.7 3.6 collective-permute-done.45
  374.5 2.8 collective-permute-start.50
  377.3 1.6 collective-permute-start.48
  379.5 1.6 collective-permute-done.50
  381.1 2.3 collective-permute-done.49
  (320 shorter events, 49.4 us)
Async XLA Ops:
  0.7 22.6 %copy-start.51 = (s32[1,576]{1,0:T(1,128)S(1)}, s32[1,576]{1,0:T(1,128)}, u32[]{:S(2)}) copy-start(s32[1,576]{1,0:T(1,128)} %param.25) | copy-start | bytes 6916
  0.7 22.9 %copy-start.56 = (s32[32]{0:T(128)S(1)}, s32[32]{0:T(128)}, u32[]{:S(2)}) copy-start(s32[32]{0:T(128)} %param.26) | copy-start | bytes 388
  2.5 24.8 %collective-permute-start.2 = (bf16[24,2432]{1,0:T(8,128)(2,1)S(1)}, bf16[24,2432]{1,0:T(8,128)(2,1)S(1)}, u32[]{:S(2)}, u32[]{:S(2)}) collective-permute-start(bf16[24,2432]{1,0:T(8,128)(2,1)S(1)} %pad_maximum_fusion.21), channel_id=1, source_target_pairs={{0,24},{1,25},{2,26},{3,27},{4,28},{5,29},{6,30},{7,31},{8,16},{9,... | collective-permute-start | bytes 350216 | tf_op jit(solution)/shard_map/ppermute | solution.py:434
  7.6 20.4 %collective-permute-start.1 = (bf16[24,2432]{1,0:T(8,128)(2,1)S(1)}, bf16[24,2432]{1,0:T(8,128)(2,1)S(1)}, u32[]{:S(2)}, u32[]{:S(2)}) collective-permute-start(bf16[24,2432]{1,0:T(8,128)(2,1)S(1)} %pad_maximum_fusion.21), channel_id=1, source_target_pairs={{0,16},{1,17},{2,18},{3,19},{4,20},{5,21},{6,22},{7,23},{8,24},{9,... | collective-permute-start | bytes 350216 | tf_op jit(solution)/shard_map/ppermute | solution.py:434
  7.6 24.1 %collective-permute-start = (bf16[24,2432]{1,0:T(8,128)(2,1)S(1)}, bf16[24,2432]{1,0:T(8,128)(2,1)S(1)}, u32[]{:S(2)}, u32[]{:S(2)}) collective-permute-start(bf16[24,2432]{1,0:T(8,128)(2,1)S(1)} %pad_maximum_fusion.21), channel_id=1, source_target_pairs={{0,8},{1,9},{2,10},{3,11},{4,12},{5,13},{6,14},{7,15},{8,0},{9,1},... | collective-permute-start | bytes 350216 | tf_op jit(solution)/shard_map/ppermute | solution.py:434
  10.1 21.7 %collective-permute-start.11 = (bf16[24,3840]{1,0:T(8,128)(2,1)S(1)}, bf16[24,3840]{1,0:T(8,128)(2,1)S(1)}, u32[]{:S(2)}, u32[]{:S(2)}) collective-permute-start(bf16[24,3840]{1,0:T(8,128)(2,1)S(1)} %pad_maximum_fusion.20), channel_id=1, source_target_pairs={{0,24},{1,25},{2,26},{3,27},{4,28},{5,29},{6,30},{7,31},{8,16},{9,... | collective-permute-start | bytes 552968 | tf_op jit(solution)/shard_map/ppermute | solution.py:434
  14.0 22.5 %collective-permute-start.10 = (bf16[24,3840]{1,0:T(8,128)(2,1)S(1)}, bf16[24,3840]{1,0:T(8,128)(2,1)S(1)}, u32[]{:S(2)}, u32[]{:S(2)}) collective-permute-start(bf16[24,3840]{1,0:T(8,128)(2,1)S(1)} %pad_maximum_fusion.20), channel_id=1, source_target_pairs={{0,16},{1,17},{2,18},{3,19},{4,20},{5,21},{6,22},{7,23},{8,24},{9,... | collective-permute-start | bytes 552968 | tf_op jit(solution)/shard_map/ppermute | solution.py:434
  27.3 13.4 %collective-permute-start.9 = (bf16[24,3840]{1,0:T(8,128)(2,1)S(1)}, bf16[24,3840]{1,0:T(8,128)(2,1)S(1)}, u32[]{:S(2)}, u32[]{:S(2)}) collective-permute-start(bf16[24,3840]{1,0:T(8,128)(2,1)S(1)} %pad_maximum_fusion.20), channel_id=1, source_target_pairs={{0,8},{1,9},{2,10},{3,11},{4,12},{5,13},{6,14},{7,15},{8,0},{9,1},... | collective-permute-start | bytes 552968 | tf_op jit(solution)/shard_map/ppermute | solution.py:434
  28.0 33.6 %collective-permute-start.16 = (bf16[96,768]{1,0:T(8,128)(2,1)S(1)}, bf16[96,768]{1,0:T(8,128)(2,1)}, u32[]{:S(2)}, u32[]{:S(2)}) collective-permute-start(bf16[96,768]{1,0:T(8,128)(2,1)S(1)} %convert_element_type.178), channel_id=1, source_target_pairs={{0,24},{1,25},{2,26},{3,27},{4,28},{5,29},{6,30},{7,31},{8,16},{9,... | collective-permute-start | bytes 442376 | tf_op jit(solution)/shard_map/ppermute | solution.py:434
  31.7 30.6 %collective-permute-start.15 = (bf16[96,768]{1,0:T(8,128)(2,1)S(1)}, bf16[96,768]{1,0:T(8,128)(2,1)}, u32[]{:S(2)}, u32[]{:S(2)}) collective-permute-start(bf16[96,768]{1,0:T(8,128)(2,1)S(1)} %convert_element_type.178), channel_id=1, source_target_pairs={{0,16},{1,17},{2,18},{3,19},{4,20},{5,21},{6,22},{7,23},{8,24},{9,... | collective-permute-start | bytes 442376 | tf_op jit(solution)/shard_map/ppermute | solution.py:434
  31.8 31.0 %collective-permute-start.14 = (bf16[96,768]{1,0:T(8,128)(2,1)S(1)}, bf16[96,768]{1,0:T(8,128)(2,1)}, u32[]{:S(2)}, u32[]{:S(2)}) collective-permute-start(bf16[96,768]{1,0:T(8,128)(2,1)S(1)} %convert_element_type.178), channel_id=1, source_target_pairs={{0,8},{1,9},{2,10},{3,11},{4,12},{5,13},{6,14},{7,15},{8,0},{9,1},... | collective-permute-start | bytes 442376 | tf_op jit(solution)/shard_map/ppermute | solution.py:434
  36.5 5.9 %collective-permute-start.3 = (bf16[96,1152]{1,0:T(8,128)(2,1)S(1)}, bf16[96,1152]{1,0:T(8,128)(2,1)S(1)}, u32[]{:S(2)}, u32[]{:S(2)}) collective-permute-start(bf16[96,1152]{1,0:T(8,128)(2,1)S(1)} %slice.371), channel_id=1, source_target_pairs={{0,2},{1,3},{2,0},{3,1},{4,6},{5,7},{6,4},{7,5},{8,10},{9,11},{10,... | collective-permute-start | bytes 663560 | tf_op jit(solution)/shard_map/ppermute | solution.py:434
  40.7 7.8 %collective-permute-start.4 = (bf16[96,1280]{1,0:T(8,128)(2,1)S(1)}, bf16[96,1280]{1,0:T(8,128)(2,1)S(1)}, u32[]{:S(2)}, u32[]{:S(2)}) collective-permute-start(bf16[96,1280]{1,0:T(8,128)(2,1)S(1)} %slice.372), channel_id=1, source_target_pairs={{0,4},{1,5},{2,6},{3,7},{4,0},{5,1},{6,2},{7,3},{8,12},{9,13},{10,... | collective-permute-start | bytes 737288 | tf_op jit(solution)/shard_map/ppermute | solution.py:434
  48.6 8.4 %collective-permute-start.5 = (bf16[192,1152]{1,0:T(8,128)(2,1)S(1)}, bf16[192,1152]{1,0:T(8,128)(2,1)S(1)}, u32[]{:S(2)}, u32[]{:S(2)}) collective-permute-start(bf16[192,1152]{1,0:T(8,128)(2,1)S(1)} %pad_maximum_fusion.16), channel_id=1, source_target_pairs={{0,4},{1,5},{2,6},{3,7},{4,0},{5,1},{6,2},{7,3},{8,12},{9,13},{10,... | collective-permute-start | bytes 1327112 | tf_op jit(solution)/shard_map/ppermute | solution.py:434
  50.1 8.8 %collective-permute-start.6 = (bf16[192,1280]{1,0:T(8,128)(2,1)S(1)}, bf16[192,1280]{1,0:T(8,128)(2,1)S(1)}, u32[]{:S(2)}, u32[]{:S(2)}) collective-permute-start(bf16[192,1280]{1,0:T(8,128)(2,1)S(1)} %pad_maximum_fusion.14), channel_id=1, source_target_pairs={{0,2},{1,3},{2,0},{3,1},{4,6},{5,7},{6,4},{7,5},{8,10},{9,11},{10,... | collective-permute-start | bytes 1474568 | tf_op jit(solution)/shard_map/ppermute | solution.py:434
  59.1 14.1 %collective-permute-start.7 = (bf16[384,1280]{1,0:T(8,128)(2,1)S(1)}, bf16[384,1280]{1,0:T(8,128)(2,1)}, u32[]{:S(2)}, u32[]{:S(2)}) collective-permute-start(bf16[384,1280]{1,0:T(8,128)(2,1)S(1)} %pad_maximum_fusion.5.refs_5_.refs_12_), channel_id=1, source_target_pairs={{0,1},{1,0},{2,3},{3,2},{4,5},{5,4},{6,7},{7,6},{8,9},{9,8},{10,11... | collective-permute-start | bytes 2949128 | tf_op jit(solution)/shard_map/ppermute | solution.py:434
  59.2 11.0 %collective-permute-start.12 = (bf16[96,1920]{1,0:T(8,128)(2,1)S(1)}, bf16[96,1920]{1,0:T(8,128)(2,1)S(1)}, u32[]{:S(2)}, u32[]{:S(2)}) collective-permute-start(bf16[96,1920]{1,0:T(8,128)(2,1)S(1)} %get-tuple-element.166), channel_id=1, source_target_pairs={{0,2},{1,3},{2,0},{3,1},{4,6},{5,7},{6,4},{7,5},{8,10},{9,11},{10,... | collective-permute-start | bytes 1105928 | tf_op jit(solution)/shard_map/ppermute | solution.py:434
  61.6 14.1 %collective-permute-start.8 = (bf16[384,1152]{1,0:T(8,128)(2,1)S(1)}, bf16[384,1152]{1,0:T(8,128)(2,1)}, u32[]{:S(2)}, u32[]{:S(2)}) collective-permute-start(bf16[384,1152]{1,0:T(8,128)(2,1)S(1)} %constant_dynamic-update-slice_fusion.refs_3_.refs_10_), channel_id=1, source_target_pairs={{0,1},{1,0},{2,3},{3,2},{4,5},{5,4},{6,7},{7,6},{8,9},{9,8},{10,11... | collective-permute-start | bytes 2654216 | tf_op jit(solution)/shard_map/ppermute | solution.py:434
  62.3 10.8 %collective-permute-start.13 = (bf16[96,1920]{1,0:T(8,128)(2,1)S(1)}, bf16[96,1920]{1,0:T(8,128)(2,1)S(1)}, u32[]{:S(2)}, u32[]{:S(2)}) collective-permute-start(bf16[96,1920]{1,0:T(8,128)(2,1)S(1)} %get-tuple-element.165), channel_id=1, source_target_pairs={{0,4},{1,5},{2,6},{3,7},{4,0},{5,1},{6,2},{7,3},{8,12},{9,13},{10,... | collective-permute-start | bytes 1105928 | tf_op jit(solution)/shard_map/ppermute | solution.py:434
  85.3 35.9 %collective-permute-start.18 = (bf16[192,1920]{1,0:T(8,128)(2,1)S(1)}, bf16[192,1920]{1,0:T(8,128)(2,1)S(1)}, u32[]{:S(2)}, u32[]{:S(2)}) collective-permute-start(bf16[192,1920]{1,0:T(8,128)(2,1)S(1)} %pad_maximum_fusion.8.refs_7_), channel_id=1, source_target_pairs={{0,2},{1,3},{2,0},{3,1},{4,6},{5,7},{6,4},{7,5},{8,10},{9,11},{10,... | collective-permute-start | bytes 2211848 | tf_op jit(solution)/shard_map/ppermute | solution.py:434
  96.2 13.3 %collective-permute-start.21 = (bf16[384,384]{1,0:T(8,128)(2,1)S(1)}, bf16[384,384]{1,0:T(8,128)(2,1)S(1)}, u32[]{:S(2)}, u32[]{:S(2)}) collective-permute-start(bf16[384,384]{1,0:T(8,128)(2,1)S(1)} %get-tuple-element.175), channel_id=1, source_target_pairs={{0,2},{1,3},{2,0},{3,1},{4,6},{5,7},{6,4},{7,5},{8,10},{9,11},{10,... | collective-permute-start | bytes 884744 | tf_op jit(solution)/shard_map/ppermute | solution.py:434
  97.3 24.2 %collective-permute-start.17 = (bf16[192,1920]{1,0:T(8,128)(2,1)S(1)}, bf16[192,1920]{1,0:T(8,128)(2,1)S(1)}, u32[]{:S(2)}, u32[]{:S(2)}) collective-permute-start(bf16[192,1920]{1,0:T(8,128)(2,1)S(1)} %copy-done.5), channel_id=1, source_target_pairs={{0,4},{1,5},{2,6},{3,7},{4,0},{5,1},{6,2},{7,3},{8,12},{9,13},{10,... | collective-permute-start | bytes 2211848 | tf_op jit(solution)/shard_map/ppermute | solution.py:434
  98.4 22.8 %collective-permute-start.22 = (bf16[384,384]{1,0:T(8,128)(2,1)S(1)}, bf16[384,384]{1,0:T(8,128)(2,1)S(1)}, u32[]{:S(2)}, u32[]{:S(2)}) collective-permute-start(bf16[384,384]{1,0:T(8,128)(2,1)S(1)} %get-tuple-element.174), channel_id=1, source_target_pairs={{0,4},{1,5},{2,6},{3,7},{4,0},{5,1},{6,2},{7,3},{8,12},{9,13},{10,... | collective-permute-start | bytes 884744 | tf_op jit(solution)/shard_map/ppermute | solution.py:434
  109.6 25.3 %copy-start.8 = (bf16[768,384]{1,0:T(8,128)(2,1)}, bf16[768,384]{1,0:T(8,128)(2,1)S(1)}, u32[]{:S(2)}) copy-start(bf16[768,384]{1,0:T(8,128)(2,1)S(1)} %pad_maximum_fusion.11.refs_9_) | copy-start | bytes 1769476
  121.6 28.0 %collective-permute-start.19 = (bf16[384,1920]{1,0:T(8,128)(2,1)S(1)}, bf16[384,1920]{1,0:T(8,128)(2,1)}, u32[]{:S(2)}, u32[]{:S(2)}) collective-permute-start(bf16[384,1920]{1,0:T(8,128)(2,1)S(1)} %constant_dynamic-update-slice_fusion.2.refs_6_.refs_5_), channel_id=1, source_target_pairs={{0,1},{1,0},{2,3},{3,2},{4,5},{5,4},{6,7},{7,6},{8,9},{9,8},{10,11... | collective-permute-start | bytes 4423688 | tf_op jit(solution)/shard_map/ppermute | solution.py:434
  121.7 28.0 %collective-permute-start.20 = (bf16[384,1920]{1,0:T(8,128)(2,1)S(1)}, bf16[384,1920]{1,0:T(8,128)(2,1)}, u32[]{:S(2)}, u32[]{:S(2)}) collective-permute-start(bf16[384,1920]{1,0:T(8,128)(2,1)S(1)} %pad_maximum_fusion.1.refs_7_), channel_id=1, source_target_pairs={{0,1},{1,0},{2,3},{3,2},{4,5},{5,4},{6,7},{7,6},{8,9},{9,8},{10,11... | collective-permute-start | bytes 4423688 | tf_op jit(solution)/shard_map/ppermute | solution.py:434
  133.4 14.5 %collective-permute-start.23 = (bf16[768,384]{1,0:T(8,128)(2,1)S(1)}, bf16[768,384]{1,0:T(8,128)(2,1)S(1)}, u32[]{:S(2)}, u32[]{:S(2)}) collective-permute-start(bf16[768,384]{1,0:T(8,128)(2,1)S(1)} %pad_maximum_fusion.11.refs_9_), channel_id=1, source_target_pairs={{0,4},{1,5},{2,6},{3,7},{4,0},{5,1},{6,2},{7,3},{8,12},{9,13},{10,... | collective-permute-start | bytes 1769480 | tf_op jit(solution)/shard_map/ppermute | solution.py:434
  134.0 14.1 %collective-permute-start.24 = (bf16[768,384]{1,0:T(8,128)(2,1)S(1)}, bf16[768,384]{1,0:T(8,128)(2,1)S(1)}, u32[]{:S(2)}, u32[]{:S(2)}) collective-permute-start(bf16[768,384]{1,0:T(8,128)(2,1)S(1)} %pad_maximum_fusion.12.refs_10_), channel_id=1, source_target_pairs={{0,2},{1,3},{2,0},{3,1},{4,6},{5,7},{6,4},{7,5},{8,10},{9,11},{10,... | collective-permute-start | bytes 1769480 | tf_op jit(solution)/shard_map/ppermute | solution.py:434
  149.1 41.9 %collective-permute-start.25 = (bf16[1536,384]{1,0:T(8,128)(2,1)S(1)}, bf16[1536,384]{1,0:T(8,128)(2,1)S(1)}, u32[]{:S(2)}, u32[]{:S(2)}) collective-permute-start(bf16[1536,384]{1,0:T(8,128)(2,1)S(1)} %constant_dynamic-update-slice_fusion.4.refs_3_.refs_6_), channel_id=1, source_target_pairs={{0,1},{1,0},{2,3},{3,2},{4,5},{5,4},{6,7},{7,6},{8,9},{9,8},{10,11... | collective-permute-start | bytes 3538952 | tf_op jit(solution)/shard_map/ppermute | solution.py:434
  149.1 41.9 %collective-permute-start.26 = (bf16[1536,384]{1,0:T(8,128)(2,1)S(1)}, bf16[1536,384]{1,0:T(8,128)(2,1)}, u32[]{:S(2)}, u32[]{:S(2)}) collective-permute-start(bf16[1536,384]{1,0:T(8,128)(2,1)S(1)} %pad_maximum_fusion.3.refs_4_.refs_8_), channel_id=1, source_target_pairs={{0,1},{1,0},{2,3},{3,2},{4,5},{5,4},{6,7},{7,6},{8,9},{9,8},{10,11... | collective-permute-start | bytes 3538952 | tf_op jit(solution)/shard_map/ppermute | solution.py:434
  168.3 22.1 %copy-start.57 = (s32[32]{0:T(128)S(1)}, s32[32]{0:T(128)}, u32[]{:S(2)}) copy-start(s32[32]{0:T(128)} %get-tuple-element.139.refs_0_) | copy-start | bytes 388
  190.4 17.3 %collective-permute-start.27 = (bf16[1536,384]{1,0:T(8,128)(2,1)}, bf16[1536,384]{1,0:T(8,128)(2,1)S(1)}, u32[]{:S(2)}, u32[]{:S(2)}) collective-permute-start(bf16[1536,384]{1,0:T(8,128)(2,1)} %get-tuple-element.90.refs_11_), channel_id=1, source_target_pairs={{0,1},{1,0},{2,3},{3,2},{4,5},{5,4},{6,7},{7,6},{8,9},{9,8},{10,11... | collective-permute-start | bytes 3538952 | tf_op jit(solution)/shard_map/ppermute | solution.py:434
  190.5 19.3 %collective-permute-start.28 = (bf16[1536,384]{1,0:T(8,128)(2,1)}, bf16[1536,384]{1,0:T(8,128)(2,1)S(1)}, u32[]{:S(2)}, u32[]{:S(2)}) collective-permute-start(bf16[1536,384]{1,0:T(8,128)(2,1)} %get-tuple-element.92.refs_13_), channel_id=1, source_target_pairs={{0,1},{1,0},{2,3},{3,2},{4,5},{5,4},{6,7},{7,6},{8,9},{9,8},{10,11... | collective-permute-start | bytes 3538952 | tf_op jit(solution)/shard_map/ppermute | solution.py:434
  208.8 22.3 %collective-permute-start.29 = (bf16[768,384]{1,0:T(8,128)(2,1)S(1)}, bf16[768,384]{1,0:T(8,128)(2,1)S(1)}, u32[]{:S(2)}, u32[]{:S(2)}) collective-permute-start(bf16[768,384]{1,0:T(8,128)(2,1)S(1)} %slice.521), channel_id=1, source_target_pairs={{0,4},{1,5},{2,6},{3,7},{4,0},{5,1},{6,2},{7,3},{8,12},{9,13},{10,... | collective-permute-start | bytes 1769480 | tf_op jit(solution)/shard_map/ppermute | solution.py:434
  211.3 22.7 %collective-permute-start.31 = (bf16[768,384]{1,0:T(8,128)(2,1)S(1)}, bf16[768,384]{1,0:T(8,128)(2,1)S(1)}, u32[]{:S(2)}, u32[]{:S(2)}) collective-permute-start(bf16[768,384]{1,0:T(8,128)(2,1)S(1)} %pad_maximum_fusion.13), channel_id=1, source_target_pairs={{0,2},{1,3},{2,0},{3,1},{4,6},{5,7},{6,4},{7,5},{8,10},{9,11},{10,... | collective-permute-start | bytes 1769480 | tf_op jit(solution)/shard_map/ppermute | solution.py:434
  232.0 14.7 %collective-permute-start.30 = (bf16[384,384]{1,0:T(8,128)(2,1)S(1)}, bf16[384,384]{1,0:T(8,128)(2,1)S(1)}, u32[]{:S(2)}, u32[]{:S(2)}) collective-permute-start(bf16[384,384]{1,0:T(8,128)(2,1)S(1)} %slice.526), channel_id=1, source_target_pairs={{0,2},{1,3},{2,0},{3,1},{4,6},{5,7},{6,4},{7,5},{8,10},{9,11},{10,... | collective-permute-start | bytes 884744 | tf_op jit(solution)/shard_map/ppermute | solution.py:434
  234.9 11.7 %collective-permute-start.32 = (bf16[384,384]{1,0:T(8,128)(2,1)S(1)}, bf16[384,384]{1,0:T(8,128)(2,1)S(1)}, u32[]{:S(2)}, u32[]{:S(2)}) collective-permute-start(bf16[384,384]{1,0:T(8,128)(2,1)S(1)} %slice.525), channel_id=1, source_target_pairs={{0,4},{1,5},{2,6},{3,7},{4,0},{5,1},{6,2},{7,3},{8,12},{9,13},{10,... | collective-permute-start | bytes 884744 | tf_op jit(solution)/shard_map/ppermute | solution.py:434
  246.1 19.9 %collective-permute-start.36 = (bf16[384,1920]{1,0:T(8,128)(2,1)}, bf16[384,1920]{1,0:T(8,128)(2,1)S(1)}, u32[]{:S(2)}, u32[]{:S(2)}) collective-permute-start(bf16[384,1920]{1,0:T(8,128)(2,1)} %get-tuple-element.101.refs_9_), channel_id=1, source_target_pairs={{0,1},{1,0},{2,3},{3,2},{4,5},{5,4},{6,7},{7,6},{8,9},{9,8},{10,11... | collective-permute-start | bytes 4423688 | tf_op jit(solution)/shard_map/ppermute | solution.py:434
  246.1 23.5 %collective-permute-start.37 = (bf16[384,1920]{1,0:T(8,128)(2,1)}, bf16[384,1920]{1,0:T(8,128)(2,1)S(1)}, u32[]{:S(2)}, u32[]{:S(2)}) collective-permute-start(bf16[384,1920]{1,0:T(8,128)(2,1)} %get-tuple-element.103.refs_11_), channel_id=1, source_target_pairs={{0,1},{1,0},{2,3},{3,2},{4,5},{5,4},{6,7},{7,6},{8,9},{9,8},{10,11... | collective-permute-start | bytes 4423688 | tf_op jit(solution)/shard_map/ppermute | solution.py:434
  247.5 17.3 %collective-permute-start.33 = (bf16[96,768]{1,0:T(8,128)(2,1)S(1)}, bf16[96,768]{1,0:T(8,128)(2,1)S(1)}, u32[]{:S(2)}, u32[]{:S(2)}) collective-permute-start(bf16[96,768]{1,0:T(8,128)(2,1)S(1)} %get-tuple-element.169), channel_id=1, source_target_pairs={{0,8},{1,9},{2,10},{3,11},{4,12},{5,13},{6,14},{7,15},{8,0},{9,1},... | collective-permute-start | bytes 442376 | tf_op jit(solution)/shard_map/ppermute | solution.py:434
  249.1 15.7 %collective-permute-start.34 = (bf16[96,768]{1,0:T(8,128)(2,1)S(1)}, bf16[96,768]{1,0:T(8,128)(2,1)S(1)}, u32[]{:S(2)}, u32[]{:S(2)}) collective-permute-start(bf16[96,768]{1,0:T(8,128)(2,1)S(1)} %get-tuple-element.168), channel_id=1, source_target_pairs={{0,16},{1,17},{2,18},{3,19},{4,20},{5,21},{6,22},{7,23},{8,24},{9,... | collective-permute-start | bytes 442376 | tf_op jit(solution)/shard_map/ppermute | solution.py:434
  252.5 12.3 %collective-permute-start.35 = (bf16[96,768]{1,0:T(8,128)(2,1)S(1)}, bf16[96,768]{1,0:T(8,128)(2,1)S(1)}, u32[]{:S(2)}, u32[]{:S(2)}) collective-permute-start(bf16[96,768]{1,0:T(8,128)(2,1)S(1)} %get-tuple-element.167), channel_id=1, source_target_pairs={{0,24},{1,25},{2,26},{3,27},{4,28},{5,29},{6,30},{7,31},{8,16},{9,... | collective-permute-start | bytes 442376 | tf_op jit(solution)/shard_map/ppermute | solution.py:434
  268.7 18.1 %collective-permute-start.38 = (bf16[192,1920]{1,0:T(8,128)(2,1)}, bf16[192,1920]{1,0:T(8,128)(2,1)S(1)}, u32[]{:S(2)}, u32[]{:S(2)}) collective-permute-start(bf16[192,1920]{1,0:T(8,128)(2,1)} %slice.520), channel_id=1, source_target_pairs={{0,4},{1,5},{2,6},{3,7},{4,0},{5,1},{6,2},{7,3},{8,12},{9,13},{10,... | collective-permute-start | bytes 2211848 | tf_op jit(solution)/shard_map/ppermute | solution.py:434
  270.9 17.7 %collective-permute-start.39 = (bf16[192,1920]{1,0:T(8,128)(2,1)S(1)}, bf16[192,1920]{1,0:T(8,128)(2,1)S(1)}, u32[]{:S(2)}, u32[]{:S(2)}) collective-permute-start(bf16[192,1920]{1,0:T(8,128)(2,1)S(1)} %pad_maximum_fusion.9), channel_id=1, source_target_pairs={{0,2},{1,3},{2,0},{3,1},{4,6},{5,7},{6,4},{7,5},{8,10},{9,11},{10,... | collective-permute-start | bytes 2211848 | tf_op jit(solution)/shard_map/ppermute | solution.py:434
  287.7 9.1 %collective-permute-start.42 = (bf16[96,1920]{1,0:T(8,128)(2,1)S(1)}, bf16[96,1920]{1,0:T(8,128)(2,1)S(1)}, u32[]{:S(2)}, u32[]{:S(2)}) collective-permute-start(bf16[96,1920]{1,0:T(8,128)(2,1)S(1)} %slice.524), channel_id=1, source_target_pairs={{0,2},{1,3},{2,0},{3,1},{4,6},{5,7},{6,4},{7,5},{8,10},{9,11},{10,... | collective-permute-start | bytes 1105928 | tf_op jit(solution)/shard_map/ppermute | solution.py:434
  289.5 8.9 %collective-permute-start.43 = (bf16[96,1920]{1,0:T(8,128)(2,1)S(1)}, bf16[96,1920]{1,0:T(8,128)(2,1)S(1)}, u32[]{:S(2)}, u32[]{:S(2)}) collective-permute-start(bf16[96,1920]{1,0:T(8,128)(2,1)S(1)} %slice.523), channel_id=1, source_target_pairs={{0,4},{1,5},{2,6},{3,7},{4,0},{5,1},{6,2},{7,3},{8,12},{9,13},{10,... | collective-permute-start | bytes 1105928 | tf_op jit(solution)/shard_map/ppermute | solution.py:434
  299.1 11.8 %collective-permute-start.53 = (bf16[24,3840]{1,0:T(8,128)(2,1)S(1)}, bf16[24,3840]{1,0:T(8,128)(2,1)S(1)}, u32[]{:S(2)}, u32[]{:S(2)}) collective-permute-start(bf16[24,3840]{1,0:T(8,128)(2,1)S(1)} %get-tuple-element.159), channel_id=1, source_target_pairs={{0,24},{1,25},{2,26},{3,27},{4,28},{5,29},{6,30},{7,31},{8,16},{9,... | collective-permute-start | bytes 552968 | tf_op jit(solution)/shard_map/ppermute | solution.py:434
  302.7 12.2 %collective-permute-start.52 = (bf16[24,3840]{1,0:T(8,128)(2,1)S(1)}, bf16[24,3840]{1,0:T(8,128)(2,1)S(1)}, u32[]{:S(2)}, u32[]{:S(2)}) collective-permute-start(bf16[24,3840]{1,0:T(8,128)(2,1)S(1)} %get-tuple-element.160), channel_id=1, source_target_pairs={{0,16},{1,17},{2,18},{3,19},{4,20},{5,21},{6,22},{7,23},{8,24},{9,... | collective-permute-start | bytes 552968 | tf_op jit(solution)/shard_map/ppermute | solution.py:434
  302.7 12.2 %collective-permute-start.51 = (bf16[24,3840]{1,0:T(8,128)(2,1)S(1)}, bf16[24,3840]{1,0:T(8,128)(2,1)S(1)}, u32[]{:S(2)}, u32[]{:S(2)}) collective-permute-start(bf16[24,3840]{1,0:T(8,128)(2,1)S(1)} %get-tuple-element.158), channel_id=1, source_target_pairs={{0,8},{1,9},{2,10},{3,11},{4,12},{5,13},{6,14},{7,15},{8,0},{9,1},... | collective-permute-start | bytes 552968 | tf_op jit(solution)/shard_map/ppermute | solution.py:434
  310.3 6.4 %collective-permute-start.40 = (bf16[384,1152]{1,0:T(8,128)(2,1)}, bf16[384,1152]{1,0:T(8,128)(2,1)S(1)}, u32[]{:S(2)}, u32[]{:S(2)}) collective-permute-start(bf16[384,1152]{1,0:T(8,128)(2,1)} %get-tuple-element.113), channel_id=1, source_target_pairs={{0,1},{1,0},{2,3},{3,2},{4,5},{5,4},{6,7},{7,6},{8,9},{9,8},{10,11... | collective-permute-start | bytes 2654216 | tf_op jit(solution)/shard_map/ppermute | solution.py:434
  310.4 6.3 %collective-permute-start.41 = (bf16[384,1152]{1,0:T(8,128)(2,1)}, bf16[384,1152]{1,0:T(8,128)(2,1)S(1)}, u32[]{:S(2)}, u32[]{:S(2)}) collective-permute-start(bf16[384,1152]{1,0:T(8,128)(2,1)} %get-tuple-element.114), channel_id=1, source_target_pairs={{0,1},{1,0},{2,3},{3,2},{4,5},{5,4},{6,7},{7,6},{8,9},{9,8},{10,11... | collective-permute-start | bytes 2654216 | tf_op jit(solution)/shard_map/ppermute | solution.py:434
  334.2 1.5 collective-permute-start.54
  335.8 4.0 %collective-permute-start.55 = (f32[8,240]{1,0:T(8,128)S(1)}, f32[8,240]{1,0:T(8,128)S(1)}, u32[]{:S(2)}, u32[]{:S(2)}) collective-permute-start(f32[8,240]{1,0:T(8,128)S(1)} %slice.435), channel_id=1, source_target_pairs={{0,4},{1,5},{2,6},{3,7},{4,0},{5,1},{6,2},{7,3},{8,12},{9,13},{10,... | collective-permute-start | bytes 23048 | tf_op jit(solution)/shard_map/ppermute | solution.py:434
  338.2 19.7 %collective-permute-start.46 = (bf16[192,1152]{1,0:T(8,128)(2,1)S(1)}, bf16[192,1152]{1,0:T(8,128)(2,1)S(1)}, u32[]{:S(2)}, u32[]{:S(2)}) collective-permute-start(bf16[192,1152]{1,0:T(8,128)(2,1)S(1)} %pad_maximum_fusion.17), channel_id=1, source_target_pairs={{0,2},{1,3},{2,0},{3,1},{4,6},{5,7},{6,4},{7,5},{8,10},{9,11},{10,... | collective-permute-start | bytes 1327112 | tf_op jit(solution)/shard_map/ppermute | solution.py:434
  339.8 10.8 %collective-permute-start.56 = (f32[4,240]{1,0:T(4,128)S(1)}, f32[4,240]{1,0:T(4,128)S(1)}, u32[]{:S(2)}, u32[]{:S(2)}) collective-permute-start(f32[4,240]{1,0:T(4,128)S(1)} %slice.437), channel_id=1, source_target_pairs={{0,2},{1,3},{2,0},{3,1},{4,6},{5,7},{6,4},{7,5},{8,10},{9,11},{10,... | collective-permute-start | bytes 11528 | tf_op jit(solution)/shard_map/ppermute | solution.py:434
  350.6 5.4 %collective-permute-start.59 = (f32[1,240]{1,0:T(1,128)S(1)}, f32[1,240]{1,0:T(1,128)S(1)}, u32[]{:S(2)}, u32[]{:S(2)}) collective-permute-start(f32[1,240]{1,0:T(1,128)S(1)} %get-tuple-element.195), channel_id=1, source_target_pairs={{0,24},{1,25},{2,26},{3,27},{4,28},{5,29},{6,30},{7,31},{8,16},{9,... | collective-permute-start | bytes 2888 | tf_op jit(solution)/shard_map/ppermute | solution.py:434
  353.4 4.5 %collective-permute-start.58 = (f32[1,240]{1,0:T(1,128)S(1)}, f32[1,240]{1,0:T(1,128)S(1)}, u32[]{:S(2)}, u32[]{:S(2)}) collective-permute-start(f32[1,240]{1,0:T(1,128)S(1)} %get-tuple-element.196), channel_id=1, source_target_pairs={{0,16},{1,17},{2,18},{3,19},{4,20},{5,21},{6,22},{7,23},{8,24},{9,... | collective-permute-start | bytes 2888 | tf_op jit(solution)/shard_map/ppermute | solution.py:434
  353.4 4.5 %collective-permute-start.57 = (f32[1,240]{1,0:T(1,128)S(1)}, f32[1,240]{1,0:T(1,128)S(1)}, u32[]{:S(2)}, u32[]{:S(2)}) collective-permute-start(f32[1,240]{1,0:T(1,128)S(1)} %get-tuple-element.194), channel_id=1, source_target_pairs={{0,8},{1,9},{2,10},{3,11},{4,12},{5,13},{6,14},{7,15},{8,0},{9,1},... | collective-permute-start | bytes 2888 | tf_op jit(solution)/shard_map/ppermute | solution.py:434
  355.2 13.1 %collective-permute-start.44 = (bf16[192,1152]{1,0:T(8,128)(2,1)S(1)}, bf16[192,1152]{1,0:T(8,128)(2,1)S(1)}, u32[]{:S(2)}, u32[]{:S(2)}) collective-permute-start(bf16[192,1152]{1,0:T(8,128)(2,1)S(1)} %slice.522), channel_id=1, source_target_pairs={{0,4},{1,5},{2,6},{3,7},{4,0},{5,1},{6,2},{7,3},{8,12},{9,13},{10,... | collective-permute-start | bytes 1327112 | tf_op jit(solution)/shard_map/ppermute | solution.py:434
  358.0 12.6 %collective-permute-start.47 = (bf16[96,1152]{1,0:T(8,128)(2,1)S(1)}, bf16[96,1152]{1,0:T(8,128)(2,1)S(1)}, u32[]{:S(2)}, u32[]{:S(2)}) collective-permute-start(bf16[96,1152]{1,0:T(8,128)(2,1)S(1)} %slice.527), channel_id=1, source_target_pairs={{0,4},{1,5},{2,6},{3,7},{4,0},{5,1},{6,2},{7,3},{8,12},{9,13},{10,... | collective-permute-start | bytes 663560 | tf_op jit(solution)/shard_map/ppermute | solution.py:434
  368.4 6.0 %collective-permute-start.45 = (bf16[96,1152]{1,0:T(8,128)(2,1)S(1)}, bf16[96,1152]{1,0:T(8,128)(2,1)S(1)}, u32[]{:S(2)}, u32[]{:S(2)}) collective-permute-start(bf16[96,1152]{1,0:T(8,128)(2,1)S(1)} %slice.528), channel_id=1, source_target_pairs={{0,2},{1,3},{2,0},{3,1},{4,6},{5,7},{6,4},{7,5},{8,10},{9,11},{10,... | collective-permute-start | bytes 663560 | tf_op jit(solution)/shard_map/ppermute | solution.py:434
  374.5 6.6 %collective-permute-start.50 = (bf16[24,2304]{1,0:T(8,128)(2,1)S(1)}, bf16[24,2304]{1,0:T(8,128)(2,1)S(1)}, u32[]{:S(2)}, u32[]{:S(2)}) collective-permute-start(bf16[24,2304]{1,0:T(8,128)(2,1)S(1)} %get-tuple-element.181), channel_id=1, source_target_pairs={{0,24},{1,25},{2,26},{3,27},{4,28},{5,29},{6,30},{7,31},{8,16},{9,... | collective-permute-start | bytes 331784 | tf_op jit(solution)/shard_map/ppermute | solution.py:434
  377.3 6.2 %collective-permute-start.49 = (bf16[24,2304]{1,0:T(8,128)(2,1)S(1)}, bf16[24,2304]{1,0:T(8,128)(2,1)S(1)}, u32[]{:S(2)}, u32[]{:S(2)}) collective-permute-start(bf16[24,2304]{1,0:T(8,128)(2,1)S(1)} %get-tuple-element.182), channel_id=1, source_target_pairs={{0,16},{1,17},{2,18},{3,19},{4,20},{5,21},{6,22},{7,23},{8,24},{9,... | collective-permute-start | bytes 331784 | tf_op jit(solution)/shard_map/ppermute | solution.py:434
  377.3 6.2 %collective-permute-start.48 = (bf16[24,2304]{1,0:T(8,128)(2,1)S(1)}, bf16[24,2304]{1,0:T(8,128)(2,1)S(1)}, u32[]{:S(2)}, u32[]{:S(2)}) collective-permute-start(bf16[24,2304]{1,0:T(8,128)(2,1)S(1)} %get-tuple-element.180), channel_id=1, source_target_pairs={{0,8},{1,9},{2,10},{3,11},{4,12},{5,13},{6,14},{7,15},{8,0},{9,1},... | collective-permute-start | bytes 331784 | tf_op jit(solution)/shard_map/ppermute | solution.py:434
  (55 other events, 350.5 us)
where the time goes:
time: 388 us; the launch traced here: 385 us
  Pallas kernels  160 us (41%)
  waiting for transfers between devices  108 us (28%)
  starting transfers between devices  62 us (16%)
  local copies, waits for them, and re-layouts  22.5 us (6%)
  other arithmetic  21.5 us (6%)
  between operations  9.84 us (3%)
    pallas_call x8, Pallas kernels, whole_call(): pl.pallas_call(later(kernel, len(args), len(after)), in_specs=specs + [pl...  115 us
    ppermute x60, waiting for transfers between devices, swap(): return lax.ppermute(value, AXES, pairs)  108 us
    ppermute x60, starting transfers between devices, swap(): return lax.ppermute(value, AXES, pairs)  62 us
    pallas_call x2, Pallas kernels, attend_back(): pl.pallas_call(later(attend_back_kernel, 6, len(after)), grid_spec=pltpu....  24.5 us
    pallas_call x2, Pallas kernels, attend(): pl.pallas_call(later(functools.partial(attend_kernel, base), 6, len(after...  20.6 us
    unnamed x121, local copies, waits for them, and re-layouts  13.3 us
  transfers between devices with their start and end apart: 60, of which 26 were waited for; matrix products, arithmetic and copies ran while one was open for 7% of the time, Pallas kernels for 35%

commit v1 on v0

--- a/solution.py
+++ b/solution.py
@@ -399,15 +399,26 @@
     return whole_call(one_grad_kernel, outs, [], 0, "one_grad", 2 * n * D * 3 * D, a, *d, after=after)
 
 
-def input_kernel(x_ref, vec_ref, order_ref, q0, q1, k0, k1, v0, v1, dh_ref, ao, ax, bo, bx, dx_ref, vg_ref, tmp):
+def input_back_kernel(order_ref, q0, q1, k0, k1, v0, v1, ao, ax, bo, bx, e_ref, tmp):
     for i, (a, b) in enumerate(((ao, bo), (ax, bx))):
         parts = ((q0, a, 0), (q1, a, 384), (k0, a, 768), (k1, b, 0), (v0, b, 384), (v1, b, 768))
         tmp[:, HALF * i : HALF * (i + 1)] = sum(nt(d[...], w[:, lo : lo + 384]) for d, w, lo in parts).astype(LOW)
-    dx_ref[...] = nt(tmp[...], order_ref[...])
+    e_ref[...] = nt(tmp[...], order_ref[...])
+
+
+def input_back(order, d, one, after=()):
+    n = d[0].shape[0]
+    return whole_call(
+        input_back_kernel, [shape(n, D, WIDE)], [pltpu.VMEM((n, D), LOW)], 0, "input_back",
+        2 * n * D * 4 * D, order, *d, *one, after=after,
+    )[0]
+
+
+def input_kernel(x_ref, vec_ref, e_ref, dh_ref, dx_ref, vg_ref):
     gain = vec_ref[0:1, :]
 
     def step(rows, sums):
-        e = dx_ref[rows, :]
+        e = e_ref[rows, :]
         n, rstd = normal(x_ref[rows, :].astype(WIDE))
         w = e * gain
         dx_ref[rows, :] = dh_ref[rows, :] + rstd * (
@@ -421,11 +432,11 @@
         vg_ref[k : k + 1, :] = jnp.sum(s, axis=0, keepdims=True)
 
 
-def input_grad(x, vec, order, d, dh, one, after=()):
+def input_grad(x, vec, e, dh, after=()):
     n = x.shape[0]
     return whole_call(
-        input_kernel, [shape(n, D, WIDE), shape(8, D, WIDE)], [pltpu.VMEM((n, D), LOW)], 0, "input_grad",
-        2 * n * D * 4 * D, x, vec, order, *d, dh, *one, after=after,
+        input_kernel, [shape(n, D, WIDE), shape(8, D, WIDE)], [], 0, "input_grad",
+        2 * n * D * 3 * D, x, vec, e, dh, after=after,
     )
 
 
@@ -438,46 +449,53 @@
     return lax.optimization_barrier((tuple(values), first))[0]
 
 
-def spread(block, cut):
-    near = jnp.concatenate([block] + [swap(block, 8 * k) for k in (1, 2, 3)], axis=0)
-    first = yield (near,)
+def transfer(firsts, stage, values, *bits):
+    values = tie(values, firsts.get((stage, "start"), ()))
+    got = firsts[stage, "got"] = tuple(swap(value, bit) for value, bit in zip(values, bits))
+    both = tie(tuple(values) + got, firsts.get((stage, "end"), ()))
+    return both[: len(values)], both[len(values) :]
+
+
+def spread(block, cut, firsts):
+    move = functools.partial(transfer, firsts)
+    (block, _, _), got = move(0, (block,) * 3, 8, 16, 24)
+    near = jnp.concatenate((block,) + got, axis=0)
+    yield (near,)
     rows = near.shape[0]
-    (near,) = tie((near,), first)
-    left, right = near[:, :cut], near[:, cut:]
-    left = jnp.concatenate([left, swap(left, 2)], axis=0)
-    right = jnp.concatenate([right, swap(right, 4)], axis=0)
-    first = yield left, right
-    left, right = tie((left, right), first)
-    left = jnp.concatenate([left, swap(left, 4)], axis=0)
-    far = swap(right, 2)
+    mine, got = move(1, (near[:, :cut], near[:, cut:]), 2, 4)
+    left, right = [jnp.concatenate(z, axis=0) for z in zip(mine, got)]
+    yield left, right
+    (left, right), (got, far) = move(2, (left, right), 4, 2)
+    left = jnp.concatenate([left, got], axis=0)
     right = jnp.concatenate([right[:rows], far[:rows], right[rows:], far[rows:]], axis=0)
-    first = yield left, right
-    left, right = tie((left, right), first)
-    yield left, swap(left, 1), right, swap(right, 1)
-
-
-def collect(pieces):
-    got = swap(pieces[1], 1), swap(pieces[3], 1)
-    yield got
+    yield left, right
+    mine, got = move(3, (left, right), 1, 1)
+    yield mine[0], got[0], mine[1], got[1]
+
+
+def collect(pieces, firsts):
+    move = functools.partial(transfer, firsts)
+    _, got = move(0, (pieces[1], pieces[3]), 1, 1)
+    yield
     left = pieces[0].astype(WIDE) + got[0].astype(WIDE)
     right = pieces[2].astype(WIDE) + got[1].astype(WIDE)
     half = left.shape[0] // 2
     rows = half // 2
     out = jnp.concatenate([right[rows:half], right[half + rows :]], axis=0).astype(LOW)
-    got = swap(left[half:].astype(LOW), 4), swap(out, 2)
-    yield got
+    _, got = move(1, (left[half:].astype(LOW), out), 4, 2)
+    yield
     left = left[:half] + got[0].astype(WIDE)
     right = jnp.concatenate([right[:rows], right[half : half + rows]], axis=0) + got[1].astype(WIDE)
-    got = swap(left[rows:].astype(LOW), 2), swap(right[rows:].astype(LOW), 4)
-    yield got
+    _, got = move(2, (left[rows:].astype(LOW), right[rows:].astype(LOW)), 2, 4)
+    yield
     both_sides = jnp.concatenate(
         [left[:rows] + got[0].astype(WIDE), right[:rows] + got[1].astype(WIDE)], axis=1
     )
     unit = rows // 4
     low = both_sides.astype(LOW)
-    got = [swap(low[unit * k : unit * (k + 1)], 8 * k) for k in (1, 2, 3)]
-    yield got
-    yield (sum((z.astype(WIDE) for z in got), both_sides[:unit]),)
+    _, got = move(3, [low[unit * k : unit * (k + 1)] for k in (1, 2, 3)], 8, 16, 24)
+    yield
+    yield sum((z.astype(WIDE) for z in got), both_sides[:unit])
 
 
 def collect_vec(blocks):
@@ -497,7 +515,7 @@
         yield value
 
 
-def spread_any(block, cut):
+def spread_any(block, cut, firsts):
     return repeat(cut_up(lax.all_gather(block, AXES, axis=0, tiled=True), cut), 4)
 
 
@@ -507,9 +525,9 @@
     )
 
 
-def collect_any(pieces):
+def collect_any(pieces, firsts):
     total = lax.psum_scatter(join(pieces), AXES, scatter_dimension=0, tiled=True).astype(WIDE)
-    return repeat((total,), 5)
+    return repeat(total, 5)
 
 
 def rearrange(whole, order, shards):
@@ -552,20 +570,19 @@
     gather, scatter = (spread, collect) if near else (spread_any, collect_any)
 
     vec_block = jnp.pad(master_vec.reshape(unit, per_row), ((0, 0), (0, 128 - per_row)))
-    one = gather(jnp.concatenate([master_qkv, vec_block], axis=1).astype(LOW), CUT_ONE)
-    two = gather(jnp.concatenate([master_out, master_up], axis=1).astype(LOW), CUT_TWO)
+    wait_two, wait_three = {}, {}
+    one = gather(jnp.concatenate([master_qkv, vec_block], axis=1).astype(LOW), CUT_ONE, {})
+    two = gather(jnp.concatenate([master_out, master_up], axis=1).astype(LOW), CUT_TWO, wait_two)
     if near:
-        three = spread(master_down.astype(LOW), CUT_THREE)
+        three = spread(master_down.astype(LOW), CUT_THREE, wait_three)
     else:
         whole = lax.all_gather(master_down.astype(LOW), AXES, axis=0, tiled=True)
         three = repeat(cut_up(rearrange(whole, owners, shards), CUT_THREE), 4)
     next(one)
-    two_near = next(two)
+    wait_two[0, "start"] = next(one)
     next(one)
-    three_near = next(three)
-    one_second = next(one)
-    two_first = two.send(one_second)
     one = next(one)
+    next(two)
 
     vec_rows = jnp.concatenate([one[2][:, 3 * D - CUT_ONE :], one[3][:, 3 * D - CUT_ONE :]], axis=0)
     vec = nn(order, vec_rows)[:, :per_row].reshape(per_row, D)
@@ -574,40 +591,75 @@
     slopes = jnp.exp2(-8.0 * (jnp.arange(HEADS, dtype=jnp.int32).astype(WIDE) + 1.0) / HEADS)
     x = tokens_in[0]
     dy = cotangent[0]
-    act_one, qkv = project(x, vec, order, one, two_near)
-    mixed_0, probs_0 = attend(0, qkv, far, spans, slopes, two_first + three_near)
-    two_second = two.send(qkv)
-    mixed_1, probs_1 = attend(3, qkv, far, spans, slopes, two_second + (mixed_0,))
-    three_first = three.send(mixed_0)
-    two = two.send(mixed_0)
-    mixed, hidden, act_two, gelu, gelu_slope = upward(x, (mixed_0, mixed_1), vec, order, two, three_first)
-    three_second = three.send(mixed_1)
-    three = three.send(mixed_1)
-    grad_three = down_grad(place_down, gelu, dy, three_second)
+    act_one, qkv = project(x, vec, order, one)
+    wait_two[1, "start"] = one
+    wait_two[1, "end"] = qkv
+    wait_three[0, "start"] = next(two)
+    mixed_0, probs_0 = attend(0, qkv, far, spans, slopes)
+    wait_two[2, "end"] = mixed_0
+    wait_three[1, "start"] = next(two)
+    wait_three[0, "end"] = mixed_0
+    next(three)
+    mixed_1, probs_1 = attend(3, qkv, far, spans, slopes, wait_three.get((0, "got"), ()) + (mixed_0,))
+    wait_three[1, "end"] = mixed_1
+    next(three)
+    two = next(two)
+    mixed, hidden, act_two, gelu, gelu_slope = upward(
+        x, (mixed_0, mixed_1), vec, order, two, wait_three.get((1, "got"), ())
+    )
+    wait_three[2, "end"] = mixed
+    next(three)
+    grad_three = down_grad(place_down, gelu, dy, wait_three.get((2, "got"), ()))
+    three = next(three)
     if not near:
         whole = join(grad_three)
         back = jnp.sum(ids[:, None] * (owners[:, None] == ids[None, :]), axis=0)
         grad_three = cut_up(rearrange(whole, back, shards), CUT_THREE)
-    sum_three = scatter(grad_three)
-    block_out, dur, sums_up = downward(place_down, vec, gelu, gelu_slope, dy, hidden, three, tuple(grad_three))
-    dh, dh_low, dmixed, sums = hidden_grad(vec, order, dur, dy, hidden, two, tuple(next(sum_three)))
-    grad_two = two_grad(mixed, act_two, dh_low, dur, tuple(next(sum_three)))
-    sum_two = scatter(grad_two)
-    d0 = attend_back(0, qkv, dmixed, probs_0, spans, tuple(next(sum_three)) + tuple(grad_two))
-    d1 = attend_back(3, qkv, dmixed, probs_1, spans, tuple(next(sum_three)) + tuple(next(sum_two)) + (d0[0],))
+    wait_two, wait_three, wait_one = {}, {}, {}
+
+    def arrived(waits, stage):
+        return waits.get((stage, "got"), ())
+
+    sum_three = scatter(grad_three, wait_three)
+    block_out, dur, sums_up = downward(place_down, vec, gelu, gelu_slope, dy, hidden, three)
+    wait_three[0, "end"] = dur
+    next(sum_three)
+    dh, dh_low, dmixed, sums = hidden_grad(vec, order, dur, dy, hidden, two, arrived(wait_three, 0))
+    wait_three[1, "end"] = dh_low
+    next(sum_three)
+    grad_two = two_grad(mixed, act_two, dh_low, dur, arrived(wait_three, 1))
+    wait_three[2, "end"] = grad_two
+    next(sum_three)
+    sum_two = scatter(grad_two, wait_two)
+    d0 = attend_back(0, qkv, dmixed, probs_0, spans, arrived(wait_three, 2) + tuple(grad_two))
+    wait_three[3, "end"] = d0[0]
+    next(sum_three)
+    wait_two[0, "end"] = d0[0]
+    next(sum_two)
+    d1 = attend_back(3, qkv, dmixed, probs_1, spans, arrived(wait_three, 3) + arrived(wait_two, 0) + (d0[0],))
+    wait_two[1, "end"] = d1[0]
+    next(sum_two)
     d = [z for pair in zip(d0, d1) for z in pair]
-    grad_one = one_grad(act_one, d, tuple(next(sum_two)))
-    sum_one = scatter(grad_one)
-    tokens_grad, sums_one = input_grad(
-        x, vec, order, d, dh, one, tuple(next(sum_one)) + tuple(next(sum_two))
-    )
+    grad_one = one_grad(act_one, d, arrived(wait_two, 1))
+    wait_two[2, "end"] = grad_one
+    next(sum_two)
+    sum_one = scatter(grad_one, wait_one)
+    dact = input_back(order, d, one, arrived(wait_two, 2) + tuple(grad_one))
+    wait_one[0, "end"] = dact
+    next(sum_one)
+    wait_two[3, "end"] = dact
+    next(sum_two)
+    tokens_grad, sums_one = input_grad(x, vec, dact, dh, arrived(wait_one, 0) + arrived(wait_two, 3))
+    wait_one[1, "end"] = tokens_grad
+    next(sum_one)
     vector_grad = jnp.concatenate([sums_one[:2], sums[:3], sums_up[:4], sums[3:4]], axis=0)
     blocks = jnp.take(vector_grad.reshape(shards, share), inverse, axis=0, mode="clip")
+    (blocks,) = tie((blocks,), arrived(wait_one, 1))
     if near:
         sum_vec = collect_vec(blocks)
     else:
         sum_vec = lax.psum_scatter(blocks.reshape(-1), AXES, scatter_dimension=0, tiled=True)
-    sum_one, sum_two, sum_three = [list(z)[-1][0] for z in (sum_one, sum_two, sum_three)]
+    sum_one, sum_two, sum_three = [list(z)[-1] for z in (sum_one, sum_two, sum_three)]
     upd_qkv = adamw(master_qkv, first_qkv, second_qkv, sum_one, RATE_MATRIX, DECAY_MATRIX)
     upd_out = adamw(master_out, first_out, second_out, sum_two[:, :D], RATE_MATRIX, DECAY_MATRIX)
     upd_up = adamw(master_up, first_up, second_up, sum_two[:, D:], RATE_MATRIX, DECAY_MATRIX)

time: 388 us -> 332 us (0.86)
  waiting for transfers between devices: 108 us -> 45.5 us
  other arithmetic: 21.5 us -> 30.7 us
  Pallas kernels: 160 us -> 152 us
    ppermute x60, waiting for transfers between devices: 108 us -> 45.5 us  [swap(): return lax.ppermute(value, AXES, pairs)]
    pallas_call x8 -> x9, Pallas kernels: 115 us -> 108 us  [whole_call(): pl.pallas_call(later(kernel, len(args), len(after)), in_specs=specs + [pl...]
    unnamed x121 -> x136, local copies, waits for them, and re-layouts: 13.3 us -> 11.4 us
  transfers between devices with their start and end apart: 60 -> 60, of which waited for: 26 -> 16; matrix products, arithmetic and copies ran while one was open for 7% -> 8% of each run, Pallas kernels for 35% -> 46%
where the time goes in v1:
time: 332 us; the launch traced here: 328 us
  Pallas kernels  152 us (46%)
  starting transfers between devices  63.1 us (19%)
  waiting for transfers between devices  45.5 us (14%)
  other arithmetic  30.7 us (9%)
  local copies, waits for them, and re-layouts  25.6 us (8%)
  between operations  10 us (3%)
    pallas_call x9, Pallas kernels, whole_call(): pl.pallas_call(later(kernel, len(args), len(after)), in_specs=specs + [pl...  108 us
    ppermute x60, starting transfers between devices, swap(): return lax.ppermute(value, AXES, pairs)  63.1 us
    ppermute x60, waiting for transfers between devices, swap(): return lax.ppermute(value, AXES, pairs)  45.5 us
    pallas_call x2, Pallas kernels, attend_back(): pl.pallas_call(later(attend_back_kernel, 6, len(after)), grid_spec=pltpu....  24.3 us
    pallas_call x2, Pallas kernels, attend(): pl.pallas_call(later(functools.partial(attend_kernel, base), 6, len(after...  20.2 us
    unnamed x136, local copies, waits for them, and re-layouts  11.4 us
  transfers between devices with their start and end apart: 60, of which 16 were waited for; matrix products, arithmetic and copies ran while one was open for 8% of the time, Pallas kernels for 46%

profile of v1, /device:TPU:0, one launch (start us, length us, event | category | flops | bytes accessed | tf_op | source)
XLA Modules:
  0.0 327.8 jit_solution(16549797965254229930)
XLA Ops:
  2.5 3.1 collective-permute-start
  5.6 2.6 collective-permute-start.1
  15.1 1.1 and_select_fusion
  19.8 1.2 broadcast_multiply_fusion
  21.2 1.3 fusion.refs_2_.refs_4_.refs_1_.refs_0_
  23.5 1.8 collective-permute-start.4
  25.8 1.6 collective-permute-start.3
  27.4 4.6 %collective-permute-done.3 = bf16[96,1152]{1,0:T(8,128)(2,1)S(1)} collective-permute-done((bf16[96,1152]{1,0:T(8,128)(2,1)S(1)}, bf16[96,1152]{1,0:T(8,128)(2,1)S(1)}, u32[]{:S(2)}, u32[]{:S(2)}) %collective-permute-start.3) | collective-permute-done | bytes 221216 | tf_op jit(solution)/shard_map/ppermute | solution.py:445
  32.8 3.5 %collective-permute-start.10 = (bf16[24,3840]{1,0:T(8,128)(2,1)S(1)}, bf16[24,3840]{1,0:T(8,128)(2,1)S(1)}, u32[]{:S(2)}, u32[]{:S(2)}) collective-permute-start(bf16[24,3840]{1,0:T(8,128)(2,1)S(1)} %pad_maximum_fusion.15), channel_id=1, source_target_pairs={{0,16},{1,17},{2,18},{3,19},{4,20},{5,21},{6,22},{7,23},{8,24},{9,... | collective-permute-start | bytes 552968 | tf_op jit(solution)/shard_map/ppermute | solution.py:445
  36.6 1.8 sqrt_select_fusion.refs_5_
  38.9 1.5 collective-permute-start.6
  40.3 8.1 %collective-permute-done.10 = bf16[24,3840]{1,0:T(8,128)(2,1)S(1)} collective-permute-done((bf16[24,3840]{1,0:T(8,128)(2,1)S(1)}, bf16[24,3840]{1,0:T(8,128)(2,1)S(1)}, u32[]{:S(2)}, u32[]{:S(2)}) %collective-permute-start.10) | collective-permute-done | bytes 184352 | tf_op jit(solution)/shard_map/ppermute | solution.py:445
  50.0 3.1 collective-permute-done.7.refs_4_.refs_8_
  54.1 1.3 collective-permute-start.12
  55.3 1.5 collective-permute-start.13
  58.4 9.6 %project.1 = (bf16[576,768]{1,0:T(8,128)(2,1)}, bf16[576,2304]{1,0:T(8,128)(2,1)}) custom-call(bf16[576,768]{1,0:T(8,128)(2,1)} %bitcast.29, f32[16,768]{1,0:T(8,128)} %pad.10.refs_1_.refs_3_.refs_0_, bf16[768,768]{1,0:T(8,128)(2,1)} %fusion.refs_2_.refs_4_.refs_1_.refs_0_, bf16[384,1152]{1,0:T(8,128)(2,1)} %copy-done.2, bf16[384,1152]{1,0:T(8,128)(2,1)} %copy-done.24, ...), custom_call_target="tpu_custom_call" | custom-call | flops 2717908992 | bytes 9388032 | tf_op jit(solution)/shard_map/project/pallas_call | solution.py:60
  69.1 1.4 collective-permute-start.14
  70.6 2.7 collective-permute-start.15
  75.1 10.1 %attend.2 = (bf16[576,384]{1,0:T(8,128)(2,1)}, bf16[6,4,256,256]{3,2,1,0:T(8,128)(2,1)}) custom-call(s32[4,3]{1,0:T(4,128)} %pad_add_fusion.1.refs_0_, f32[12]{0:T(128)} %multiply_exponential_fusion.refs_1_, bf16[576,2304]{1,0:T(8,128)(2,1)} %get-tuple-element.210.refs_2_.refs_3_.refs_4_.refs_1_, ...), custom_call_target="tpu_custom_call" | custom-call | flops 8999999488 | bytes 6000000 | tf_op jit(solution)/shard_map/attend/pallas_call | solution.py:142
  85.3 5.4 %collective-permute-done.17 = bf16[192,1920]{1,0:T(8,128)(2,1)S(1)} collective-permute-done((bf16[192,1920]{1,0:T(8,128)(2,1)S(1)}, bf16[192,1920]{1,0:T(8,128)(2,1)S(1)}, u32[]{:S(2)}, u32[]{:S(2)}) %collective-permute-start.17) | collective-permute-done | bytes 737312 | tf_op jit(solution)/shard_map/ppermute | solution.py:445
  95.2 10.1 %attend.3 = (bf16[576,384]{1,0:T(8,128)(2,1)}, bf16[6,4,256,256]{3,2,1,0:T(8,128)(2,1)}) custom-call(s32[4,3]{1,0:T(4,128)} %pad_add_fusion.1.refs_0_, f32[12]{0:T(128)} %multiply_exponential_fusion.refs_1_, bf16[576,2304]{1,0:T(8,128)(2,1)} %get-tuple-element.210.refs_2_.refs_3_.refs_4_.refs_1_, ...), custom_call_target="tpu_custom_call" | custom-call | flops 8999999488 | bytes 6000000 | tf_op jit(solution)/shard_map/attend/pallas_call | solution.py:142
  105.5 1.3 collective-permute-start.23
  107.1 18.9 %upward.1 = (bf16[576,768]{1,0:T(8,128)(2,1)}, f32[576,768]{1,0:T(8,128)}, bf16[576,768]{1,0:T(8,128)(2,1)}, bf16[576,3072]{1,0:T(8,128)(2,1)}, bf16[576,3072]{1,0:T(8,128)(2,1)}) custom-call(bf16[576,768]{1,0:T(8,128)(2,1)} %bitcast.30, bf16[576,384]{1,0:T(8,128)(2,1)} %get-tuple-element.211.refs_9_.refs_1_, bf16[576,384]{1,0:T(8,128)(2,1)} %get-tuple-element.228.refs_2_, ...), custom_call_target="tpu_custom_call" | custom-call | flops 9512681472 | bytes 19513344 | tf_op jit(solution)/shard_map/upward/pallas_call | solution.py:60
  127.8 12.2 %down_grad.1 = (bf16[1536,384]{1,0:T(8,128)(2,1)}, bf16[1536,384]{1,0:T(8,128)(2,1)}, bf16[1536,384]{1,0:T(8,128)(2,1)}, bf16[1536,384]{1,0:T(8,128)(2,1)}) custom-call(s32[32]{0:T(128)} %get-tuple-element.371.refs_0_, bf16[576,3072]{1,0:T(8,128)(2,1)} %get-tuple-element.247.refs_2_.refs_1_, bf16[576,768]{1,0:T(8,128)(2,1)} %bitcast.26, ...), custom_call_target="tpu_custom_call" | custom-call | flops 2717908992 | bytes 9142400 | tf_op jit(solution)/shard_map/down_grad/pallas_call | solution.py:60
  142.2 14.9 %downward.1 = (bf16[576,768]{1,0:T(8,128)(2,1)}, bf16[576,3072]{1,0:T(8,128)(2,1)}, f32[8,768]{1,0:T(8,128)}) custom-call(s32[32]{0:T(128)} %get-tuple-element.371.refs_0_, f32[16,768]{1,0:T(8,128)} %pad.10.refs_1_.refs_3_.refs_0_, bf16[576,3072]{1,0:T(8,128)(2,1)} %get-tuple-element.247.refs_2_.refs_1_, bf16[576,3072]{1,0:T(8,128)(2,1)} %get-tuple-element.248.refs_3_, ...), custom_call_target="tpu_custom_call" | custom-call | flops 5435817984 | bytes 18948224 | tf_op jit(solution)/shard_map/downward/pallas_call | solution.py:60
  159.9 2.0 collective-permute-start.29
  162.5 18.0 %hidden_grad.1 = (f32[576,768]{1,0:T(8,128)}, bf16[576,768]{1,0:T(8,128)(2,1)}, bf16[576,768]{1,0:T(8,128)(2,1)}, f32[8,768]{1,0:T(8,128)}) custom-call(f32[16,768]{1,0:T(8,128)} %pad.10.refs_1_.refs_3_.refs_0_, bf16[768,768]{1,0:T(8,128)(2,1)} %fusion.refs_2_.refs_4_.refs_1_.refs_0_, bf16[576,3072]{1,0:T(8,128)(2,1)} %get-tuple-element.268.refs_2_.refs_3_, ...), custom_call_target="tpu_custom_call" | custom-call | flops 4756340736 | bytes 16883712 | tf_op jit(solution)/shard_map/hidden_grad/pallas_call | solution.py:60
  183.9 1.5 collective-permute-start.31
  185.5 10.2 %two_grad.1 = (bf16[384,1920]{1,0:T(8,128)(2,1)}, bf16[384,1920]{1,0:T(8,128)(2,1)}, bf16[384,1920]{1,0:T(8,128)(2,1)}, bf16[384,1920]{1,0:T(8,128)(2,1)}) custom-call(bf16[576,768]{1,0:T(8,128)(2,1)} %get-tuple-element.256.refs_0_, bf16[576,768]{1,0:T(8,128)(2,1)} %get-tuple-element.286.refs_1_, bf16[576,768]{1,0:T(8,128)(2,1)} %get-tuple-element.281.refs_2_, ...), custom_call_target="tpu_custom_call" | custom-call | flops 3397386240 | bytes 12091392 | tf_op jit(solution)/shard_map/two_grad/pallas_call | solution.py:60
  197.5 4.1 %collective-permute-start.34 = (bf16[96,768]{1,0:T(8,128)(2,1)S(1)}, bf16[96,768]{1,0:T(8,128)(2,1)S(1)}, u32[]{:S(2)}, u32[]{:S(2)}) collective-permute-start(bf16[96,768]{1,0:T(8,128)(2,1)S(1)} %get-tuple-element.296), channel_id=1, source_target_pairs={{0,16},{1,17},{2,18},{3,19},{4,20},{5,21},{6,22},{7,23},{8,24},{9,... | collective-permute-start | bytes 442376 | tf_op jit(solution)/shard_map/ppermute | solution.py:445
  201.6 12.1 %attend_back.2 = (bf16[576,384]{1,0:T(8,128)(2,1)}, bf16[576,384]{1,0:T(8,128)(2,1)}, bf16[576,384]{1,0:T(8,128)(2,1)}) custom-call(s32[4,3]{1,0:T(4,128)} %pad_add_fusion.1.refs_0_, bf16[576,2304]{1,0:T(8,128)(2,1)} %get-tuple-element.210.refs_2_.refs_3_.refs_4_.refs_1_, bf16[576,2304]{1,0:T(8,128)(2,1)} %get-tuple-element.210.refs_2_.refs_3_.refs_4_.refs_1_, ...), custom_call_target="tpu_custom_call" | custom-call | flops 12000000000 | bytes 6000000 | tf_op jit(solution)/shard_map/attend_back/pallas_call | solution.py:189
  213.8 2.7 convert_add_fusion.1
  218.2 1.8 convert_add_fusion
  221.0 1.8 collective-permute-start.38
  222.9 12.3 %attend_back.3 = (bf16[576,384]{1,0:T(8,128)(2,1)}, bf16[576,384]{1,0:T(8,128)(2,1)}, bf16[576,384]{1,0:T(8,128)(2,1)}) custom-call(s32[4,3]{1,0:T(4,128)} %pad_add_fusion.1.refs_0_, bf16[576,2304]{1,0:T(8,128)(2,1)} %get-tuple-element.210.refs_2_.refs_3_.refs_4_.refs_1_, bf16[576,2304]{1,0:T(8,128)(2,1)} %get-tuple-element.210.refs_2_.refs_3_.refs_4_.refs_1_, ...), custom_call_target="tpu_custom_call" | custom-call | flops 12000000000 | bytes 6000000 | tf_op jit(solution)/shard_map/attend_back/pallas_call | solution.py:189
  235.2 1.7 collective-permute-done.38.refs_7_
  236.9 2.4 collective-permute-done.39.refs_8_
  239.6 1.4 maximum_add_fusion
  241.0 2.0 collective-permute-start.40
  243.0 1.1 collective-permute-start.41
  244.1 1.1 multiply_subtract_fusion
  245.2 6.8 %one_grad.1 = (bf16[384,1152]{1,0:T(8,128)(2,1)}, bf16[384,1152]{1,0:T(8,128)(2,1)}, bf16[384,1152]{1,0:T(8,128)(2,1)}, bf16[384,1152]{1,0:T(8,128)(2,1)}) custom-call(bf16[576,768]{1,0:T(8,128)(2,1)} %get-tuple-element.313.refs_0_, bf16[576,384]{1,0:T(8,128)(2,1)} %get-tuple-element.291.refs_11_.refs_1_, bf16[576,384]{1,0:T(8,128)(2,1)} %get-tuple-element.300.refs_2_, ...), custom_call_target="tpu_custom_call" | custom-call | flops 2038431744 | bytes 7077888 | tf_op jit(solution)/shard_map/one_grad/pallas_call | solution.py:60
  254.5 2.7 collective-permute-start.45
  257.9 8.8 %input_back.1.refs_2_ = f32[576,768]{1,0:T(8,128)} custom-call(bf16[768,768]{1,0:T(8,128)(2,1)} %fusion.refs_2_.refs_4_.refs_1_.refs_0_, bf16[576,384]{1,0:T(8,128)(2,1)} %get-tuple-element.291.refs_11_.refs_1_, bf16[576,384]{1,0:T(8,128)(2,1)} %get-tuple-element.300.refs_2_, bf16[576,384]{1,0:T(8,128)(2,1)} %get-tuple-element.301.refs_3_, ...), custom_call_target="tpu_custom_call" | custom-call | flops 2717908992 | bytes 9338880 | tf_op jit(solution)/shard_map/input_back/pallas_call | solution.py:60
  266.7 4.1 %collective-permute-done.45.refs_7_ = bf16[24,3840]{1,0:T(8,128)(2,1)S(1)} collective-permute-done((bf16[24,3840]{1,0:T(8,128)(2,1)S(1)}, bf16[24,3840]{1,0:T(8,128)(2,1)S(1)}, u32[]{:S(2)}, u32[]{:S(2)}) %collective-permute-start.45) | collective-permute-done | bytes 184352 | tf_op jit(solution)/shard_map/ppermute | solution.py:445
  272.6 1.5 convert_add_fusion.4
  276.0 1.1 collective-permute-start.47
  277.1 1.4 collective-permute-start.48
  278.6 1.1 multiply_subtract_fusion.1
  279.7 8.5 %input_grad.1 = (f32[576,768]{1,0:T(8,128)}, f32[8,768]{1,0:T(8,128)}) custom-call(bf16[576,768]{1,0:T(8,128)(2,1)} %bitcast.31, f32[16,768]{1,0:T(8,128)} %pad.10.refs_1_.refs_3_.refs_0_, f32[576,768]{1,0:T(8,128)} %input_back.1.refs_2_, f32[576,768]{1,0:T(8,128)} %get-tuple-element.318.refs_3_, bf16[384,1152]{1,0:T(8,128)(2,1)} %copy-done.21, ...), custom_call_target="tpu_custom_call" | custom-call | flops 2038431744 | bytes 6266880 | tf_op jit(solution)/shard_map/input_grad/pallas_call | solution.py:60
  289.5 1.5 reshape.168
  291.0 2.1 gather_fusion
  293.9 1.7 multiply_subtract_fusion.3
  297.3 2.7 collective-permute-done.55
  300.5 1.1 slice_add_fusion.2
  301.6 1.9 collective-permute-done.56
  303.6 2.5 collective-permute-start.59
  306.1 2.3 collective-permute-start.58
  308.5 1.1 maximum_add_fusion.2
  312.0 3.7 %collective-permute-done.49 = bf16[96,1152]{1,0:T(8,128)(2,1)S(1)} collective-permute-done((bf16[96,1152]{1,0:T(8,128)(2,1)S(1)}, bf16[96,1152]{1,0:T(8,128)(2,1)S(1)}, u32[]{:S(2)}, u32[]{:S(2)}) %collective-permute-start.49) | collective-permute-done | bytes 221216 | tf_op jit(solution)/shard_map/ppermute | solution.py:445
  316.5 2.0 collective-permute-start.51
  318.5 1.1 collective-permute-start.52
  319.6 1.4 collective-permute-start.53
  322.4 4.1 %collective-permute-done.52 = bf16[24,2304]{1,0:T(8,128)(2,1)S(1)} collective-permute-done((bf16[24,2304]{1,0:T(8,128)(2,1)S(1)}, bf16[24,2304]{1,0:T(8,128)(2,1)S(1)}, u32[]{:S(2)}, u32[]{:S(2)}) %collective-permute-start.52) | collective-permute-done | bytes 110624 | tf_op jit(solution)/shard_map/ppermute | solution.py:445
  (334 shorter events, 51.9 us)
Async XLA Ops:
  0.7 21.9 %copy-start.15 = (f32[24,3072]{1,0:T(8,128)S(1)}, f32[24,3072]{1,0:T(8,128)}, u32[]{:S(2)}) copy-start(f32[24,3072]{1,0:T(8,128)} %param.29) | copy-start | bytes 884740
  0.7 21.9 %copy-start.33 = (f32[24,768]{1,0:T(8,128)S(1)}, f32[24,768]{1,0:T(8,128)}, u32[]{:S(2)}) copy-start(f32[24,768]{1,0:T(8,128)} %param.28) | copy-start | bytes 221188
  2.5 20.9 %collective-permute-start = (bf16[24,2432]{1,0:T(8,128)(2,1)S(1)}, bf16[24,2432]{1,0:T(8,128)(2,1)S(1)}, u32[]{:S(2)}, u32[]{:S(2)}) collective-permute-start(bf16[24,2432]{1,0:T(8,128)(2,1)S(1)} %fusion.23), channel_id=1, source_target_pairs={{0,8},{1,9},{2,10},{3,11},{4,12},{5,13},{6,14},{7,15},{8,0},{9,1},... | collective-permute-start | bytes 350216 | tf_op jit(solution)/shard_map/ppermute | solution.py:445
  5.6 17.8 %collective-permute-start.1 = (bf16[24,2432]{1,0:T(8,128)(2,1)S(1)}, bf16[24,2432]{1,0:T(8,128)(2,1)S(1)}, u32[]{:S(2)}, u32[]{:S(2)}) collective-permute-start(bf16[24,2432]{1,0:T(8,128)(2,1)S(1)} %fusion.23), channel_id=1, source_target_pairs={{0,16},{1,17},{2,18},{3,19},{4,20},{5,21},{6,22},{7,23},{8,24},{9,... | collective-permute-start | bytes 350216 | tf_op jit(solution)/shard_map/ppermute | solution.py:445
  8.2 15.2 %collective-permute-start.2 = (bf16[24,2432]{1,0:T(8,128)(2,1)S(1)}, bf16[24,2432]{1,0:T(8,128)(2,1)S(1)}, u32[]{:S(2)}, u32[]{:S(2)}) collective-permute-start(bf16[24,2432]{1,0:T(8,128)(2,1)S(1)} %fusion.23), channel_id=1, source_target_pairs={{0,24},{1,25},{2,26},{3,27},{4,28},{5,29},{6,30},{7,31},{8,16},{9,... | collective-permute-start | bytes 350216 | tf_op jit(solution)/shard_map/ppermute | solution.py:445
  23.5 8.5 %collective-permute-start.4 = (bf16[96,1280]{1,0:T(8,128)(2,1)S(1)}, bf16[96,1280]{1,0:T(8,128)(2,1)S(1)}, u32[]{:S(2)}, u32[]{:S(2)}) collective-permute-start(bf16[96,1280]{1,0:T(8,128)(2,1)S(1)} %slice.372), channel_id=1, source_target_pairs={{0,4},{1,5},{2,6},{3,7},{4,0},{5,1},{6,2},{7,3},{8,12},{9,13},{10,... | collective-permute-start | bytes 737288 | tf_op jit(solution)/shard_map/ppermute | solution.py:445
  25.8 6.2 %collective-permute-start.3 = (bf16[96,1152]{1,0:T(8,128)(2,1)S(1)}, bf16[96,1152]{1,0:T(8,128)(2,1)S(1)}, u32[]{:S(2)}, u32[]{:S(2)}) collective-permute-start(bf16[96,1152]{1,0:T(8,128)(2,1)S(1)} %slice.371), channel_id=1, source_target_pairs={{0,2},{1,3},{2,0},{3,1},{4,6},{5,7},{6,4},{7,5},{8,10},{9,11},{10,... | collective-permute-start | bytes 663560 | tf_op jit(solution)/shard_map/ppermute | solution.py:445
  32.1 8.2 %collective-permute-start.9 = (bf16[24,3840]{1,0:T(8,128)(2,1)S(1)}, bf16[24,3840]{1,0:T(8,128)(2,1)S(1)}, u32[]{:S(2)}, u32[]{:S(2)}) collective-permute-start(bf16[24,3840]{1,0:T(8,128)(2,1)S(1)} %pad_maximum_fusion.15), channel_id=1, source_target_pairs={{0,8},{1,9},{2,10},{3,11},{4,12},{5,13},{6,14},{7,15},{8,0},{9,1},... | collective-permute-start | bytes 552968 | tf_op jit(solution)/shard_map/ppermute | solution.py:445
  32.8 15.7 %collective-permute-start.10 = (bf16[24,3840]{1,0:T(8,128)(2,1)S(1)}, bf16[24,3840]{1,0:T(8,128)(2,1)S(1)}, u32[]{:S(2)}, u32[]{:S(2)}) collective-permute-start(bf16[24,3840]{1,0:T(8,128)(2,1)S(1)} %pad_maximum_fusion.15), channel_id=1, source_target_pairs={{0,16},{1,17},{2,18},{3,19},{4,20},{5,21},{6,22},{7,23},{8,24},{9,... | collective-permute-start | bytes 552968 | tf_op jit(solution)/shard_map/ppermute | solution.py:445
  36.3 12.2 %collective-permute-start.11 = (bf16[24,3840]{1,0:T(8,128)(2,1)S(1)}, bf16[24,3840]{1,0:T(8,128)(2,1)S(1)}, u32[]{:S(2)}, u32[]{:S(2)}) collective-permute-start(bf16[24,3840]{1,0:T(8,128)(2,1)S(1)} %pad_maximum_fusion.15), channel_id=1, source_target_pairs={{0,24},{1,25},{2,26},{3,27},{4,28},{5,29},{6,30},{7,31},{8,16},{9,... | collective-permute-start | bytes 552968 | tf_op jit(solution)/shard_map/ppermute | solution.py:445
  38.3 10.2 %collective-permute-start.5 = (bf16[192,1152]{1,0:T(8,128)(2,1)S(1)}, bf16[192,1152]{1,0:T(8,128)(2,1)S(1)}, u32[]{:S(2)}, u32[]{:S(2)}) collective-permute-start(bf16[192,1152]{1,0:T(8,128)(2,1)S(1)} %constant_dynamic-update-slice_fusion.4), channel_id=1, source_target_pairs={{0,4},{1,5},{2,6},{3,7},{4,0},{5,1},{6,2},{7,3},{8,12},{9,13},{10,... | collective-permute-start | bytes 1327112 | tf_op jit(solution)/shard_map/ppermute | solution.py:445
  38.9 10.1 %collective-permute-start.6 = (bf16[192,1280]{1,0:T(8,128)(2,1)S(1)}, bf16[192,1280]{1,0:T(8,128)(2,1)S(1)}, u32[]{:S(2)}, u32[]{:S(2)}) collective-permute-start(bf16[192,1280]{1,0:T(8,128)(2,1)S(1)} %constant_dynamic-update-slice_fusion.6), channel_id=1, source_target_pairs={{0,2},{1,3},{2,0},{3,1},{4,6},{5,7},{6,4},{7,5},{8,10},{9,11},{10,... | collective-permute-start | bytes 1474568 | tf_op jit(solution)/shard_map/ppermute | solution.py:445
  49.2 3.9 %collective-permute-start.8 = (bf16[384,1280]{1,0:T(8,128)(2,1)S(1)}, bf16[384,1280]{1,0:T(8,128)(2,1)S(1)}, u32[]{:S(2)}, u32[]{:S(2)}) collective-permute-start(bf16[384,1280]{1,0:T(8,128)(2,1)S(1)} %pad_maximum_fusion.6.refs_5_.refs_9_), channel_id=1, source_target_pairs={{0,1},{1,0},{2,3},{3,2},{4,5},{5,4},{6,7},{7,6},{8,9},{9,8},{10,11... | collective-permute-start | bytes 2949128 | tf_op jit(solution)/shard_map/ppermute | solution.py:445
  49.9 3.2 collective-permute-start.7
  54.1 13.9 %collective-permute-start.12 = (bf16[96,1920]{1,0:T(8,128)(2,1)S(1)}, bf16[96,1920]{1,0:T(8,128)(2,1)S(1)}, u32[]{:S(2)}, u32[]{:S(2)}) collective-permute-start(bf16[96,1920]{1,0:T(8,128)(2,1)S(1)} %get-tuple-element.221), channel_id=1, source_target_pairs={{0,2},{1,3},{2,0},{3,1},{4,6},{5,7},{6,4},{7,5},{8,10},{9,11},{10,... | collective-permute-start | bytes 1105928 | tf_op jit(solution)/shard_map/ppermute | solution.py:445
  55.3 12.7 %collective-permute-start.13 = (bf16[96,1920]{1,0:T(8,128)(2,1)S(1)}, bf16[96,1920]{1,0:T(8,128)(2,1)}, u32[]{:S(2)}, u32[]{:S(2)}) collective-permute-start(bf16[96,1920]{1,0:T(8,128)(2,1)S(1)} %get-tuple-element.223), channel_id=1, source_target_pairs={{0,4},{1,5},{2,6},{3,7},{4,0},{5,1},{6,2},{7,3},{8,12},{9,13},{10,... | collective-permute-start | bytes 1105928 | tf_op jit(solution)/shard_map/ppermute | solution.py:445
  69.1 16.0 %collective-permute-start.14 = (bf16[96,768]{1,0:T(8,128)(2,1)S(1)}, bf16[96,768]{1,0:T(8,128)(2,1)S(1)}, u32[]{:S(2)}, u32[]{:S(2)}) collective-permute-start(bf16[96,768]{1,0:T(8,128)(2,1)S(1)} %convert_element_type.178), channel_id=1, source_target_pairs={{0,8},{1,9},{2,10},{3,11},{4,12},{5,13},{6,14},{7,15},{8,0},{9,1},... | collective-permute-start | bytes 442376 | tf_op jit(solution)/shard_map/ppermute | solution.py:445
  70.6 14.6 %collective-permute-start.15 = (bf16[96,768]{1,0:T(8,128)(2,1)S(1)}, bf16[96,768]{1,0:T(8,128)(2,1)S(1)}, u32[]{:S(2)}, u32[]{:S(2)}) collective-permute-start(bf16[96,768]{1,0:T(8,128)(2,1)S(1)} %convert_element_type.178), channel_id=1, source_target_pairs={{0,16},{1,17},{2,18},{3,19},{4,20},{5,21},{6,22},{7,23},{8,24},{9,... | collective-permute-start | bytes 442376 | tf_op jit(solution)/shard_map/ppermute | solution.py:445
  73.3 12.0 %collective-permute-start.16 = (bf16[96,768]{1,0:T(8,128)(2,1)S(1)}, bf16[96,768]{1,0:T(8,128)(2,1)S(1)}, u32[]{:S(2)}, u32[]{:S(2)}) collective-permute-start(bf16[96,768]{1,0:T(8,128)(2,1)S(1)} %convert_element_type.178), channel_id=1, source_target_pairs={{0,24},{1,25},{2,26},{3,27},{4,28},{5,29},{6,30},{7,31},{8,16},{9,... | collective-permute-start | bytes 442376 | tf_op jit(solution)/shard_map/ppermute | solution.py:445
  73.6 17.1 %collective-permute-start.17 = (bf16[192,1920]{1,0:T(8,128)(2,1)S(1)}, bf16[192,1920]{1,0:T(8,128)(2,1)S(1)}, u32[]{:S(2)}, u32[]{:S(2)}) collective-permute-start(bf16[192,1920]{1,0:T(8,128)(2,1)S(1)} %constant_dynamic-update-slice_fusion.12), channel_id=1, source_target_pairs={{0,4},{1,5},{2,6},{3,7},{4,0},{5,1},{6,2},{7,3},{8,12},{9,13},{10,... | collective-permute-start | bytes 2211848 | tf_op jit(solution)/shard_map/ppermute | solution.py:445
  74.6 17.1 %collective-permute-start.18 = (bf16[192,1920]{1,0:T(8,128)(2,1)S(1)}, bf16[192,1920]{1,0:T(8,128)(2,1)S(1)}, u32[]{:S(2)}, u32[]{:S(2)}) collective-permute-start(bf16[192,1920]{1,0:T(8,128)(2,1)S(1)} %constant_dynamic-update-slice_fusion.14), channel_id=1, source_target_pairs={{0,2},{1,3},{2,0},{3,1},{4,6},{5,7},{6,4},{7,5},{8,10},{9,11},{10,... | collective-permute-start | bytes 2211848 | tf_op jit(solution)/shard_map/ppermute | solution.py:445
  93.2 14.0 %collective-permute-start.19 = (bf16[384,1920]{1,0:T(8,128)(2,1)S(1)}, bf16[384,1920]{1,0:T(8,128)(2,1)}, u32[]{:S(2)}, u32[]{:S(2)}) collective-permute-start(bf16[384,1920]{1,0:T(8,128)(2,1)S(1)} %constant_dynamic-update-slice_fusion.16.refs_5_), channel_id=1, source_target_pairs={{0,1},{1,0},{2,3},{3,2},{4,5},{5,4},{6,7},{7,6},{8,9},{9,8},{10,11... | collective-permute-start | bytes 4423688 | tf_op jit(solution)/shard_map/ppermute | solution.py:445
  93.2 14.0 %collective-permute-start.20 = (bf16[384,1920]{1,0:T(8,128)(2,1)S(1)}, bf16[384,1920]{1,0:T(8,128)(2,1)}, u32[]{:S(2)}, u32[]{:S(2)}) collective-permute-start(bf16[384,1920]{1,0:T(8,128)(2,1)S(1)} %pad_maximum_fusion.1.refs_7_), channel_id=1, source_target_pairs={{0,1},{1,0},{2,3},{3,2},{4,5},{5,4},{6,7},{7,6},{8,9},{9,8},{10,11... | collective-permute-start | bytes 4423688 | tf_op jit(solution)/shard_map/ppermute | solution.py:445
  93.8 11.6 %collective-permute-start.21 = (bf16[384,384]{1,0:T(8,128)(2,1)S(1)}, bf16[384,384]{1,0:T(8,128)(2,1)S(1)}, u32[]{:S(2)}, u32[]{:S(2)}) collective-permute-start(bf16[384,384]{1,0:T(8,128)(2,1)S(1)} %get-tuple-element.250), channel_id=1, source_target_pairs={{0,2},{1,3},{2,0},{3,1},{4,6},{5,7},{6,4},{7,5},{8,10},{9,11},{10,... | collective-permute-start | bytes 884744 | tf_op jit(solution)/shard_map/ppermute | solution.py:445
  94.4 10.9 %collective-permute-start.22 = (bf16[384,384]{1,0:T(8,128)(2,1)S(1)}, bf16[384,384]{1,0:T(8,128)(2,1)S(1)}, u32[]{:S(2)}, u32[]{:S(2)}) collective-permute-start(bf16[384,384]{1,0:T(8,128)(2,1)S(1)} %get-tuple-element.252), channel_id=1, source_target_pairs={{0,4},{1,5},{2,6},{3,7},{4,0},{5,1},{6,2},{7,3},{8,12},{9,13},{10,... | collective-permute-start | bytes 884744 | tf_op jit(solution)/shard_map/ppermute | solution.py:445
  105.5 20.5 %collective-permute-start.23 = (bf16[768,384]{1,0:T(8,128)(2,1)S(1)}, bf16[768,384]{1,0:T(8,128)(2,1)S(1)}, u32[]{:S(2)}, u32[]{:S(2)}) collective-permute-start(bf16[768,384]{1,0:T(8,128)(2,1)S(1)} %pad_maximum_fusion.9), channel_id=1, source_target_pairs={{0,4},{1,5},{2,6},{3,7},{4,0},{5,1},{6,2},{7,3},{8,12},{9,13},{10,... | collective-permute-start | bytes 1769480 | tf_op jit(solution)/shard_map/ppermute | solution.py:445
  106.9 19.2 %collective-permute-start.24 = (bf16[768,384]{1,0:T(8,128)(2,1)S(1)}, bf16[768,384]{1,0:T(8,128)(2,1)S(1)}, u32[]{:S(2)}, u32[]{:S(2)}) collective-permute-start(bf16[768,384]{1,0:T(8,128)(2,1)S(1)} %pad_maximum_fusion.10), channel_id=1, source_target_pairs={{0,2},{1,3},{2,0},{3,1},{4,6},{5,7},{6,4},{7,5},{8,10},{9,11},{10,... | collective-permute-start | bytes 1769480 | tf_op jit(solution)/shard_map/ppermute | solution.py:445
  127.2 14.0 %collective-permute-start.25 = (bf16[1536,384]{1,0:T(8,128)(2,1)S(1)}, bf16[1536,384]{1,0:T(8,128)(2,1)S(1)}, u32[]{:S(2)}, u32[]{:S(2)}) collective-permute-start(bf16[1536,384]{1,0:T(8,128)(2,1)S(1)} %pad_maximum_fusion.3.refs_6_), channel_id=1, source_target_pairs={{0,1},{1,0},{2,3},{3,2},{4,5},{5,4},{6,7},{7,6},{8,9},{9,8},{10,11... | collective-permute-start | bytes 3538952 | tf_op jit(solution)/shard_map/ppermute | solution.py:445
  127.3 13.9 %collective-permute-start.26 = (bf16[1536,384]{1,0:T(8,128)(2,1)S(1)}, bf16[1536,384]{1,0:T(8,128)(2,1)}, u32[]{:S(2)}, u32[]{:S(2)}) collective-permute-start(bf16[1536,384]{1,0:T(8,128)(2,1)S(1)} %pad_maximum_fusion.4.refs_8_), channel_id=1, source_target_pairs={{0,1},{1,0},{2,3},{3,2},{4,5},{5,4},{6,7},{7,6},{8,9},{9,8},{10,11... | collective-permute-start | bytes 3538952 | tf_op jit(solution)/shard_map/ppermute | solution.py:445
  140.0 17.2 %collective-permute-start.27 = (bf16[1536,384]{1,0:T(8,128)(2,1)}, bf16[1536,384]{1,0:T(8,128)(2,1)S(1)}, u32[]{:S(2)}, u32[]{:S(2)}) collective-permute-start(bf16[1536,384]{1,0:T(8,128)(2,1)} %get-tuple-element.271), channel_id=1, source_target_pairs={{0,1},{1,0},{2,3},{3,2},{4,5},{5,4},{6,7},{7,6},{8,9},{9,8},{10,11... | collective-permute-start | bytes 3538952 | tf_op jit(solution)/shard_map/ppermute | solution.py:445
  140.1 17.0 %collective-permute-start.28 = (bf16[1536,384]{1,0:T(8,128)(2,1)}, bf16[1536,384]{1,0:T(8,128)(2,1)S(1)}, u32[]{:S(2)}, u32[]{:S(2)}) collective-permute-start(bf16[1536,384]{1,0:T(8,128)(2,1)} %get-tuple-element.272), channel_id=1, source_target_pairs={{0,1},{1,0},{2,3},{3,2},{4,5},{5,4},{6,7},{7,6},{8,9},{9,8},{10,11... | collective-permute-start | bytes 3538952 | tf_op jit(solution)/shard_map/ppermute | solution.py:445
  142.2 14.9 %copy-start.20 = (bf16[1536,384]{1,0:T(8,128)(2,1)S(1)}, bf16[1536,384]{1,0:T(8,128)(2,1)}, u32[]{:S(2)}) copy-start(bf16[1536,384]{1,0:T(8,128)(2,1)} %get-tuple-element.275) | copy-start | bytes 3538948
  159.9 22.1 %copy-start.55 = (f32[8,768]{1,0:T(8,128)S(1)}, f32[8,768]{1,0:T(8,128)}, u32[]{:S(2)}) copy-start(f32[8,768]{1,0:T(8,128)} %get-tuple-element.351) | copy-start | bytes 73732
  159.9 22.7 %collective-permute-start.29 = (bf16[768,384]{1,0:T(8,128)(2,1)S(1)}, bf16[768,384]{1,0:T(8,128)(2,1)S(1)}, u32[]{:S(2)}, u32[]{:S(2)}) collective-permute-start(bf16[768,384]{1,0:T(8,128)(2,1)S(1)} %slice.516), channel_id=1, source_target_pairs={{0,4},{1,5},{2,6},{3,7},{4,0},{5,1},{6,2},{7,3},{8,12},{9,13},{10,... | collective-permute-start | bytes 1769480 | tf_op jit(solution)/shard_map/ppermute | solution.py:445
  162.0 20.7 %collective-permute-start.30 = (bf16[768,384]{1,0:T(8,128)(2,1)S(1)}, bf16[768,384]{1,0:T(8,128)(2,1)S(1)}, u32[]{:S(2)}, u32[]{:S(2)}) collective-permute-start(bf16[768,384]{1,0:T(8,128)(2,1)S(1)} %pad_maximum_fusion.11), channel_id=1, source_target_pairs={{0,2},{1,3},{2,0},{3,1},{4,6},{5,7},{6,4},{7,5},{8,10},{9,11},{10,... | collective-permute-start | bytes 1769480 | tf_op jit(solution)/shard_map/ppermute | solution.py:445
  183.9 12.3 %collective-permute-start.31 = (bf16[384,384]{1,0:T(8,128)(2,1)S(1)}, bf16[384,384]{1,0:T(8,128)(2,1)S(1)}, u32[]{:S(2)}, u32[]{:S(2)}) collective-permute-start(bf16[384,384]{1,0:T(8,128)(2,1)S(1)} %slice.521), channel_id=1, source_target_pairs={{0,2},{1,3},{2,0},{3,1},{4,6},{5,7},{6,4},{7,5},{8,10},{9,11},{10,... | collective-permute-start | bytes 884744 | tf_op jit(solution)/shard_map/ppermute | solution.py:445
  185.4 10.8 %collective-permute-start.32 = (bf16[384,384]{1,0:T(8,128)(2,1)S(1)}, bf16[384,384]{1,0:T(8,128)(2,1)S(1)}, u32[]{:S(2)}, u32[]{:S(2)}) collective-permute-start(bf16[384,384]{1,0:T(8,128)(2,1)S(1)} %slice.520), channel_id=1, source_target_pairs={{0,4},{1,5},{2,6},{3,7},{4,0},{5,1},{6,2},{7,3},{8,12},{9,13},{10,... | collective-permute-start | bytes 884744 | tf_op jit(solution)/shard_map/ppermute | solution.py:445
  195.7 18.1 %collective-permute-start.36 = (bf16[384,1920]{1,0:T(8,128)(2,1)}, bf16[384,1920]{1,0:T(8,128)(2,1)}, u32[]{:S(2)}, u32[]{:S(2)}) collective-permute-start(bf16[384,1920]{1,0:T(8,128)(2,1)} %get-tuple-element.298.refs_9_), channel_id=1, source_target_pairs={{0,1},{1,0},{2,3},{3,2},{4,5},{5,4},{6,7},{7,6},{8,9},{9,8},{10,11... | collective-permute-start | bytes 4423688 | tf_op jit(solution)/shard_map/ppermute | solution.py:445
  195.7 18.1 %collective-permute-start.37 = (bf16[384,1920]{1,0:T(8,128)(2,1)}, bf16[384,1920]{1,0:T(8,128)(2,1)S(1)}, u32[]{:S(2)}, u32[]{:S(2)}) collective-permute-start(bf16[384,1920]{1,0:T(8,128)(2,1)} %get-tuple-element.299.refs_11_), channel_id=1, source_target_pairs={{0,1},{1,0},{2,3},{3,2},{4,5},{5,4},{6,7},{7,6},{8,9},{9,8},{10,11... | collective-permute-start | bytes 4423688 | tf_op jit(solution)/shard_map/ppermute | solution.py:445
  197.1 16.6 %collective-permute-start.33 = (bf16[96,768]{1,0:T(8,128)(2,1)S(1)}, bf16[96,768]{1,0:T(8,128)(2,1)S(1)}, u32[]{:S(2)}, u32[]{:S(2)}) collective-permute-start(bf16[96,768]{1,0:T(8,128)(2,1)S(1)} %get-tuple-element.295), channel_id=1, source_target_pairs={{0,8},{1,9},{2,10},{3,11},{4,12},{5,13},{6,14},{7,15},{8,0},{9,1},... | collective-permute-start | bytes 442376 | tf_op jit(solution)/shard_map/ppermute | solution.py:445
  197.5 16.2 %collective-permute-start.34 = (bf16[96,768]{1,0:T(8,128)(2,1)S(1)}, bf16[96,768]{1,0:T(8,128)(2,1)S(1)}, u32[]{:S(2)}, u32[]{:S(2)}) collective-permute-start(bf16[96,768]{1,0:T(8,128)(2,1)S(1)} %get-tuple-element.296), channel_id=1, source_target_pairs={{0,16},{1,17},{2,18},{3,19},{4,20},{5,21},{6,22},{7,23},{8,24},{9,... | collective-permute-start | bytes 442376 | tf_op jit(solution)/shard_map/ppermute | solution.py:445
  201.6 12.1 %collective-permute-start.35 = (bf16[96,768]{1,0:T(8,128)(2,1)S(1)}, bf16[96,768]{1,0:T(8,128)(2,1)S(1)}, u32[]{:S(2)}, u32[]{:S(2)}) collective-permute-start(bf16[96,768]{1,0:T(8,128)(2,1)S(1)} %get-tuple-element.297), channel_id=1, source_target_pairs={{0,24},{1,25},{2,26},{3,27},{4,28},{5,29},{6,30},{7,31},{8,16},{9,... | collective-permute-start | bytes 442376 | tf_op jit(solution)/shard_map/ppermute | solution.py:445
  221.0 15.9 %collective-permute-start.38 = (bf16[192,1920]{1,0:T(8,128)(2,1)}, bf16[192,1920]{1,0:T(8,128)(2,1)S(1)}, u32[]{:S(2)}, u32[]{:S(2)}) collective-permute-start(bf16[192,1920]{1,0:T(8,128)(2,1)} %slice.515), channel_id=1, source_target_pairs={{0,4},{1,5},{2,6},{3,7},{4,0},{5,1},{6,2},{7,3},{8,12},{9,13},{10,... | collective-permute-start | bytes 2211848 | tf_op jit(solution)/shard_map/ppermute | solution.py:445
  222.9 16.4 %collective-permute-start.39 = (bf16[192,1920]{1,0:T(8,128)(2,1)}, bf16[192,1920]{1,0:T(8,128)(2,1)}, u32[]{:S(2)}, u32[]{:S(2)}) collective-permute-start(bf16[192,1920]{1,0:T(8,128)(2,1)} %pad_maximum_fusion.8), channel_id=1, source_target_pairs={{0,2},{1,3},{2,0},{3,1},{4,6},{5,7},{6,4},{7,5},{8,10},{9,11},{10,... | collective-permute-start | bytes 2211848 | tf_op jit(solution)/shard_map/ppermute | solution.py:445
  241.0 11.5 %collective-permute-start.40 = (bf16[96,1920]{1,0:T(8,128)(2,1)S(1)}, bf16[96,1920]{1,0:T(8,128)(2,1)S(1)}, u32[]{:S(2)}, u32[]{:S(2)}) collective-permute-start(bf16[96,1920]{1,0:T(8,128)(2,1)S(1)} %slice.519), channel_id=1, source_target_pairs={{0,2},{1,3},{2,0},{3,1},{4,6},{5,7},{6,4},{7,5},{8,10},{9,11},{10,... | collective-permute-start | bytes 1105928 | tf_op jit(solution)/shard_map/ppermute | solution.py:445
  243.0 9.6 %collective-permute-start.41 = (bf16[96,1920]{1,0:T(8,128)(2,1)S(1)}, bf16[96,1920]{1,0:T(8,128)(2,1)S(1)}, u32[]{:S(2)}, u32[]{:S(2)}) collective-permute-start(bf16[96,1920]{1,0:T(8,128)(2,1)S(1)} %slice.518), channel_id=1, source_target_pairs={{0,4},{1,5},{2,6},{3,7},{4,0},{5,1},{6,2},{7,3},{8,12},{9,13},{10,... | collective-permute-start | bytes 1105928 | tf_op jit(solution)/shard_map/ppermute | solution.py:445
  252.0 19.0 %collective-permute-start.42 = (bf16[384,1152]{1,0:T(8,128)(2,1)}, bf16[384,1152]{1,0:T(8,128)(2,1)S(1)}, u32[]{:S(2)}, u32[]{:S(2)}) collective-permute-start(bf16[384,1152]{1,0:T(8,128)(2,1)} %get-tuple-element.319.refs_14_), channel_id=1, source_target_pairs={{0,1},{1,0},{2,3},{3,2},{4,5},{5,4},{6,7},{7,6},{8,9},{9,8},{10,11... | collective-permute-start | bytes 2654216 | tf_op jit(solution)/shard_map/ppermute | solution.py:445
  252.0 20.6 %collective-permute-start.43 = (bf16[384,1152]{1,0:T(8,128)(2,1)}, bf16[384,1152]{1,0:T(8,128)(2,1)}, u32[]{:S(2)}, u32[]{:S(2)}) collective-permute-start(bf16[384,1152]{1,0:T(8,128)(2,1)} %get-tuple-element.320.refs_16_), channel_id=1, source_target_pairs={{0,1},{1,0},{2,3},{3,2},{4,5},{5,4},{6,7},{7,6},{8,9},{9,8},{10,11... | collective-permute-start | bytes 2654216 | tf_op jit(solution)/shard_map/ppermute | solution.py:445
  253.5 13.2 %collective-permute-start.44 = (bf16[24,3840]{1,0:T(8,128)(2,1)S(1)}, bf16[24,3840]{1,0:T(8,128)(2,1)S(1)}, u32[]{:S(2)}, u32[]{:S(2)}) collective-permute-start(bf16[24,3840]{1,0:T(8,128)(2,1)S(1)} %get-tuple-element.323), channel_id=1, source_target_pairs={{0,8},{1,9},{2,10},{3,11},{4,12},{5,13},{6,14},{7,15},{8,0},{9,1},... | collective-permute-start | bytes 552968 | tf_op jit(solution)/shard_map/ppermute | solution.py:445
  254.5 16.3 %collective-permute-start.45 = (bf16[24,3840]{1,0:T(8,128)(2,1)S(1)}, bf16[24,3840]{1,0:T(8,128)(2,1)S(1)}, u32[]{:S(2)}, u32[]{:S(2)}) collective-permute-start(bf16[24,3840]{1,0:T(8,128)(2,1)S(1)} %get-tuple-element.324), channel_id=1, source_target_pairs={{0,16},{1,17},{2,18},{3,19},{4,20},{5,21},{6,22},{7,23},{8,24},{9,... | collective-permute-start | bytes 552968 | tf_op jit(solution)/shard_map/ppermute | solution.py:445
  257.2 13.6 %collective-permute-start.46 = (bf16[24,3840]{1,0:T(8,128)(2,1)S(1)}, bf16[24,3840]{1,0:T(8,128)(2,1)S(1)}, u32[]{:S(2)}, u32[]{:S(2)}) collective-permute-start(bf16[24,3840]{1,0:T(8,128)(2,1)S(1)} %get-tuple-element.325), channel_id=1, source_target_pairs={{0,24},{1,25},{2,26},{3,27},{4,28},{5,29},{6,30},{7,31},{8,16},{9,... | collective-permute-start | bytes 552968 | tf_op jit(solution)/shard_map/ppermute | solution.py:445
  276.0 17.1 %collective-permute-start.47 = (bf16[192,1152]{1,0:T(8,128)(2,1)}, bf16[192,1152]{1,0:T(8,128)(2,1)}, u32[]{:S(2)}, u32[]{:S(2)}) collective-permute-start(bf16[192,1152]{1,0:T(8,128)(2,1)} %slice.517), channel_id=1, source_target_pairs={{0,4},{1,5},{2,6},{3,7},{4,0},{5,1},{6,2},{7,3},{8,12},{9,13},{10,... | collective-permute-start | bytes 1327112 | tf_op jit(solution)/shard_map/ppermute | solution.py:445
  277.1 16.0 %collective-permute-start.48 = (bf16[192,1152]{1,0:T(8,128)(2,1)}, bf16[192,1152]{1,0:T(8,128)(2,1)}, u32[]{:S(2)}, u32[]{:S(2)}) collective-permute-start(bf16[192,1152]{1,0:T(8,128)(2,1)} %pad_maximum_fusion.12), channel_id=1, source_target_pairs={{0,2},{1,3},{2,0},{3,1},{4,6},{5,7},{6,4},{7,5},{8,10},{9,11},{10,... | collective-permute-start | bytes 1327112 | tf_op jit(solution)/shard_map/ppermute | solution.py:445
  293.9 1.7 collective-permute-start.54
  296.3 3.7 %collective-permute-start.55 = (f32[8,240]{1,0:T(8,128)S(1)}, f32[8,240]{1,0:T(8,128)S(1)}, u32[]{:S(2)}, u32[]{:S(2)}) collective-permute-start(f32[8,240]{1,0:T(8,128)S(1)} %slice.430), channel_id=1, source_target_pairs={{0,4},{1,5},{2,6},{3,7},{4,0},{5,1},{6,2},{7,3},{8,12},{9,13},{10,... | collective-permute-start | bytes 23048 | tf_op jit(solution)/shard_map/ppermute | solution.py:445
  300.0 3.6 %collective-permute-start.56 = (f32[4,240]{1,0:T(4,128)S(1)}, f32[4,240]{1,0:T(4,128)S(1)}, u32[]{:S(2)}, u32[]{:S(2)}) collective-permute-start(f32[4,240]{1,0:T(4,128)S(1)} %slice.432), channel_id=1, source_target_pairs={{0,2},{1,3},{2,0},{3,1},{4,6},{5,7},{6,4},{7,5},{8,10},{9,11},{10,... | collective-permute-start | bytes 11528 | tf_op jit(solution)/shard_map/ppermute | solution.py:445
  303.6 7.7 %collective-permute-start.59 = (f32[1,240]{1,0:T(1,128)S(1)}, f32[1,240]{1,0:T(1,128)S(1)}, u32[]{:S(2)}, u32[]{:S(2)}) collective-permute-start(f32[1,240]{1,0:T(1,128)S(1)} %get-tuple-element.427), channel_id=1, source_target_pairs={{0,24},{1,25},{2,26},{3,27},{4,28},{5,29},{6,30},{7,31},{8,16},{9,... | collective-permute-start | bytes 2888 | tf_op jit(solution)/shard_map/ppermute | solution.py:445
  306.1 5.2 %collective-permute-start.58 = (f32[1,240]{1,0:T(1,128)S(1)}, f32[1,240]{1,0:T(1,128)S(1)}, u32[]{:S(2)}, u32[]{:S(2)}) collective-permute-start(f32[1,240]{1,0:T(1,128)S(1)} %get-tuple-element.428), channel_id=1, source_target_pairs={{0,16},{1,17},{2,18},{3,19},{4,20},{5,21},{6,22},{7,23},{8,24},{9,... | collective-permute-start | bytes 2888 | tf_op jit(solution)/shard_map/ppermute | solution.py:445
  308.4 3.6 %collective-permute-start.57 = (f32[1,240]{1,0:T(1,128)S(1)}, f32[1,240]{1,0:T(1,128)S(1)}, u32[]{:S(2)}, u32[]{:S(2)}) collective-permute-start(f32[1,240]{1,0:T(1,128)S(1)} %get-tuple-element.426), channel_id=1, source_target_pairs={{0,8},{1,9},{2,10},{3,11},{4,12},{5,13},{6,14},{7,15},{8,0},{9,1},... | collective-permute-start | bytes 2888 | tf_op jit(solution)/shard_map/ppermute | solution.py:445
  309.7 6.0 %collective-permute-start.49 = (bf16[96,1152]{1,0:T(8,128)(2,1)S(1)}, bf16[96,1152]{1,0:T(8,128)(2,1)S(1)}, u32[]{:S(2)}, u32[]{:S(2)}) collective-permute-start(bf16[96,1152]{1,0:T(8,128)(2,1)S(1)} %slice.523), channel_id=1, source_target_pairs={{0,2},{1,3},{2,0},{3,1},{4,6},{5,7},{6,4},{7,5},{8,10},{9,11},{10,... | collective-permute-start | bytes 663560 | tf_op jit(solution)/shard_map/ppermute | solution.py:445
  310.3 5.9 %collective-permute-start.50 = (bf16[96,1152]{1,0:T(8,128)(2,1)S(1)}, bf16[96,1152]{1,0:T(8,128)(2,1)S(1)}, u32[]{:S(2)}, u32[]{:S(2)}) collective-permute-start(bf16[96,1152]{1,0:T(8,128)(2,1)S(1)} %slice.522), channel_id=1, source_target_pairs={{0,4},{1,5},{2,6},{3,7},{4,0},{5,1},{6,2},{7,3},{8,12},{9,13},{10,... | collective-permute-start | bytes 663560 | tf_op jit(solution)/shard_map/ppermute | solution.py:445
  316.5 5.9 %collective-permute-start.51 = (bf16[24,2304]{1,0:T(8,128)(2,1)S(1)}, bf16[24,2304]{1,0:T(8,128)(2,1)S(1)}, u32[]{:S(2)}, u32[]{:S(2)}) collective-permute-start(bf16[24,2304]{1,0:T(8,128)(2,1)S(1)} %get-tuple-element.337), channel_id=1, source_target_pairs={{0,8},{1,9},{2,10},{3,11},{4,12},{5,13},{6,14},{7,15},{8,0},{9,1},... | collective-permute-start | bytes 331784 | tf_op jit(solution)/shard_map/ppermute | solution.py:445
  318.5 8.0 %collective-permute-start.52 = (bf16[24,2304]{1,0:T(8,128)(2,1)S(1)}, bf16[24,2304]{1,0:T(8,128)(2,1)S(1)}, u32[]{:S(2)}, u32[]{:S(2)}) collective-permute-start(bf16[24,2304]{1,0:T(8,128)(2,1)S(1)} %get-tuple-element.338), channel_id=1, source_target_pairs={{0,16},{1,17},{2,18},{3,19},{4,20},{5,21},{6,22},{7,23},{8,24},{9,... | collective-permute-start | bytes 331784 | tf_op jit(solution)/shard_map/ppermute | solution.py:445
  319.6 7.0 %collective-permute-start.53 = (bf16[24,2304]{1,0:T(8,128)(2,1)S(1)}, bf16[24,2304]{1,0:T(8,128)(2,1)S(1)}, u32[]{:S(2)}, u32[]{:S(2)}) collective-permute-start(bf16[24,2304]{1,0:T(8,128)(2,1)S(1)} %get-tuple-element.339), channel_id=1, source_target_pairs={{0,24},{1,25},{2,26},{3,27},{4,28},{5,29},{6,30},{7,31},{8,16},{9,... | collective-permute-start | bytes 331784 | tf_op jit(solution)/shard_map/ppermute | solution.py:445
  (57 other events, 240.5 us)

commit v2 on v1

--- a/solution.py
+++ b/solution.py
@@ -28,7 +28,7 @@
 AXES = ("dp", "fsdp")
 LOW = jnp.bfloat16
 WIDE = jnp.float32
-VMEM_BYTES = 56 * 2**20
+VMEM_BYTES = 12 * 2**20
 
 
 def nn(left, right):

time: 332 us -> 282 us (0.85)
  Pallas kernels: 152 us -> 105 us
  waiting for transfers between devices: 45.5 us -> 55.2 us
  other arithmetic: 30.7 us -> 21.3 us
  local copies, waits for them, and re-layouts: 25.6 us -> 21.5 us
    pallas_call x9, Pallas kernels: 108 us -> 68.9 us  [whole_call(): pl.pallas_call(later(kernel, len(args), len(after)), in_specs=specs + [pl...]
    ppermute x60, waiting for transfers between devices: 45.5 us -> 55.2 us  [swap(): return lax.ppermute(value, AXES, pairs)]
    pallas_call x2, Pallas kernels: 20.2 us -> 15.5 us  [attend(): pl.pallas_call(later(functools.partial(attend_kernel, base), 6, len(after...]
    pallas_call x2, Pallas kernels: 24.3 us -> 20.6 us  [attend_back(): pl.pallas_call(later(attend_back_kernel, 6, len(after)), grid_spec=pltpu....]
    unnamed x136 -> x76, local copies, waits for them, and re-layouts: 11.4 us -> 9.06 us
  transfers between devices with their start and end apart: 60 -> 60, of which waited for: 16 -> 24; matrix products, arithmetic and copies ran while one was open for 8% -> 8% of each run, Pallas kernels for 46% -> 38%
where the time goes in v2:
time: 282 us; the launch traced here: 279 us
  Pallas kernels  105 us (37%)
  starting transfers between devices  64.4 us (23%)
  waiting for transfers between devices  55.2 us (20%)
  local copies, waits for them, and re-layouts  21.5 us (8%)
  other arithmetic  21.3 us (8%)
  between operations  9.84 us (3%)
    pallas_call x9, Pallas kernels, whole_call(): pl.pallas_call(later(kernel, len(args), len(after)), in_specs=specs + [pl...  68.9 us
    ppermute x60, starting transfers between devices, swap(): return lax.ppermute(value, AXES, pairs)  64.4 us
    ppermute x60, waiting for transfers between devices, swap(): return lax.ppermute(value, AXES, pairs)  55.2 us
    pallas_call x2, Pallas kernels, attend_back(): pl.pallas_call(later(attend_back_kernel, 6, len(after)), grid_spec=pltpu....  20.6 us
    pallas_call x2, Pallas kernels, attend(): pl.pallas_call(later(functools.partial(attend_kernel, base), 6, len(after...  15.5 us
    unnamed x76, local copies, waits for them, and re-layouts  9.06 us
  transfers between devices with their start and end apart: 60, of which 24 were waited for; matrix products, arithmetic and copies ran while one was open for 8% of the time, Pallas kernels for 38%

profile of v2, /device:TPU:0, one launch (start us, length us, event | category | flops | bytes accessed | tf_op | source)
XLA Modules:
  0.0 278.6 jit_solution(1617864660524152210)
XLA Ops:
  2.5 3.1 %collective-permute-start = (bf16[24,2432]{1,0:T(8,128)(2,1)S(1)}, bf16[24,2432]{1,0:T(8,128)(2,1)S(1)}, u32[]{:S(2)}, u32[]{:S(2)}) collective-permute-start(bf16[24,2432]{1,0:T(8,128)(2,1)S(1)} %fusion.23), channel_id=1, source_target_pairs={{0,8},{1,9},{2,10},{3,11},{4,12},{5,13},{6,14},{7,15},{8,0},{9,1},... | collective-permute-start | bytes 350216 | tf_op jit(solution)/shard_map/ppermute | solution.py:445
  5.6 2.6 collective-permute-start.1
  15.1 1.1 and_select_fusion
  21.4 1.8 collective-permute-start.4
  23.9 1.5 collective-permute-start.3
  25.4 4.6 %collective-permute-done.3 = bf16[96,1152]{1,0:T(8,128)(2,1)S(1)} collective-permute-done((bf16[96,1152]{1,0:T(8,128)(2,1)S(1)}, bf16[96,1152]{1,0:T(8,128)(2,1)S(1)}, u32[]{:S(2)}, u32[]{:S(2)}) %collective-permute-start.3) | collective-permute-done | bytes 221216 | tf_op jit(solution)/shard_map/ppermute | solution.py:445
  30.8 3.5 %collective-permute-start.10 = (bf16[24,3840]{1,0:T(8,128)(2,1)S(1)}, bf16[24,3840]{1,0:T(8,128)(2,1)S(1)}, u32[]{:S(2)}, u32[]{:S(2)}) collective-permute-start(bf16[24,3840]{1,0:T(8,128)(2,1)S(1)} %pad_maximum_fusion.15), channel_id=1, source_target_pairs={{0,16},{1,17},{2,18},{3,19},{4,20},{5,21},{6,22},{7,23},{8,24},{9,... | collective-permute-start | bytes 552968 | tf_op jit(solution)/shard_map/ppermute | solution.py:445
  34.6 2.1 sqrt_select_fusion.refs_5_
  37.4 1.5 collective-permute-start.6
  38.9 7.6 %collective-permute-done.10 = bf16[24,3840]{1,0:T(8,128)(2,1)S(1)} collective-permute-done((bf16[24,3840]{1,0:T(8,128)(2,1)S(1)}, bf16[24,3840]{1,0:T(8,128)(2,1)S(1)}, u32[]{:S(2)}, u32[]{:S(2)}) %collective-permute-start.10) | collective-permute-done | bytes 184352 | tf_op jit(solution)/shard_map/ppermute | solution.py:445
  49.2 2.4 collective-permute-done.7.refs_4_.refs_8_
  53.6 1.5 collective-permute-start.12
  56.2 1.3 fusion.1
  57.5 1.3 reshape.167
  58.8 1.2 copy-done.1
  60.0 1.2 copy-done.5
  61.2 1.2 copy-done.8
  62.3 5.4 %project.1 = (bf16[576,768]{1,0:T(8,128)(2,1)S(1)}, bf16[576,2304]{1,0:T(8,128)(2,1)S(1)}) custom-call(bf16[576,768]{1,0:T(8,128)(2,1)S(1)} %bitcast.26, f32[16,768]{1,0:T(8,128)S(1)} %pad.10.refs_1_.refs_3_.refs_0_, bf16[768,768]{1,0:T(8,128)(2,1)S(1)} %fusion.refs_2_.refs_4_.refs_1_.refs_0_, bf16[384,1152]{1,0:T(8,128)(2,1)S(1)} %pad_maximum_fusion.7.refs_3_.refs_7_, ...), custom_call_target="tpu_custom_call" | custom-call | flops 2717908992 | bytes 9388032 | tf_op jit(solution)/shard_map/project/pallas_call | solution.py:60
  67.8 1.1 constant_dynamic-update-slice_fusion.13
  71.0 1.6 collective-permute-start.14
  72.6 2.5 collective-permute-start.15
  77.0 7.8 %attend.2 = (bf16[576,384]{1,0:T(8,128)(2,1)S(1)}, bf16[6,4,256,256]{3,2,1,0:T(8,128)(2,1)S(1)}) custom-call(s32[4,3]{1,0:T(4,128)S(1)} %pad_add_fusion.1.refs_0_, f32[12]{0:T(128)S(1)} %multiply_exponential_fusion.refs_1_, bf16[576,2304]{1,0:T(8,128)(2,1)S(1)} %get-tuple-element.210.refs_2_.refs_3_.refs_4_.refs_1_, ...), custom_call_target="tpu_custom_call" | custom-call | flops 8999999488 | bytes 6000000 | tf_op jit(solution)/shard_map/attend/pallas_call | solution.py:142
  84.8 1.7 copy-done.12
  86.5 6.0 %collective-permute-done.17 = bf16[192,1920]{1,0:T(8,128)(2,1)S(1)} collective-permute-done((bf16[192,1920]{1,0:T(8,128)(2,1)S(1)}, bf16[192,1920]{1,0:T(8,128)(2,1)S(1)}, u32[]{:S(2)}, u32[]{:S(2)}) %collective-permute-start.17) | collective-permute-done | bytes 737312 | tf_op jit(solution)/shard_map/ppermute | solution.py:445
  96.0 7.7 %attend.3 = (bf16[576,384]{1,0:T(8,128)(2,1)S(1)}, bf16[6,4,256,256]{3,2,1,0:T(8,128)(2,1)S(1)}) custom-call(s32[4,3]{1,0:T(4,128)S(1)} %pad_add_fusion.1.refs_0_, f32[12]{0:T(128)S(1)} %multiply_exponential_fusion.refs_1_, bf16[576,2304]{1,0:T(8,128)(2,1)S(1)} %get-tuple-element.210.refs_2_.refs_3_.refs_4_.refs_1_, ...), custom_call_target="tpu_custom_call" | custom-call | flops 8999999488 | bytes 6000000 | tf_op jit(solution)/shard_map/attend/pallas_call | solution.py:142
  103.9 1.1 collective-permute-start.23
  105.1 1.4 collective-permute-start.24
  106.4 12.4 %upward.1 = (bf16[576,768]{1,0:T(8,128)(2,1)S(1)}, f32[576,768]{1,0:T(8,128)S(1)}, bf16[576,768]{1,0:T(8,128)(2,1)S(1)}, bf16[576,3072]{1,0:T(8,128)(2,1)S(1)}, bf16[576,3072]{1,0:T(8,128)(2,1)S(1)}) custom-call(bf16[576,768]{1,0:T(8,128)(2,1)S(1)} %bitcast.27, bf16[576,384]{1,0:T(8,128)(2,1)S(1)} %get-tuple-element.211.refs_9_.refs_1_, ...), custom_call_target="tpu_custom_call" | custom-call | flops 9512681472 | bytes 19513344 | tf_op jit(solution)/shard_map/upward/pallas_call | solution.py:60
  120.9 8.0 %down_grad.1 = (bf16[1536,384]{1,0:T(8,128)(2,1)S(1)}, bf16[1536,384]{1,0:T(8,128)(2,1)S(1)}, bf16[1536,384]{1,0:T(8,128)(2,1)S(1)}, bf16[1536,384]{1,0:T(8,128)(2,1)S(1)}) custom-call(s32[32]{0:T(128)S(1)} %get-tuple-element.371.refs_0_, bf16[576,3072]{1,0:T(8,128)(2,1)S(1)} %get-tuple-element.247.refs_2_.refs_1_, bf16[576,768]{1,0:T(8,128)(2,1)S(1)} %bitcast.23, ...), custom_call_target="tpu_custom_call" | custom-call | flops 2717908992 | bytes 9142400 | tf_op jit(solution)/shard_map/down_grad/pallas_call | solution.py:60
  129.6 10.4 %downward.1 = (bf16[576,768]{1,0:T(8,128)(2,1)}, bf16[576,3072]{1,0:T(8,128)(2,1)S(1)}, f32[8,768]{1,0:T(8,128)S(1)}) custom-call(s32[32]{0:T(128)S(1)} %get-tuple-element.371.refs_0_, f32[16,768]{1,0:T(8,128)S(1)} %pad.10.refs_1_.refs_3_.refs_0_, bf16[576,3072]{1,0:T(8,128)(2,1)S(1)} %get-tuple-element.247.refs_2_.refs_1_, ...), custom_call_target="tpu_custom_call" | custom-call | flops 5435817984 | bytes 18948224 | tf_op jit(solution)/shard_map/downward/pallas_call | solution.py:60
  140.8 1.1 collective-permute-start.29
  141.9 1.5 collective-permute-start.30
  143.4 12.5 %hidden_grad.1 = (f32[576,768]{1,0:T(8,128)S(1)}, bf16[576,768]{1,0:T(8,128)(2,1)S(1)}, bf16[576,768]{1,0:T(8,128)(2,1)S(1)}, f32[8,768]{1,0:T(8,128)S(1)}) custom-call(f32[16,768]{1,0:T(8,128)S(1)} %pad.10.refs_1_.refs_3_.refs_0_, bf16[768,768]{1,0:T(8,128)(2,1)S(1)} %fusion.refs_2_.refs_4_.refs_1_.refs_0_, ...), custom_call_target="tpu_custom_call" | custom-call | flops 4756340736 | bytes 16883712 | tf_op jit(solution)/shard_map/hidden_grad/pallas_call | solution.py:60
  157.3 1.6 collective-permute-start.31
  159.8 5.8 %two_grad.1 = (bf16[384,1920]{1,0:T(8,128)(2,1)S(1)}, bf16[384,1920]{1,0:T(8,128)(2,1)S(1)}, bf16[384,1920]{1,0:T(8,128)(2,1)S(1)}, bf16[384,1920]{1,0:T(8,128)(2,1)S(1)}) custom-call(bf16[576,768]{1,0:T(8,128)(2,1)S(1)} %get-tuple-element.256.refs_0_, bf16[576,768]{1,0:T(8,128)(2,1)S(1)} %get-tuple-element.286.refs_1_, ...), custom_call_target="tpu_custom_call" | custom-call | flops 3397386240 | bytes 12091392 | tf_op jit(solution)/shard_map/two_grad/pallas_call | solution.py:60
  167.4 3.4 %collective-permute-start.34 = (bf16[96,768]{1,0:T(8,128)(2,1)S(1)}, bf16[96,768]{1,0:T(8,128)(2,1)S(1)}, u32[]{:S(2)}, u32[]{:S(2)}) collective-permute-start(bf16[96,768]{1,0:T(8,128)(2,1)S(1)} %get-tuple-element.296), channel_id=1, source_target_pairs={{0,16},{1,17},{2,18},{3,19},{4,20},{5,21},{6,22},{7,23},{8,24},{9,... | collective-permute-start | bytes 442376 | tf_op jit(solution)/shard_map/ppermute | solution.py:445
  171.1 10.2 %attend_back.2 = (bf16[576,384]{1,0:T(8,128)(2,1)S(1)}, bf16[576,384]{1,0:T(8,128)(2,1)S(1)}, bf16[576,384]{1,0:T(8,128)(2,1)S(1)}) custom-call(s32[4,3]{1,0:T(4,128)S(1)} %pad_add_fusion.1.refs_0_, bf16[576,2304]{1,0:T(8,128)(2,1)S(1)} %get-tuple-element.210.refs_2_.refs_3_.refs_4_.refs_1_, ...), custom_call_target="tpu_custom_call" | custom-call | flops 12000000000 | bytes 6000000 | tf_op jit(solution)/shard_map/attend_back/pallas_call | solution.py:189
  184.3 10.4 %attend_back.3 = (bf16[576,384]{1,0:T(8,128)(2,1)S(1)}, bf16[576,384]{1,0:T(8,128)(2,1)S(1)}, bf16[576,384]{1,0:T(8,128)(2,1)S(1)}) custom-call(s32[4,3]{1,0:T(4,128)S(1)} %pad_add_fusion.1.refs_0_, bf16[576,2304]{1,0:T(8,128)(2,1)S(1)} %get-tuple-element.210.refs_2_.refs_3_.refs_4_.refs_1_, ...), custom_call_target="tpu_custom_call" | custom-call | flops 12000000000 | bytes 6000000 | tf_op jit(solution)/shard_map/attend_back/pallas_call | solution.py:189
  194.9 5.1 %collective-permute-done.38.refs_7_ = bf16[192,1920]{1,0:T(8,128)(2,1)S(1)} collective-permute-done((bf16[192,1920]{1,0:T(8,128)(2,1)S(1)}, bf16[192,1920]{1,0:T(8,128)(2,1)S(1)}, u32[]{:S(2)}, u32[]{:S(2)}) %collective-permute-start.38) | collective-permute-done | bytes 737312 | tf_op jit(solution)/shard_map/ppermute | solution.py:445
  202.8 1.1 multiply_subtract_fusion
  203.9 3.6 %one_grad.1 = (bf16[384,1152]{1,0:T(8,128)(2,1)S(1)}, bf16[384,1152]{1,0:T(8,128)(2,1)S(1)}, bf16[384,1152]{1,0:T(8,128)(2,1)S(1)}, bf16[384,1152]{1,0:T(8,128)(2,1)S(1)}) custom-call(bf16[576,768]{1,0:T(8,128)(2,1)S(1)} %get-tuple-element.313.refs_0_, bf16[576,384]{1,0:T(8,128)(2,1)S(1)} %get-tuple-element.291.refs_11_.refs_1_, ...), custom_call_target="tpu_custom_call" | custom-call | flops 2038431744 | bytes 7077888 | tf_op jit(solution)/shard_map/one_grad/pallas_call | solution.py:60
  208.0 1.3 collective-permute-done.40.refs_11_
  209.8 3.6 %collective-permute-start.44 = (bf16[24,3840]{1,0:T(8,128)(2,1)S(1)}, bf16[24,3840]{1,0:T(8,128)(2,1)S(1)}, u32[]{:S(2)}, u32[]{:S(2)}) collective-permute-start(bf16[24,3840]{1,0:T(8,128)(2,1)S(1)} %get-tuple-element.323), channel_id=1, source_target_pairs={{0,8},{1,9},{2,10},{3,11},{4,12},{5,13},{6,14},{7,15},{8,0},{9,1},... | collective-permute-start | bytes 552968 | tf_op jit(solution)/shard_map/ppermute | solution.py:445
  213.5 1.1 collective-permute-start.45
  214.5 1.4 collective-permute-start.46
  215.9 4.4 %input_back.1.refs_2_ = f32[576,768]{1,0:T(8,128)S(1)} custom-call(bf16[768,768]{1,0:T(8,128)(2,1)S(1)} %fusion.refs_2_.refs_4_.refs_1_.refs_0_, bf16[576,384]{1,0:T(8,128)(2,1)S(1)} %get-tuple-element.291.refs_11_.refs_1_, bf16[576,384]{1,0:T(8,128)(2,1)S(1)} %get-tuple-element.300.refs_2_, bf16[576,384]{1,0:T(8,128)(2,1)S(1)} %get-tuple-element.301.refs_3_, ...), custom_call_target="tpu_custom_call" | custom-call | flops 2717908992 | bytes 9338880 | tf_op jit(solution)/shard_map/input_back/pallas_call | solution.py:60
  220.4 8.3 %collective-permute-done.45.refs_7_ = bf16[24,3840]{1,0:T(8,128)(2,1)S(1)} collective-permute-done((bf16[24,3840]{1,0:T(8,128)(2,1)S(1)}, bf16[24,3840]{1,0:T(8,128)(2,1)S(1)}, u32[]{:S(2)}, u32[]{:S(2)}) %collective-permute-start.45) | collective-permute-done | bytes 184352 | tf_op jit(solution)/shard_map/ppermute | solution.py:445
  230.8 1.1 collective-permute-start.47
  231.9 1.6 collective-permute-start.48
  233.6 1.0 multiply_subtract_fusion.1
  234.6 6.2 %input_grad.1 = (f32[576,768]{1,0:T(8,128)}, f32[8,768]{1,0:T(8,128)S(1)}) custom-call(bf16[576,768]{1,0:T(8,128)(2,1)S(1)} %bitcast.28, f32[16,768]{1,0:T(8,128)S(1)} %pad.10.refs_1_.refs_3_.refs_0_, f32[576,768]{1,0:T(8,128)S(1)} %input_back.1.refs_2_, f32[576,768]{1,0:T(8,128)S(1)} %get-tuple-element.318.refs_3_, ...), custom_call_target="tpu_custom_call" | custom-call | flops 2038431744 | bytes 6266880 | tf_op jit(solution)/shard_map/input_grad/pallas_call | solution.py:60
  241.5 1.5 reshape.168
  243.0 2.0 gather_fusion
  245.7 1.7 multiply_subtract_fusion.3
  248.5 3.3 %collective-permute-done.55 = f32[8,240]{1,0:T(8,128)S(1)} collective-permute-done((f32[8,240]{1,0:T(8,128)S(1)}, f32[8,240]{1,0:T(8,128)S(1)}, u32[]{:S(2)}, u32[]{:S(2)}) %collective-permute-start.55) | collective-permute-done | bytes 7712 | tf_op jit(solution)/shard_map/ppermute | solution.py:445
  252.2 1.1 slice_add_fusion.2
  253.3 2.1 collective-permute-done.56
  255.4 2.0 collective-permute-start.59
  257.4 2.1 collective-permute-start.58
  259.8 1.1 maximum_add_fusion.2
  263.0 4.0 %collective-permute-done.49 = bf16[96,1152]{1,0:T(8,128)(2,1)S(1)} collective-permute-done((bf16[96,1152]{1,0:T(8,128)(2,1)S(1)}, bf16[96,1152]{1,0:T(8,128)(2,1)S(1)}, u32[]{:S(2)}, u32[]{:S(2)}) %collective-permute-start.49) | collective-permute-done | bytes 221216 | tf_op jit(solution)/shard_map/ppermute | solution.py:445
  267.7 1.7 collective-permute-start.51
  270.4 1.7 collective-permute-start.53
  273.3 4.1 %collective-permute-done.52 = bf16[24,2304]{1,0:T(8,128)(2,1)S(1)} collective-permute-done((bf16[24,2304]{1,0:T(8,128)(2,1)S(1)}, bf16[24,2304]{1,0:T(8,128)(2,1)S(1)}, u32[]{:S(2)}, u32[]{:S(2)}) %collective-permute-start.52) | collective-permute-done | bytes 110624 | tf_op jit(solution)/shard_map/ppermute | solution.py:445
  (274 shorter events, 47.6 us)
Async XLA Ops:
  0.7 20.3 %copy-start.17 = (f32[24,3072]{1,0:T(8,128)S(1)}, f32[24,3072]{1,0:T(8,128)}, u32[]{:S(2)}) copy-start(f32[24,3072]{1,0:T(8,128)} %param.29) | copy-start | bytes 884740
  0.7 20.4 %copy-start.23 = (f32[24,768]{1,0:T(8,128)S(1)}, f32[24,768]{1,0:T(8,128)}, u32[]{:S(2)}) copy-start(f32[24,768]{1,0:T(8,128)} %param.28) | copy-start | bytes 221188
  2.5 18.8 %collective-permute-start = (bf16[24,2432]{1,0:T(8,128)(2,1)S(1)}, bf16[24,2432]{1,0:T(8,128)(2,1)S(1)}, u32[]{:S(2)}, u32[]{:S(2)}) collective-permute-start(bf16[24,2432]{1,0:T(8,128)(2,1)S(1)} %fusion.23), channel_id=1, source_target_pairs={{0,8},{1,9},{2,10},{3,11},{4,12},{5,13},{6,14},{7,15},{8,0},{9,1},... | collective-permute-start | bytes 350216 | tf_op jit(solution)/shard_map/ppermute | solution.py:445
  5.6 15.7 %collective-permute-start.1 = (bf16[24,2432]{1,0:T(8,128)(2,1)S(1)}, bf16[24,2432]{1,0:T(8,128)(2,1)S(1)}, u32[]{:S(2)}, u32[]{:S(2)}) collective-permute-start(bf16[24,2432]{1,0:T(8,128)(2,1)S(1)} %fusion.23), channel_id=1, source_target_pairs={{0,16},{1,17},{2,18},{3,19},{4,20},{5,21},{6,22},{7,23},{8,24},{9,... | collective-permute-start | bytes 350216 | tf_op jit(solution)/shard_map/ppermute | solution.py:445
  8.2 13.1 %collective-permute-start.2 = (bf16[24,2432]{1,0:T(8,128)(2,1)S(1)}, bf16[24,2432]{1,0:T(8,128)(2,1)S(1)}, u32[]{:S(2)}, u32[]{:S(2)}) collective-permute-start(bf16[24,2432]{1,0:T(8,128)(2,1)S(1)} %fusion.23), channel_id=1, source_target_pairs={{0,24},{1,25},{2,26},{3,27},{4,28},{5,29},{6,30},{7,31},{8,16},{9,... | collective-permute-start | bytes 350216 | tf_op jit(solution)/shard_map/ppermute | solution.py:445
  21.4 8.6 %collective-permute-start.4 = (bf16[96,1280]{1,0:T(8,128)(2,1)S(1)}, bf16[96,1280]{1,0:T(8,128)(2,1)S(1)}, u32[]{:S(2)}, u32[]{:S(2)}) collective-permute-start(bf16[96,1280]{1,0:T(8,128)(2,1)S(1)} %slice.372), channel_id=1, source_target_pairs={{0,4},{1,5},{2,6},{3,7},{4,0},{5,1},{6,2},{7,3},{8,12},{9,13},{10,... | collective-permute-start | bytes 737288 | tf_op jit(solution)/shard_map/ppermute | solution.py:445
  23.9 6.1 %collective-permute-start.3 = (bf16[96,1152]{1,0:T(8,128)(2,1)S(1)}, bf16[96,1152]{1,0:T(8,128)(2,1)S(1)}, u32[]{:S(2)}, u32[]{:S(2)}) collective-permute-start(bf16[96,1152]{1,0:T(8,128)(2,1)S(1)} %slice.371), channel_id=1, source_target_pairs={{0,2},{1,3},{2,0},{3,1},{4,6},{5,7},{6,4},{7,5},{8,10},{9,11},{10,... | collective-permute-start | bytes 663560 | tf_op jit(solution)/shard_map/ppermute | solution.py:445
  30.1 8.8 %collective-permute-start.9 = (bf16[24,3840]{1,0:T(8,128)(2,1)S(1)}, bf16[24,3840]{1,0:T(8,128)(2,1)S(1)}, u32[]{:S(2)}, u32[]{:S(2)}) collective-permute-start(bf16[24,3840]{1,0:T(8,128)(2,1)S(1)} %pad_maximum_fusion.15), channel_id=1, source_target_pairs={{0,8},{1,9},{2,10},{3,11},{4,12},{5,13},{6,14},{7,15},{8,0},{9,1},... | collective-permute-start | bytes 552968 | tf_op jit(solution)/shard_map/ppermute | solution.py:445
  30.8 15.7 %collective-permute-start.10 = (bf16[24,3840]{1,0:T(8,128)(2,1)S(1)}, bf16[24,3840]{1,0:T(8,128)(2,1)S(1)}, u32[]{:S(2)}, u32[]{:S(2)}) collective-permute-start(bf16[24,3840]{1,0:T(8,128)(2,1)S(1)} %pad_maximum_fusion.15), channel_id=1, source_target_pairs={{0,16},{1,17},{2,18},{3,19},{4,20},{5,21},{6,22},{7,23},{8,24},{9,... | collective-permute-start | bytes 552968 | tf_op jit(solution)/shard_map/ppermute | solution.py:445
  34.3 12.2 %collective-permute-start.11 = (bf16[24,3840]{1,0:T(8,128)(2,1)S(1)}, bf16[24,3840]{1,0:T(8,128)(2,1)S(1)}, u32[]{:S(2)}, u32[]{:S(2)}) collective-permute-start(bf16[24,3840]{1,0:T(8,128)(2,1)S(1)} %pad_maximum_fusion.15), channel_id=1, source_target_pairs={{0,24},{1,25},{2,26},{3,27},{4,28},{5,29},{6,30},{7,31},{8,16},{9,... | collective-permute-start | bytes 552968 | tf_op jit(solution)/shard_map/ppermute | solution.py:445
  36.6 9.9 %collective-permute-start.5 = (bf16[192,1152]{1,0:T(8,128)(2,1)S(1)}, bf16[192,1152]{1,0:T(8,128)(2,1)S(1)}, u32[]{:S(2)}, u32[]{:S(2)}) collective-permute-start(bf16[192,1152]{1,0:T(8,128)(2,1)S(1)} %constant_dynamic-update-slice_fusion.4), channel_id=1, source_target_pairs={{0,4},{1,5},{2,6},{3,7},{4,0},{5,1},{6,2},{7,3},{8,12},{9,13},{10,... | collective-permute-start | bytes 1327112 | tf_op jit(solution)/shard_map/ppermute | solution.py:445
  37.4 10.1 %collective-permute-start.6 = (bf16[192,1280]{1,0:T(8,128)(2,1)S(1)}, bf16[192,1280]{1,0:T(8,128)(2,1)S(1)}, u32[]{:S(2)}, u32[]{:S(2)}) collective-permute-start(bf16[192,1280]{1,0:T(8,128)(2,1)S(1)} %constant_dynamic-update-slice_fusion.6), channel_id=1, source_target_pairs={{0,2},{1,3},{2,0},{3,1},{4,6},{5,7},{6,4},{7,5},{8,10},{9,11},{10,... | collective-permute-start | bytes 1474568 | tf_op jit(solution)/shard_map/ppermute | solution.py:445
  47.8 4.8 %collective-permute-start.8 = (bf16[384,1280]{1,0:T(8,128)(2,1)S(1)}, bf16[384,1280]{1,0:T(8,128)(2,1)S(1)}, u32[]{:S(2)}, u32[]{:S(2)}) collective-permute-start(bf16[384,1280]{1,0:T(8,128)(2,1)S(1)} %pad_maximum_fusion.6.refs_5_.refs_9_), channel_id=1, source_target_pairs={{0,1},{1,0},{2,3},{3,2},{4,5},{5,4},{6,7},{7,6},{8,9},{9,8},{10,11... | collective-permute-start | bytes 2949128 | tf_op jit(solution)/shard_map/ppermute | solution.py:445
  47.9 3.8 %collective-permute-start.7 = (bf16[384,1152]{1,0:T(8,128)(2,1)S(1)}, bf16[384,1152]{1,0:T(8,128)(2,1)S(1)}, u32[]{:S(2)}, u32[]{:S(2)}) collective-permute-start(bf16[384,1152]{1,0:T(8,128)(2,1)S(1)} %pad_maximum_fusion.7.refs_3_.refs_7_), channel_id=1, source_target_pairs={{0,1},{1,0},{2,3},{3,2},{4,5},{5,4},{6,7},{7,6},{8,9},{9,8},{10,11... | collective-permute-start | bytes 2654216 | tf_op jit(solution)/shard_map/ppermute | solution.py:445
  53.6 14.1 %collective-permute-start.12 = (bf16[96,1920]{1,0:T(8,128)(2,1)}, bf16[96,1920]{1,0:T(8,128)(2,1)}, u32[]{:S(2)}, u32[]{:S(2)}) collective-permute-start(bf16[96,1920]{1,0:T(8,128)(2,1)} %get-tuple-element.221), channel_id=1, source_target_pairs={{0,2},{1,3},{2,0},{3,1},{4,6},{5,7},{6,4},{7,5},{8,10},{9,11},{10,... | collective-permute-start | bytes 1105928 | tf_op jit(solution)/shard_map/ppermute | solution.py:445
  55.1 12.6 %collective-permute-start.13 = (bf16[96,1920]{1,0:T(8,128)(2,1)S(1)}, bf16[96,1920]{1,0:T(8,128)(2,1)}, u32[]{:S(2)}, u32[]{:S(2)}) collective-permute-start(bf16[96,1920]{1,0:T(8,128)(2,1)S(1)} %get-tuple-element.223), channel_id=1, source_target_pairs={{0,4},{1,5},{2,6},{3,7},{4,0},{5,1},{6,2},{7,3},{8,12},{9,13},{10,... | collective-permute-start | bytes 1105928 | tf_op jit(solution)/shard_map/ppermute | solution.py:445
  71.0 15.4 %collective-permute-start.14 = (bf16[96,768]{1,0:T(8,128)(2,1)S(1)}, bf16[96,768]{1,0:T(8,128)(2,1)S(1)}, u32[]{:S(2)}, u32[]{:S(2)}) collective-permute-start(bf16[96,768]{1,0:T(8,128)(2,1)S(1)} %copy-done.20), channel_id=1, source_target_pairs={{0,8},{1,9},{2,10},{3,11},{4,12},{5,13},{6,14},{7,15},{8,0},{9,1},... | collective-permute-start | bytes 442376 | tf_op jit(solution)/shard_map/ppermute | solution.py:445
  72.6 13.9 %collective-permute-start.15 = (bf16[96,768]{1,0:T(8,128)(2,1)S(1)}, bf16[96,768]{1,0:T(8,128)(2,1)S(1)}, u32[]{:S(2)}, u32[]{:S(2)}) collective-permute-start(bf16[96,768]{1,0:T(8,128)(2,1)S(1)} %copy-done.20), channel_id=1, source_target_pairs={{0,16},{1,17},{2,18},{3,19},{4,20},{5,21},{6,22},{7,23},{8,24},{9,... | collective-permute-start | bytes 442376 | tf_op jit(solution)/shard_map/ppermute | solution.py:445
  75.1 11.4 %collective-permute-start.16 = (bf16[96,768]{1,0:T(8,128)(2,1)S(1)}, bf16[96,768]{1,0:T(8,128)(2,1)S(1)}, u32[]{:S(2)}, u32[]{:S(2)}) collective-permute-start(bf16[96,768]{1,0:T(8,128)(2,1)S(1)} %copy-done.20), channel_id=1, source_target_pairs={{0,24},{1,25},{2,26},{3,27},{4,28},{5,29},{6,30},{7,31},{8,16},{9,... | collective-permute-start | bytes 442376 | tf_op jit(solution)/shard_map/ppermute | solution.py:445
  75.5 17.1 %collective-permute-start.17 = (bf16[192,1920]{1,0:T(8,128)(2,1)S(1)}, bf16[192,1920]{1,0:T(8,128)(2,1)S(1)}, u32[]{:S(2)}, u32[]{:S(2)}) collective-permute-start(bf16[192,1920]{1,0:T(8,128)(2,1)S(1)} %constant_dynamic-update-slice_fusion.12), channel_id=1, source_target_pairs={{0,4},{1,5},{2,6},{3,7},{4,0},{5,1},{6,2},{7,3},{8,12},{9,13},{10,... | collective-permute-start | bytes 2211848 | tf_op jit(solution)/shard_map/ppermute | solution.py:445
  76.4 16.9 %collective-permute-start.18 = (bf16[192,1920]{1,0:T(8,128)(2,1)S(1)}, bf16[192,1920]{1,0:T(8,128)(2,1)S(1)}, u32[]{:S(2)}, u32[]{:S(2)}) collective-permute-start(bf16[192,1920]{1,0:T(8,128)(2,1)S(1)} %constant_dynamic-update-slice_fusion.14), channel_id=1, source_target_pairs={{0,2},{1,3},{2,0},{3,1},{4,6},{5,7},{6,4},{7,5},{8,10},{9,11},{10,... | collective-permute-start | bytes 2211848 | tf_op jit(solution)/shard_map/ppermute | solution.py:445
  93.7 12.7 %collective-permute-start.19 = (bf16[384,1920]{1,0:T(8,128)(2,1)S(1)}, bf16[384,1920]{1,0:T(8,128)(2,1)S(1)}, u32[]{:S(2)}, u32[]{:S(2)}) collective-permute-start(bf16[384,1920]{1,0:T(8,128)(2,1)S(1)} %constant_dynamic-update-slice_fusion.16.refs_5_), channel_id=1, source_target_pairs={{0,1},{1,0},{2,3},{3,2},{4,5},{5,4},{6,7},{7,6},{8,9},{9,8},{10,11... | collective-permute-start | bytes 4423688 | tf_op jit(solution)/shard_map/ppermute | solution.py:445
  93.8 12.6 %collective-permute-start.20 = (bf16[384,1920]{1,0:T(8,128)(2,1)S(1)}, bf16[384,1920]{1,0:T(8,128)(2,1)S(1)}, u32[]{:S(2)}, u32[]{:S(2)}) collective-permute-start(bf16[384,1920]{1,0:T(8,128)(2,1)S(1)} %pad_maximum_fusion.1.refs_7_), channel_id=1, source_target_pairs={{0,1},{1,0},{2,3},{3,2},{4,5},{5,4},{6,7},{7,6},{8,9},{9,8},{10,11... | collective-permute-start | bytes 4423688 | tf_op jit(solution)/shard_map/ppermute | solution.py:445
  94.4 9.4 %collective-permute-start.21 = (bf16[384,384]{1,0:T(8,128)(2,1)S(1)}, bf16[384,384]{1,0:T(8,128)(2,1)S(1)}, u32[]{:S(2)}, u32[]{:S(2)}) collective-permute-start(bf16[384,384]{1,0:T(8,128)(2,1)S(1)} %get-tuple-element.250), channel_id=1, source_target_pairs={{0,2},{1,3},{2,0},{3,1},{4,6},{5,7},{6,4},{7,5},{8,10},{9,11},{10,... | collective-permute-start | bytes 884744 | tf_op jit(solution)/shard_map/ppermute | solution.py:445
  95.0 8.8 %collective-permute-start.22 = (bf16[384,384]{1,0:T(8,128)(2,1)S(1)}, bf16[384,384]{1,0:T(8,128)(2,1)S(1)}, u32[]{:S(2)}, u32[]{:S(2)}) collective-permute-start(bf16[384,384]{1,0:T(8,128)(2,1)S(1)} %get-tuple-element.252), channel_id=1, source_target_pairs={{0,4},{1,5},{2,6},{3,7},{4,0},{5,1},{6,2},{7,3},{8,12},{9,13},{10,... | collective-permute-start | bytes 884744 | tf_op jit(solution)/shard_map/ppermute | solution.py:445
  103.8 15.1 %copy-start.10 = (bf16[6,4,256,256]{3,2,1,0:T(8,128)(2,1)}, bf16[6,4,256,256]{3,2,1,0:T(8,128)(2,1)S(1)}, u32[]{:S(2)}) copy-start(bf16[6,4,256,256]{3,2,1,0:T(8,128)(2,1)S(1)} %get-tuple-element.292.refs_5_) | copy-start | bytes 9437188
  103.9 14.9 %collective-permute-start.23 = (bf16[768,384]{1,0:T(8,128)(2,1)S(1)}, bf16[768,384]{1,0:T(8,128)(2,1)S(1)}, u32[]{:S(2)}, u32[]{:S(2)}) collective-permute-start(bf16[768,384]{1,0:T(8,128)(2,1)S(1)} %pad_maximum_fusion.9), channel_id=1, source_target_pairs={{0,4},{1,5},{2,6},{3,7},{4,0},{5,1},{6,2},{7,3},{8,12},{9,13},{10,... | collective-permute-start | bytes 1769480 | tf_op jit(solution)/shard_map/ppermute | solution.py:445
  105.1 14.5 %collective-permute-start.24 = (bf16[768,384]{1,0:T(8,128)(2,1)S(1)}, bf16[768,384]{1,0:T(8,128)(2,1)S(1)}, u32[]{:S(2)}, u32[]{:S(2)}) collective-permute-start(bf16[768,384]{1,0:T(8,128)(2,1)S(1)} %pad_maximum_fusion.10), channel_id=1, source_target_pairs={{0,2},{1,3},{2,0},{3,1},{4,6},{5,7},{6,4},{7,5},{8,10},{9,11},{10,... | collective-permute-start | bytes 1769480 | tf_op jit(solution)/shard_map/ppermute | solution.py:445
  119.9 9.7 %collective-permute-start.25 = (bf16[1536,384]{1,0:T(8,128)(2,1)S(1)}, bf16[1536,384]{1,0:T(8,128)(2,1)S(1)}, u32[]{:S(2)}, u32[]{:S(2)}) collective-permute-start(bf16[1536,384]{1,0:T(8,128)(2,1)S(1)} %pad_maximum_fusion.3.refs_6_), channel_id=1, source_target_pairs={{0,1},{1,0},{2,3},{3,2},{4,5},{5,4},{6,7},{7,6},{8,9},{9,8},{10,11... | collective-permute-start | bytes 3538952 | tf_op jit(solution)/shard_map/ppermute | solution.py:445
  120.0 9.6 %collective-permute-start.26 = (bf16[1536,384]{1,0:T(8,128)(2,1)S(1)}, bf16[1536,384]{1,0:T(8,128)(2,1)S(1)}, u32[]{:S(2)}, u32[]{:S(2)}) collective-permute-start(bf16[1536,384]{1,0:T(8,128)(2,1)S(1)} %pad_maximum_fusion.4.refs_8_), channel_id=1, source_target_pairs={{0,1},{1,0},{2,3},{3,2},{4,5},{5,4},{6,7},{7,6},{8,9},{9,8},{10,11... | collective-permute-start | bytes 3538952 | tf_op jit(solution)/shard_map/ppermute | solution.py:445
  128.9 11.1 %collective-permute-start.27 = (bf16[1536,384]{1,0:T(8,128)(2,1)S(1)}, bf16[1536,384]{1,0:T(8,128)(2,1)S(1)}, u32[]{:S(2)}, u32[]{:S(2)}) collective-permute-start(bf16[1536,384]{1,0:T(8,128)(2,1)S(1)} %get-tuple-element.271), channel_id=1, source_target_pairs={{0,1},{1,0},{2,3},{3,2},{4,5},{5,4},{6,7},{7,6},{8,9},{9,8},{10,11... | collective-permute-start | bytes 3538952 | tf_op jit(solution)/shard_map/ppermute | solution.py:445
  129.0 11.1 %collective-permute-start.28 = (bf16[1536,384]{1,0:T(8,128)(2,1)S(1)}, bf16[1536,384]{1,0:T(8,128)(2,1)S(1)}, u32[]{:S(2)}, u32[]{:S(2)}) collective-permute-start(bf16[1536,384]{1,0:T(8,128)(2,1)S(1)} %get-tuple-element.272), channel_id=1, source_target_pairs={{0,1},{1,0},{2,3},{3,2},{4,5},{5,4},{6,7},{7,6},{8,9},{9,8},{10,11... | collective-permute-start | bytes 3538952 | tf_op jit(solution)/shard_map/ppermute | solution.py:445
  140.8 15.4 %collective-permute-start.29 = (bf16[768,384]{1,0:T(8,128)(2,1)S(1)}, bf16[768,384]{1,0:T(8,128)(2,1)S(1)}, u32[]{:S(2)}, u32[]{:S(2)}) collective-permute-start(bf16[768,384]{1,0:T(8,128)(2,1)S(1)} %slice.516), channel_id=1, source_target_pairs={{0,4},{1,5},{2,6},{3,7},{4,0},{5,1},{6,2},{7,3},{8,12},{9,13},{10,... | collective-permute-start | bytes 1769480 | tf_op jit(solution)/shard_map/ppermute | solution.py:445
  141.9 15.0 %collective-permute-start.30 = (bf16[768,384]{1,0:T(8,128)(2,1)S(1)}, bf16[768,384]{1,0:T(8,128)(2,1)S(1)}, u32[]{:S(2)}, u32[]{:S(2)}) collective-permute-start(bf16[768,384]{1,0:T(8,128)(2,1)S(1)} %pad_maximum_fusion.11), channel_id=1, source_target_pairs={{0,2},{1,3},{2,0},{3,1},{4,6},{5,7},{6,4},{7,5},{8,10},{9,11},{10,... | collective-permute-start | bytes 1769480 | tf_op jit(solution)/shard_map/ppermute | solution.py:445
  157.3 9.0 %collective-permute-start.31 = (bf16[384,384]{1,0:T(8,128)(2,1)S(1)}, bf16[384,384]{1,0:T(8,128)(2,1)S(1)}, u32[]{:S(2)}, u32[]{:S(2)}) collective-permute-start(bf16[384,384]{1,0:T(8,128)(2,1)S(1)} %slice.521), channel_id=1, source_target_pairs={{0,2},{1,3},{2,0},{3,1},{4,6},{5,7},{6,4},{7,5},{8,10},{9,11},{10,... | collective-permute-start | bytes 884744 | tf_op jit(solution)/shard_map/ppermute | solution.py:445
  158.9 7.6 %collective-permute-start.32 = (bf16[384,384]{1,0:T(8,128)(2,1)S(1)}, bf16[384,384]{1,0:T(8,128)(2,1)S(1)}, u32[]{:S(2)}, u32[]{:S(2)}) collective-permute-start(bf16[384,384]{1,0:T(8,128)(2,1)S(1)} %slice.520), channel_id=1, source_target_pairs={{0,4},{1,5},{2,6},{3,7},{4,0},{5,1},{6,2},{7,3},{8,12},{9,13},{10,... | collective-permute-start | bytes 884744 | tf_op jit(solution)/shard_map/ppermute | solution.py:445
  165.7 16.1 %collective-permute-start.36 = (bf16[384,1920]{1,0:T(8,128)(2,1)S(1)}, bf16[384,1920]{1,0:T(8,128)(2,1)S(1)}, u32[]{:S(2)}, u32[]{:S(2)}) collective-permute-start(bf16[384,1920]{1,0:T(8,128)(2,1)S(1)} %get-tuple-element.298.refs_9_), channel_id=1, source_target_pairs={{0,1},{1,0},{2,3},{3,2},{4,5},{5,4},{6,7},{7,6},{8,9},{9,8},{10,11... | collective-permute-start | bytes 4423688 | tf_op jit(solution)/shard_map/ppermute | solution.py:445
  165.8 16.0 %collective-permute-start.37 = (bf16[384,1920]{1,0:T(8,128)(2,1)S(1)}, bf16[384,1920]{1,0:T(8,128)(2,1)S(1)}, u32[]{:S(2)}, u32[]{:S(2)}) collective-permute-start(bf16[384,1920]{1,0:T(8,128)(2,1)S(1)} %get-tuple-element.299.refs_11_), channel_id=1, source_target_pairs={{0,1},{1,0},{2,3},{3,2},{4,5},{5,4},{6,7},{7,6},{8,9},{9,8},{10,11... | collective-permute-start | bytes 4423688 | tf_op jit(solution)/shard_map/ppermute | solution.py:445
  166.7 14.7 %collective-permute-start.33 = (bf16[96,768]{1,0:T(8,128)(2,1)S(1)}, bf16[96,768]{1,0:T(8,128)(2,1)S(1)}, u32[]{:S(2)}, u32[]{:S(2)}) collective-permute-start(bf16[96,768]{1,0:T(8,128)(2,1)S(1)} %get-tuple-element.295), channel_id=1, source_target_pairs={{0,8},{1,9},{2,10},{3,11},{4,12},{5,13},{6,14},{7,15},{8,0},{9,1},... | collective-permute-start | bytes 442376 | tf_op jit(solution)/shard_map/ppermute | solution.py:445
  167.4 14.4 %collective-permute-start.34 = (bf16[96,768]{1,0:T(8,128)(2,1)S(1)}, bf16[96,768]{1,0:T(8,128)(2,1)S(1)}, u32[]{:S(2)}, u32[]{:S(2)}) collective-permute-start(bf16[96,768]{1,0:T(8,128)(2,1)S(1)} %get-tuple-element.296), channel_id=1, source_target_pairs={{0,16},{1,17},{2,18},{3,19},{4,20},{5,21},{6,22},{7,23},{8,24},{9,... | collective-permute-start | bytes 442376 | tf_op jit(solution)/shard_map/ppermute | solution.py:445
  170.8 11.0 %collective-permute-start.35 = (bf16[96,768]{1,0:T(8,128)(2,1)S(1)}, bf16[96,768]{1,0:T(8,128)(2,1)S(1)}, u32[]{:S(2)}, u32[]{:S(2)}) collective-permute-start(bf16[96,768]{1,0:T(8,128)(2,1)S(1)} %get-tuple-element.297), channel_id=1, source_target_pairs={{0,24},{1,25},{2,26},{3,27},{4,28},{5,29},{6,30},{7,31},{8,16},{9,... | collective-permute-start | bytes 442376 | tf_op jit(solution)/shard_map/ppermute | solution.py:445
  182.7 17.2 %collective-permute-start.38 = (bf16[192,1920]{1,0:T(8,128)(2,1)S(1)}, bf16[192,1920]{1,0:T(8,128)(2,1)S(1)}, u32[]{:S(2)}, u32[]{:S(2)}) collective-permute-start(bf16[192,1920]{1,0:T(8,128)(2,1)S(1)} %slice.515), channel_id=1, source_target_pairs={{0,4},{1,5},{2,6},{3,7},{4,0},{5,1},{6,2},{7,3},{8,12},{9,13},{10,... | collective-permute-start | bytes 2211848 | tf_op jit(solution)/shard_map/ppermute | solution.py:445
  183.8 16.9 %collective-permute-start.39 = (bf16[192,1920]{1,0:T(8,128)(2,1)S(1)}, bf16[192,1920]{1,0:T(8,128)(2,1)S(1)}, u32[]{:S(2)}, u32[]{:S(2)}) collective-permute-start(bf16[192,1920]{1,0:T(8,128)(2,1)S(1)} %pad_maximum_fusion.8), channel_id=1, source_target_pairs={{0,2},{1,3},{2,0},{3,1},{4,6},{5,7},{6,4},{7,5},{8,10},{9,11},{10,... | collective-permute-start | bytes 2211848 | tf_op jit(solution)/shard_map/ppermute | solution.py:445
  201.1 8.2 %collective-permute-start.40 = (bf16[96,1920]{1,0:T(8,128)(2,1)S(1)}, bf16[96,1920]{1,0:T(8,128)(2,1)S(1)}, u32[]{:S(2)}, u32[]{:S(2)}) collective-permute-start(bf16[96,1920]{1,0:T(8,128)(2,1)S(1)} %slice.519), channel_id=1, source_target_pairs={{0,2},{1,3},{2,0},{3,1},{4,6},{5,7},{6,4},{7,5},{8,10},{9,11},{10,... | collective-permute-start | bytes 1105928 | tf_op jit(solution)/shard_map/ppermute | solution.py:445
  201.7 7.8 %collective-permute-start.41 = (bf16[96,1920]{1,0:T(8,128)(2,1)S(1)}, bf16[96,1920]{1,0:T(8,128)(2,1)S(1)}, u32[]{:S(2)}, u32[]{:S(2)}) collective-permute-start(bf16[96,1920]{1,0:T(8,128)(2,1)S(1)} %slice.518), channel_id=1, source_target_pairs={{0,4},{1,5},{2,6},{3,7},{4,0},{5,1},{6,2},{7,3},{8,12},{9,13},{10,... | collective-permute-start | bytes 1105928 | tf_op jit(solution)/shard_map/ppermute | solution.py:445
  207.4 21.3 %collective-permute-start.42 = (bf16[384,1152]{1,0:T(8,128)(2,1)S(1)}, bf16[384,1152]{1,0:T(8,128)(2,1)S(1)}, u32[]{:S(2)}, u32[]{:S(2)}) collective-permute-start(bf16[384,1152]{1,0:T(8,128)(2,1)S(1)} %get-tuple-element.319.refs_14_), channel_id=1, source_target_pairs={{0,1},{1,0},{2,3},{3,2},{4,5},{5,4},{6,7},{7,6},{8,9},{9,8},{10,11... | collective-permute-start | bytes 2654216 | tf_op jit(solution)/shard_map/ppermute | solution.py:445
  207.5 21.2 %collective-permute-start.43 = (bf16[384,1152]{1,0:T(8,128)(2,1)S(1)}, bf16[384,1152]{1,0:T(8,128)(2,1)S(1)}, u32[]{:S(2)}, u32[]{:S(2)}) collective-permute-start(bf16[384,1152]{1,0:T(8,128)(2,1)S(1)} %get-tuple-element.320.refs_16_), channel_id=1, source_target_pairs={{0,1},{1,0},{2,3},{3,2},{4,5},{5,4},{6,7},{7,6},{8,9},{9,8},{10,11... | collective-permute-start | bytes 2654216 | tf_op jit(solution)/shard_map/ppermute | solution.py:445
  209.8 10.5 %collective-permute-start.44 = (bf16[24,3840]{1,0:T(8,128)(2,1)S(1)}, bf16[24,3840]{1,0:T(8,128)(2,1)S(1)}, u32[]{:S(2)}, u32[]{:S(2)}) collective-permute-start(bf16[24,3840]{1,0:T(8,128)(2,1)S(1)} %get-tuple-element.323), channel_id=1, source_target_pairs={{0,8},{1,9},{2,10},{3,11},{4,12},{5,13},{6,14},{7,15},{8,0},{9,1},... | collective-permute-start | bytes 552968 | tf_op jit(solution)/shard_map/ppermute | solution.py:445
  213.5 15.2 %collective-permute-start.45 = (bf16[24,3840]{1,0:T(8,128)(2,1)S(1)}, bf16[24,3840]{1,0:T(8,128)(2,1)S(1)}, u32[]{:S(2)}, u32[]{:S(2)}) collective-permute-start(bf16[24,3840]{1,0:T(8,128)(2,1)S(1)} %get-tuple-element.324), channel_id=1, source_target_pairs={{0,16},{1,17},{2,18},{3,19},{4,20},{5,21},{6,22},{7,23},{8,24},{9,... | collective-permute-start | bytes 552968 | tf_op jit(solution)/shard_map/ppermute | solution.py:445
  214.5 14.1 %collective-permute-start.46 = (bf16[24,3840]{1,0:T(8,128)(2,1)S(1)}, bf16[24,3840]{1,0:T(8,128)(2,1)S(1)}, u32[]{:S(2)}, u32[]{:S(2)}) collective-permute-start(bf16[24,3840]{1,0:T(8,128)(2,1)S(1)} %get-tuple-element.325), channel_id=1, source_target_pairs={{0,24},{1,25},{2,26},{3,27},{4,28},{5,29},{6,30},{7,31},{8,16},{9,... | collective-permute-start | bytes 552968 | tf_op jit(solution)/shard_map/ppermute | solution.py:445
  230.8 14.1 %collective-permute-start.47 = (bf16[192,1152]{1,0:T(8,128)(2,1)}, bf16[192,1152]{1,0:T(8,128)(2,1)}, u32[]{:S(2)}, u32[]{:S(2)}) collective-permute-start(bf16[192,1152]{1,0:T(8,128)(2,1)} %slice.517), channel_id=1, source_target_pairs={{0,4},{1,5},{2,6},{3,7},{4,0},{5,1},{6,2},{7,3},{8,12},{9,13},{10,... | collective-permute-start | bytes 1327112 | tf_op jit(solution)/shard_map/ppermute | solution.py:445
  231.9 13.0 %collective-permute-start.48 = (bf16[192,1152]{1,0:T(8,128)(2,1)}, bf16[192,1152]{1,0:T(8,128)(2,1)}, u32[]{:S(2)}, u32[]{:S(2)}) collective-permute-start(bf16[192,1152]{1,0:T(8,128)(2,1)} %pad_maximum_fusion.12), channel_id=1, source_target_pairs={{0,2},{1,3},{2,0},{3,1},{4,6},{5,7},{6,4},{7,5},{8,10},{9,11},{10,... | collective-permute-start | bytes 1327112 | tf_op jit(solution)/shard_map/ppermute | solution.py:445
  245.7 1.7 collective-permute-start.54
  248.1 3.7 %collective-permute-start.55 = (f32[8,240]{1,0:T(8,128)S(1)}, f32[8,240]{1,0:T(8,128)S(1)}, u32[]{:S(2)}, u32[]{:S(2)}) collective-permute-start(f32[8,240]{1,0:T(8,128)S(1)} %slice.430), channel_id=1, source_target_pairs={{0,4},{1,5},{2,6},{3,7},{4,0},{5,1},{6,2},{7,3},{8,12},{9,13},{10,... | collective-permute-start | bytes 23048 | tf_op jit(solution)/shard_map/ppermute | solution.py:445
  251.8 3.6 %collective-permute-start.56 = (f32[4,240]{1,0:T(4,128)S(1)}, f32[4,240]{1,0:T(4,128)S(1)}, u32[]{:S(2)}, u32[]{:S(2)}) collective-permute-start(f32[4,240]{1,0:T(4,128)S(1)} %slice.432), channel_id=1, source_target_pairs={{0,2},{1,3},{2,0},{3,1},{4,6},{5,7},{6,4},{7,5},{8,10},{9,11},{10,... | collective-permute-start | bytes 11528 | tf_op jit(solution)/shard_map/ppermute | solution.py:445
  255.4 7.0 %collective-permute-start.59 = (f32[1,240]{1,0:T(1,128)S(1)}, f32[1,240]{1,0:T(1,128)S(1)}, u32[]{:S(2)}, u32[]{:S(2)}) collective-permute-start(f32[1,240]{1,0:T(1,128)S(1)} %get-tuple-element.427), channel_id=1, source_target_pairs={{0,24},{1,25},{2,26},{3,27},{4,28},{5,29},{6,30},{7,31},{8,16},{9,... | collective-permute-start | bytes 2888 | tf_op jit(solution)/shard_map/ppermute | solution.py:445
  257.4 5.0 %collective-permute-start.58 = (f32[1,240]{1,0:T(1,128)S(1)}, f32[1,240]{1,0:T(1,128)S(1)}, u32[]{:S(2)}, u32[]{:S(2)}) collective-permute-start(f32[1,240]{1,0:T(1,128)S(1)} %get-tuple-element.428), channel_id=1, source_target_pairs={{0,16},{1,17},{2,18},{3,19},{4,20},{5,21},{6,22},{7,23},{8,24},{9,... | collective-permute-start | bytes 2888 | tf_op jit(solution)/shard_map/ppermute | solution.py:445
  259.4 3.6 %collective-permute-start.57 = (f32[1,240]{1,0:T(1,128)S(1)}, f32[1,240]{1,0:T(1,128)S(1)}, u32[]{:S(2)}, u32[]{:S(2)}) collective-permute-start(f32[1,240]{1,0:T(1,128)S(1)} %get-tuple-element.426), channel_id=1, source_target_pairs={{0,8},{1,9},{2,10},{3,11},{4,12},{5,13},{6,14},{7,15},{8,0},{9,1},... | collective-permute-start | bytes 2888 | tf_op jit(solution)/shard_map/ppermute | solution.py:445
  261.0 6.0 %collective-permute-start.49 = (bf16[96,1152]{1,0:T(8,128)(2,1)S(1)}, bf16[96,1152]{1,0:T(8,128)(2,1)S(1)}, u32[]{:S(2)}, u32[]{:S(2)}) collective-permute-start(bf16[96,1152]{1,0:T(8,128)(2,1)S(1)} %slice.523), channel_id=1, source_target_pairs={{0,2},{1,3},{2,0},{3,1},{4,6},{5,7},{6,4},{7,5},{8,10},{9,11},{10,... | collective-permute-start | bytes 663560 | tf_op jit(solution)/shard_map/ppermute | solution.py:445
  261.5 5.9 %collective-permute-start.50 = (bf16[96,1152]{1,0:T(8,128)(2,1)S(1)}, bf16[96,1152]{1,0:T(8,128)(2,1)S(1)}, u32[]{:S(2)}, u32[]{:S(2)}) collective-permute-start(bf16[96,1152]{1,0:T(8,128)(2,1)S(1)} %slice.522), channel_id=1, source_target_pairs={{0,4},{1,5},{2,6},{3,7},{4,0},{5,1},{6,2},{7,3},{8,12},{9,13},{10,... | collective-permute-start | bytes 663560 | tf_op jit(solution)/shard_map/ppermute | solution.py:445
  267.5 9.9 %copy-start.19 = (f32[24,2304]{1,0:T(8,128)S(1)}, f32[24,2304]{1,0:T(8,128)}, u32[]{:S(2)}) copy-start(f32[24,2304]{1,0:T(8,128)} %param.27) | copy-start | bytes 663556
  267.7 5.6 %collective-permute-start.51 = (bf16[24,2304]{1,0:T(8,128)(2,1)S(1)}, bf16[24,2304]{1,0:T(8,128)(2,1)S(1)}, u32[]{:S(2)}, u32[]{:S(2)}) collective-permute-start(bf16[24,2304]{1,0:T(8,128)(2,1)S(1)} %get-tuple-element.337), channel_id=1, source_target_pairs={{0,8},{1,9},{2,10},{3,11},{4,12},{5,13},{6,14},{7,15},{8,0},{9,1},... | collective-permute-start | bytes 331784 | tf_op jit(solution)/shard_map/ppermute | solution.py:445
  269.4 8.0 %collective-permute-start.52 = (bf16[24,2304]{1,0:T(8,128)(2,1)S(1)}, bf16[24,2304]{1,0:T(8,128)(2,1)S(1)}, u32[]{:S(2)}, u32[]{:S(2)}) collective-permute-start(bf16[24,2304]{1,0:T(8,128)(2,1)S(1)} %get-tuple-element.338), channel_id=1, source_target_pairs={{0,16},{1,17},{2,18},{3,19},{4,20},{5,21},{6,22},{7,23},{8,24},{9,... | collective-permute-start | bytes 331784 | tf_op jit(solution)/shard_map/ppermute | solution.py:445
  270.4 7.0 %collective-permute-start.53 = (bf16[24,2304]{1,0:T(8,128)(2,1)S(1)}, bf16[24,2304]{1,0:T(8,128)(2,1)S(1)}, u32[]{:S(2)}, u32[]{:S(2)}) collective-permute-start(bf16[24,2304]{1,0:T(8,128)(2,1)S(1)} %get-tuple-element.339), channel_id=1, source_target_pairs={{0,24},{1,25},{2,26},{3,27},{4,28},{5,29},{6,30},{7,31},{8,16},{9,... | collective-permute-start | bytes 331784 | tf_op jit(solution)/shard_map/ppermute | solution.py:445
  (27 other events, 102.3 us)

commit v3 on v2

v3 whole, which is shorter than its diff:
```python
import functools

import jax
import jax.numpy as jnp
from jax import lax
from jax.experimental import pallas as pl
from jax.experimental.pallas import tpu as pltpu
from jax.sharding import PartitionSpec as P

D = 768
HEADS = 12
FF = 3072
STEP = 10
HALF = 384
WIN = 256
SMALL = 160
LARGE = 240
LOG2E = 1.4426950408889634
CUT_ONE = 1152
WIDTH_ONE = 1280
WIDTH_TWO = 1920
WIDTH_THREE = 384

EPSILON = 1e-05
BETA_ONE = 0.9
BETA_TWO = 0.999
ADAM_EPS = 1e-08
RATE_MATRIX = 0.05
DECAY_MATRIX = 0.05
RATE_VECTOR = 0.3

AXES = ("dp", "fsdp")
LOW = jnp.bfloat16
WIDE = jnp.float32
VMEM_BYTES = 12 * 2**20


def nn(left, right):
    return lax.dot_general(left, right, (((1,), (0,)), ((), ())), preferred_element_type=WIDE)


def nt(left, right):
    return lax.dot_general(left, right, (((1,), (1,)), ((), ())), preferred_element_type=WIDE)


def tn(left, right):
    return lax.dot_general(left, right, (((0,), (0,)), ((), ())), preferred_element_type=WIDE)


def shape(rows, cols, kind=LOW):
    return jax.ShapeDtypeStruct((rows, cols), kind)


def later(kernel, inputs, extra):
    return lambda *refs: kernel(*refs[:inputs], *refs[inputs + extra :])


def whole_call(kernel, outs, scratch, smem, name, flops, *args, anywhere=(), after=()):
    specs = []
    for i in range(len(args)):
        space = pltpu.SMEM if i < smem else pl.ANY if i in anywhere else pltpu.VMEM
        specs.append(pl.BlockSpec(memory_space=space))
    moved = sum(a.size * a.dtype.itemsize for a in args) + sum(o.size * o.dtype.itemsize for o in outs)
    return pl.pallas_call(
        later(kernel, len(args), len(after)),
        in_specs=specs + [pl.BlockSpec(memory_space=pl.ANY)] * len(after),
        out_specs=[pl.BlockSpec(memory_space=pltpu.VMEM)] * len(outs),
        out_shape=outs,
        scratch_shapes=scratch,
        compiler_params=pltpu.CompilerParams(vmem_limit_bytes=VMEM_BYTES),
        cost_estimate=pl.CostEstimate(flops=flops, bytes_accessed=moved, transcendentals=0),
        name=name,
    )(*args, *after)


def over_rows(count, step, body, init=None):
    return lax.fori_loop(0, count // step, lambda i, c: body(pl.ds(pl.multiple_of(i * step, step), step), c), init)


def normal(values):
    centre = values - jnp.mean(values, axis=-1, keepdims=True)
    rstd = lax.rsqrt(jnp.mean(centre * centre, axis=-1, keepdims=True) + EPSILON)
    return centre * rstd, rstd


def both(pair, side, lo, width):
    rows = slice(HALF * side, HALF * (side + 1))
    return jnp.concatenate([z[rows, lo : lo + width] for z in pair], axis=0)


def qkv_kernel(x_ref, vec_ref, order_ref, own, other, a_ref, qkv_ref, tmp):
    gain, shift = vec_ref[0:1, :], vec_ref[1:2, :]

    def norm(rows, _):
        tmp[rows, :] = (normal(x_ref[rows, :].astype(WIDE))[0] * gain + shift).astype(LOW)

    over_rows(x_ref.shape[0], 144, norm)
    a_ref[...] = nn(tmp[...], order_ref[...]).astype(LOW)
    for col in range(0, 3 * D, 384):
        w = both((own, other), *divmod(col, CUT_ONE), 384)
        qkv_ref[:, col : col + 384] = nn(a_ref[...], w).astype(LOW)


def project(x, vec, order, one, after=()):
    n = x.shape[0]
    return whole_call(
        qkv_kernel, [shape(n, D), shape(n, 3 * D)], [pltpu.VMEM((n, D), LOW)], 0, "project",
        2 * n * D * (4 * D), x, vec, order, *one, after=after,
    )


def each_tile(spans, body):
    def step(t, carry):
        for kind, rows in ((1, SMALL), (2, LARGE)):

            @pl.when(spans[t, 4] == kind)
            def _():
                body(t, pl.multiple_of(spans[t, 2], 16), rows, pl.multiple_of(spans[t, 3], 16))

        return carry

    lax.fori_loop(0, 4, step, 0)


def padding_rows(spans, shape_):
    return lax.broadcasted_iota(jnp.int32, shape_, 0) >= spans[4, 0]


def own_half(values, e):
    lane = lax.broadcasted_iota(jnp.int32, values.shape, 1)
    return jnp.where((lane < 64) if e == 0 else (lane >= 64), values, jnp.zeros_like(values))


def attend_kernel(base, spans, slopes, qkv_ref, far_ref, o_ref, p_ref, acc):
    acc[...] = jnp.zeros_like(acc)

    def tile(t, at, count, key):
        rows, keys = pl.ds(at, count), pl.ds(key, WIN)
        row = lax.broadcasted_iota(jnp.int32, (count, 1), 0) + at
        inside = ((row >= spans[t, 0]) & (row < spans[t, 1])).astype(WIDE)
        far = far_ref[t, :count, :]
        for pair in range(3):
            col = (base + pair) * 128
            q, k, v = [qkv_ref[z, col + i * D : col + i * D + 128] for i, z in enumerate((rows, keys, keys))]
            out = None
            for e in range(2):
                s = nt(q, own_half(k, e)) * (0.125 * LOG2E) - slopes[2 * (base + pair) + e] * far
                p = jnp.exp2(s - jnp.max(s, axis=1, keepdims=True))
                p = (p * (inside / jnp.sum(p, axis=1, keepdims=True))).astype(LOW)
                p_ref[t, 2 * pair + e, :count, :] = p
                part = nn(p, own_half(v, e))
                out = part if out is None else out + part
            acc[rows, pair * 128 : pair * 128 + 128] += out

    each_tile(spans, tile)
    v = qkv_ref[:, base * 128 + 2 * D : base * 128 + 2 * D + HALF]
    o_ref[...] = jnp.where(padding_rows(spans, v.shape), v, acc[...].astype(LOW))


def attend(base, qkv, far, spans, slopes, after=()):
    n = qkv.shape[0]
    return whole_call(
        functools.partial(attend_kernel, base),
        [shape(n, HALF), jax.ShapeDtypeStruct((4, HEADS // 2, LARGE, WIN), LOW)],
        [pltpu.VMEM((n, HALF), WIDE)], 2, "attend", 9 * 10**9, spans, slopes, qkv, far, after=after,
    )


def attend_back_kernel(base, spans, qkv_ref, g_ref, p_ref, dq_ref, dk_ref, dv_ref, aq, ak, av):
    for acc in (aq, ak, av):
        acc[...] = jnp.zeros_like(acc)

    def tile(t, at, count, key):
        rows, keys = pl.ds(at, count), pl.ds(key, WIN)
        for pair in range(3):
            col = (base + pair) * 128
            q, k, v = [qkv_ref[z, col + i * D : col + i * D + 128] for i, z in enumerate((rows, keys, keys))]
            g = g_ref[rows, col : col + 128]
            sums = None
            for e in range(2):
                ge = own_half(g, e)
                p = p_ref[t, 2 * pair + e, :count, :]
                wide = p.astype(WIDE)
                d = wide * nt(ge * 0.125, v)
                d = (d - wide * jnp.sum(d, axis=1, keepdims=True)).astype(LOW)
                parts = (nn(d, own_half(k, e)), tn(d, own_half(q, e)), tn(p, ge))
                sums = parts if sums is None else tuple(a + b for a, b in zip(sums, parts))
            part = slice(pair * 128, pair * 128 + 128)
            aq[rows, part] += sums[0]
            ak[keys, part] += sums[1]
            av[keys, part] += sums[2]

    each_tile(spans, tile)
    dq_ref[...] = aq[...].astype(LOW)
    dk_ref[...] = ak[...].astype(LOW)
    g = g_ref[:, base * 128 : base * 128 + HALF]
    dv_ref[...] = jnp.where(padding_rows(spans, g.shape), g, av[...].astype(LOW))


def attend_back(base, qkv, grad, probs, spans, after=()):
    n = qkv.shape[0]
    return whole_call(
        functools.partial(attend_back_kernel, base), [shape(n, HALF)] * 3, [pltpu.VMEM((n, HALF), WIDE)] * 3, 1,
        "attend_back", 12 * 10**9, spans, qkv, grad, probs, after=after,
    )


def tables(seg, side, valid):
    n = seg.shape[0]
    tiles = jnp.arange(4, dtype=jnp.int32)
    low = jnp.sum((seg[None, :] < tiles[:, None]).astype(jnp.int32), axis=1)
    high = jnp.sum((seg[None, :] <= tiles[:, None]).astype(jnp.int32), axis=1)
    live = jnp.sum(valid)
    small = high - low <= SMALL - 16
    kind = jnp.where((high > low) & (low < live), jnp.where(small, 1, 2), 0)
    at = jnp.minimum(low // 16 * 16, jnp.where(small, n - SMALL, n - LARGE))
    key = jnp.minimum(low // 16 * 16, n - WIN)
    spans = jnp.stack([low, high, at, key, kind], axis=1)
    spans = jnp.concatenate([spans, jnp.broadcast_to(live, (1, 5))], axis=0)
    place = jnp.arange(n, dtype=jnp.int32) - jnp.sum((seg[None, :] < seg[:, None]).astype(jnp.int32), axis=1)
    packed = jnp.stack([place // side, place % side, seg], axis=0)
    packed = jnp.pad(packed, ((0, 0), (0, WIN)), constant_values=-1)
    row = jnp.stack([lax.dynamic_slice(packed, (0, at[t]), (3, LARGE)) for t in range(4)], axis=0)[:, :, :, None]
    col = jnp.stack([lax.dynamic_slice(packed, (0, key[t]), (3, WIN)) for t in range(4)], axis=0)[:, :, None, :]
    allowed = (row[:, 2] == tiles[:, None, None]) & (col[:, 2] == tiles[:, None, None])
    down, along = [(row[:, i] - col[:, i]).astype(WIDE) for i in (0, 1)]
    return spans, jnp.where(allowed, jnp.sqrt(down * down + along * along), 1e12)


def bell(u):
    share = 0.5 + 0.5 * lax.erf(u * 0.7071067811865476)
    return u * share, share + u * (jnp.exp2(u * u * -0.7213475204444817) * 0.3989422804014327)


def up_kernel(x_ref, o0_ref, o1_ref, vec_ref, order_ref, own, other, mixed_ref, h_ref, a_ref, gl_ref, gp_ref, tmp):
    mixed_ref[...] = (
        nn(o0_ref[...], order_ref[:HALF, :]) + nn(o1_ref[...], order_ref[HALF:, :])
    ).astype(LOW)
    for col in (0, 384):
        part = slice(col, col + 384)
        h_ref[:, part] = x_ref[:, part].astype(WIDE) + nn(mixed_ref[...], both((own, other), 0, col, 384)) + vec_ref[2:3, part]
    gain, shift = vec_ref[3:4, :], vec_ref[4:5, :]

    def norm(rows, _):
        tmp[rows, :] = (normal(h_ref[rows, :])[0] * gain + shift).astype(LOW)

    over_rows(x_ref.shape[0], 144, norm)
    a_ref[...] = nn(tmp[...], order_ref[...]).astype(LOW)
    for col in range(0, FF, 384):
        k = 5 + col // D
        u = nn(a_ref[...], both((own, other), *divmod(col + D, WIDTH_TWO), 384)) + vec_ref[k : k + 1, col % D : col % D + 384]
        value, slope = bell(u)
        gl_ref[:, col : col + 384] = value.astype(LOW)
        gp_ref[:, col : col + 384] = slope.astype(LOW)


def upward(x, o, vec, order, two, after=()):
    n = x.shape[0]
    return whole_call(
        up_kernel, [shape(n, D), shape(n, D, WIDE), shape(n, D), shape(n, FF), shape(n, FF)],
        [pltpu.VMEM((n, D), LOW)], 0, "upward", 2 * n * D * (7 * D) * 2, x, *o, vec, order, *two,
        after=after,
    )


def down_kernel(place, vec_ref, gl_ref, gp_ref, dy_ref, h_ref, own, other, out_ref, dur_ref, vg_ref, wd, sem):
    def copies(b, piece, row):
        dst = pl.ds(pl.multiple_of(b * 96, 96), 96)
        return [
            pltpu.make_async_copy(
                piece.at[pl.ds(pl.multiple_of(row * 96 + side * (FF // 2), 96), 96), :],
                wd.at[dst, pl.ds(side * WIDTH_THREE, WIDTH_THREE)],
                sem.at[b // 4],
            )
            for side in (0, 1)
        ]

    def begin(b, carry):
        p = place[b]
        pl.when(p < 16)(lambda: [z.start() for z in copies(b, own, p)] and None)
        pl.when(p >= 16)(lambda: [z.start() for z in copies(b, other, p - 16)] and None)
        return carry

    def finish(b, carry):
        for z in copies(b, own, 0):
            z.wait()
        return carry

    lax.fori_loop(0, 32, begin, 0)
    for col in range(0, FF, 384):
        part = slice(col, col + 384)
        lax.fori_loop(col // 96, col // 96 + 4, finish, 0)
        du = nt(dy_ref[...], wd[part, :]) * gp_ref[:, part].astype(WIDE)
        dur_ref[:, part] = du.astype(LOW)
        k = col // D
        vg_ref[k : k + 1, col % D : col % D + 384] = jnp.sum(du, axis=0, keepdims=True)
    for col in (0, 384):
        part = slice(col, col + 384)
        out_ref[:, part] = (h_ref[:, part] + nn(gl_ref[...], wd[:, part]) + vec_ref[9:10, part]).astype(LOW)


def downward(place, vec, gl, gp, dy, h, three, after=()):
    n = h.shape[0]
    return whole_call(
        down_kernel, [shape(n, D), shape(n, FF), shape(8, D, WIDE)],
        [pltpu.VMEM((FF, D), LOW), pltpu.SemaphoreType.DMA((8,))], 1, "downward",
        2 * n * D * (8 * D), place, vec, gl, gp, dy, h, *three, anywhere=(6, 7), after=after,
    )


def hidden_kernel(vec_ref, order_ref, dur_ref, dy_ref, h_ref, own, other, dh_ref, dhr_ref, dor_ref, vg_ref, tmp):
    split = WIDTH_TWO - D
    for i, w in enumerate((own, other)):
        tmp[:, HALF * i : HALF * (i + 1)] = (
            nt(dur_ref[:, :split], w[:HALF, D:]) + nt(dur_ref[:, split:], w[HALF:, :])
        ).astype(LOW)
    dh_ref[...] = nt(tmp[...], order_ref[...])
    gain = vec_ref[3:4, :]

    def step(rows, sums):
        e = dh_ref[rows, :]
        dy = dy_ref[rows, :].astype(WIDE)
        n, rstd = normal(h_ref[rows, :])
        w = e * gain
        dh = dy + rstd * (w - jnp.mean(w, axis=-1, keepdims=True) - n * jnp.mean(w * n, axis=-1, keepdims=True))
        dh_ref[rows, :] = dh
        dhr_ref[rows, :] = dh.astype(LOW)
        return tuple(s + jnp.sum(z.reshape(-1, 8, D), axis=0) for s, z in zip(sums, (dh, e * n, e, dy)))

    zero = jnp.zeros((8, D), WIDE)
    sums = over_rows(h_ref.shape[0], 144, step, (zero,) * 4)
    for k, s in enumerate(sums):
        vg_ref[k : k + 1, :] = jnp.sum(s, axis=0, keepdims=True)
    for i, w in enumerate((own, other)):
        tmp[:, HALF * i : HALF * (i + 1)] = nt(dhr_ref[...], w[:HALF, :D]).astype(LOW)
    dor_ref[...] = nt(tmp[...], order_ref[...]).astype(LOW)


def hidden_grad(vec, order, dur, dy, h, two, after=()):
    n = h.shape[0]
    return whole_call(
        hidden_kernel, [shape(n, D, WIDE), shape(n, D), shape(n, D), shape(8, D, WIDE)],
        [pltpu.VMEM((n, D), LOW)], 0, "hidden_grad",
        2 * n * D * (7 * D), vec, order, dur, dy, h, *two, after=after,
    )


def down_grad_kernel(place, gl_ref, dy_ref, own, other):
    for c in range(8):
        t = tn(gl_ref[:, 384 * c : 384 * (c + 1)], dy_ref[...]).astype(LOW)
        for i in range(4):
            p = place[4 * c + i]

            def put(piece, row):
                for side in (0, 1):
                    rows = pl.ds(pl.multiple_of(row * 96 + side * (FF // 2), 96), 96)
                    piece[rows, :] = t[96 * i : 96 * (i + 1), side * WIDTH_THREE : (side + 1) * WIDTH_THREE]

            pl.when(p < 16)(lambda: put(own, p))
            pl.when(p >= 16)(lambda: put(other, p - 16))


def down_grad(place, gl, dy, after=()):
    n = dy.shape[0]
    return whole_call(down_grad_kernel, [shape(FF, WIDTH_THREE)] * 2, [], 1, "down_grad", 2 * n * D * FF, place, gl, dy, after=after)


def two_grad_kernel(mixed_ref, a_ref, dhr_ref, dur_ref, own, other):
    for col in range(0, D + FF, 384):
        left, right = (mixed_ref, dhr_ref[:, col : col + 384]) if col < D else (a_ref, dur_ref[:, col - D : col - D + 384])
        t = tn(left[...], right).astype(LOW)
        side, lo = divmod(col, WIDTH_TWO)
        own[HALF * side : HALF * (side + 1), lo : lo + 384] = t[:HALF]
        other[HALF * side : HALF * (side + 1), lo : lo + 384] = t[HALF:]


def two_grad(mixed, a, dhr, dur, after=()):
    n = a.shape[0]
    return whole_call(two_grad_kernel, [shape(D, WIDTH_TWO)] * 2, [], 0, "two_grad", 2 * n * D * (D + FF), mixed, a, dhr, dur,
                      after=after)


def one_grad_kernel(a_ref, *refs):
    halves, (own, other) = refs[:6], refs[6:]
    for i, half in enumerate(halves):
        t = tn(a_ref[...], half[...]).astype(LOW)
        side, lo = divmod(384 * i, CUT_ONE)
        own[HALF * side : HALF * (side + 1), lo : lo + 384] = t[:HALF]
        other[HALF * side : HALF * (side + 1), lo : lo + 384] = t[HALF:]


def one_grad(a, d, after=()):
    n = a.shape[0]
    return whole_call(one_grad_kernel, [shape(D, CUT_ONE)] * 2, [], 0, "one_grad", 2 * n * D * 3 * D, a, *d, after=after)


def input_back_kernel(order_ref, q0, q1, k0, k1, v0, v1, own, other, e_ref, tmp):
    for i, w in enumerate((own, other)):
        total = 0.0
        for j, d in enumerate((q0, q1, k0, k1, v0, v1)):
            side, lo = divmod(384 * j, CUT_ONE)
            total = total + nt(d[...], w[HALF * side : HALF * (side + 1), lo : lo + 384])
        tmp[:, HALF * i : HALF * (i + 1)] = total.astype(LOW)
    e_ref[...] = nt(tmp[...], order_ref[...])


def input_back(order, d, one, after=()):
    n = d[0].shape[0]
    return whole_call(
        input_back_kernel, [shape(n, D, WIDE)], [pltpu.VMEM((n, D), LOW)], 0, "input_back",
        2 * n * D * 4 * D, order, *d, *one, after=after,
    )[0]


def input_kernel(x_ref, vec_ref, e_ref, dh_ref, dx_ref, vg_ref):
    gain = vec_ref[0:1, :]

    def step(rows, sums):
        e = e_ref[rows, :]
        n, rstd = normal(x_ref[rows, :].astype(WIDE))
        w = e * gain
        dx_ref[rows, :] = dh_ref[rows, :] + rstd * (
            w - jnp.mean(w, axis=-1, keepdims=True) - n * jnp.mean(w * n, axis=-1, keepdims=True)
        )
        return tuple(s + jnp.sum(z.reshape(-1, 8, D), axis=0) for s, z in zip(sums, (e * n, e)))

    zero = jnp.zeros((8, D), WIDE)
    sums = over_rows(x_ref.shape[0], 144, step, (zero,) * 2)
    for k, s in enumerate(sums):
        vg_ref[k : k + 1, :] = jnp.sum(s, axis=0, keepdims=True)


def input_grad(x, vec, e, dh, after=()):
    n = x.shape[0]
    return whole_call(
        input_kernel, [shape(n, D, WIDE), shape(8, D, WIDE)], [], 0, "input_grad",
        2 * n * D * 3 * D, x, vec, e, dh, after=after,
    )


def near_kernel(a, b, c, d, left_ref, right_ref):
    cut = left_ref.shape[1]
    for out, lo in ((left_ref, 0), (right_ref, cut)):
        out[...] = jnp.concatenate([z[:, lo : lo + cut].astype(WIDE) for z in (a, b, c, d)], axis=0).astype(LOW)


def near_pieces(pieces, after=()):
    rows, cols = pieces[0].shape
    return whole_call(near_kernel, [shape(4 * rows, cols // 2)] * 2, [], 0, "near", 1, *pieces, after=after)


def first_kernel(left, got_left, right, got_right, left_ref, right_ref):
    rows = left.shape[0]
    for out, mine, got in ((left_ref, left, got_left), (right_ref, right, got_right)):
        out[:rows, :] = mine[...]
        out[rows:, :] = got[...]


def first_pieces(left, right, got, after=()):
    rows, cols = left.shape
    return whole_call(
        first_kernel, [shape(2 * rows, cols)] * 2, [], 0, "first", 1, left, got[0], right, got[1], after=after
    )


def second_kernel(left, got, right, far, own_ref):
    rows = left.shape[0]
    half = rows // 2
    own_ref[:rows, :] = left[...]
    own_ref[rows : 2 * rows, :] = got[...]
    for i in (0, 1):
        own_ref[2 * rows + 2 * i * half : 2 * rows + (2 * i + 1) * half, :] = right[i * half : (i + 1) * half, :]
        own_ref[2 * rows + (2 * i + 1) * half : 2 * rows + (2 * i + 2) * half, :] = far[i * half : (i + 1) * half, :]


def second_pieces(left, right, got, after=()):
    rows, cols = left.shape
    return whole_call(
        second_kernel, [shape(4 * rows, cols)], [], 0, "second", 1, left, got[0], right, got[1], after=after
    )[0]


def core_sum_kernel(own, got, left_keep, right_keep, left_out, right_out):
    half = left_keep.shape[0]
    rows = half // 2

    def total(lo, count):
        return own[lo : lo + count, :].astype(WIDE) + got[lo : lo + count, :].astype(WIDE)

    left_keep[...] = total(0, half)
    left_out[...] = total(half, half).astype(LOW)
    for i in (0, 1):
        lo = 2 * half + 2 * i * rows
        right_keep[i * rows : (i + 1) * rows, :] = total(lo, rows)
        right_out[i * rows : (i + 1) * rows, :] = total(lo + rows, rows).astype(LOW)


def core_sum(own, got, after=()):
    rows, cols = own.shape[0] // 4, own.shape[1]
    return whole_call(
        core_sum_kernel, [shape(rows, cols, WIDE)] * 2 + [shape(rows, cols)] * 2, [], 0, "core_sum", 1, own, got,
        after=after,
    )


def half_sum_kernel(left, got_left, right, got_right, left_keep, right_keep, left_out, right_out):
    rows = left_keep.shape[0]
    for mine, got, keep, out in ((left, got_left, left_keep, left_out), (right, got_right, right_keep, right_out)):
        keep[...] = mine[:rows, :] + got[:rows, :].astype(WIDE)
        out[...] = (mine[rows:, :] + got[rows:, :].astype(WIDE)).astype(LOW)


def half_sum(left, right, got, after=()):
    rows, cols = left.shape[0] // 2, left.shape[1]
    return whole_call(
        half_sum_kernel, [shape(rows, cols, WIDE)] * 2 + [shape(rows, cols)] * 2, [], 0, "half_sum", 1,
        left, got[0], right, got[1], after=after,
    )


def last_sum_kernel(left, got_left, right, got_right, keep, *outs):
    unit, cut = keep.shape[0], left.shape[1]
    for lo, mine, got in ((0, left, got_left), (cut, right, got_right)):
        total = mine[...] + got[...].astype(WIDE)
        keep[:, lo : lo + cut] = total[:unit]
        for i, out in enumerate(outs):
            out[:, lo : lo + cut] = total[unit * (i + 1) : unit * (i + 2)].astype(LOW)


def last_sum(left, right, got, after=()):
    unit, cols = left.shape[0] // 4, 2 * left.shape[1]
    return whole_call(
        last_sum_kernel, [shape(unit, cols, WIDE)] + [shape(unit, cols)] * 3, [], 0, "last_sum", 1,
        left, got[0], right, got[1], after=after,
    )


def swap(value, bits):
    pairs = [(i, i ^ bits) for i in range(32)]
    return lax.ppermute(value, AXES, pairs)


def tie(values, *first):
    return lax.optimization_barrier((tuple(values), first))[0]


def transfer(firsts, stage, values, *bits):
    values = tie(values, firsts.get((stage, "start"), ()))
    got = firsts[stage, "got"] = tuple(swap(value, bit) for value, bit in zip(values, bits))
    return tie(got, firsts.get((stage, "end"), ()))


def spread(block, firsts):
    move = functools.partial(transfer, firsts)
    left, right = firsts[0, "ready"] = tuple(near_pieces((block,) + move(0, (block,) * 3, 8, 16, 24)))
    yield
    left, right = firsts[1, "ready"] = tuple(first_pieces(left, right, move(1, (left, right), 2, 4)))
    yield
    own = second_pieces(left, right, move(2, (left, right), 4, 2))
    firsts[2, "ready"] = (own,)
    yield
    (other,) = move(3, (own,), 1)
    yield own, other


def collect(pieces, firsts):
    move = functools.partial(transfer, firsts)
    (got,) = move(0, (pieces[1],), 1)
    left, right, *out = firsts[0, "ready"] = tuple(core_sum(pieces[0], got))
    yield
    left, right, *out = firsts[1, "ready"] = tuple(half_sum(left, right, move(1, out, 4, 2)))
    yield
    total, *out = firsts[2, "ready"] = tuple(last_sum(left, right, move(2, out, 2, 4)))
    yield
    got = move(3, out, 8, 16, 24)
    yield
    yield sum((z.astype(WIDE) for z in got), total)


def collect_vec(blocks, ends):
    half = blocks.shape[0] // 2
    (got,) = tie((swap(blocks[half:], 1),), ends[0])
    blocks = blocks[:half] + got
    rows = half // 4
    got = tie([swap(blocks[rows * k : rows * (k + 1)], 2 * k) for k in (1, 2, 3)], ends[1])
    blocks = sum(got, blocks[:rows])
    return sum((swap(blocks[k : k + 1], 8 * k) for k in (1, 2, 3)), blocks[:1]).reshape(-1)


def stack(whole):
    half, cut = whole.shape[0] // 2, whole.shape[1] // 2
    return tuple(jnp.concatenate([z[:, :cut], z[:, cut:]], axis=0) for z in (whole[:half], whole[half:]))


def unstack(pieces):
    half = pieces[0].shape[0] // 2
    return jnp.concatenate([jnp.concatenate([z[:half], z[half:]], axis=1) for z in pieces], axis=0)


def repeat(value, count):
    for _ in range(count):
        yield value


def spread_any(block, firsts):
    return repeat(stack(lax.all_gather(block, AXES, axis=0, tiled=True)), 4)


def collect_any(pieces, firsts):
    total = lax.psum_scatter(unstack(pieces), AXES, scatter_dimension=0, tiled=True).astype(WIDE)
    return repeat(total, 5)


def rearrange(whole, order, shards):
    return jnp.take(whole.reshape(shards, -1, whole.shape[1]), order, axis=0, mode="clip").reshape(whole.shape)


def adamw(master, moment_one, moment_two, gradient, step_rate, decay_rate):
    first_new = BETA_ONE * moment_one + (1.0 - BETA_ONE) * gradient
    second_new = BETA_TWO * moment_two + (1.0 - BETA_TWO) * gradient * gradient
    first_hat = first_new / (1.0 - BETA_ONE**STEP)
    second_hat = second_new / (1.0 - BETA_TWO**STEP)
    master_new = master - step_rate * (
        first_hat / (jnp.sqrt(second_hat) + ADAM_EPS) + decay_rate * master
    )
    return (first_new, second_new, master_new)


def local(
    tokens_in, cotangent, segments, tile_sides, valid_slots, owners,
    master_qkv, master_out, master_up, master_down, master_vec,
    first_qkv, first_out, first_up, first_down, first_vec,
    second_qkv, second_out, second_up, second_down, second_vec,
):
    shards = lax.axis_size(AXES)
    near = shards == 32
    unit = D // shards
    per_row = master_vec.shape[0] // unit
    share = master_vec.shape[0]
    ids = jnp.arange(shards, dtype=jnp.int32)
    if near:
        away = owners ^ lax.axis_index(AXES).astype(jnp.int32)
        place = (away >> 3) + 4 * ((away >> 1) & 1) + 8 * ((away >> 2) & 1) + 16 * (away & 1)
        place_down = place
    else:
        place = owners
        place_down = jnp.arange(32, dtype=jnp.int32)
    inverse = jnp.sum(ids[:, None] * (place[:, None] == ids[None, :]), axis=0)
    target = (place[:, None] * unit + jnp.arange(unit, dtype=jnp.int32)[None, :]).reshape(-1)
    order = (target[:, None] == jnp.arange(D, dtype=jnp.int32)[None, :]).astype(LOW)
    gather, scatter = (spread, collect) if near else (spread_any, collect_any)

    vec_block = jnp.pad(master_vec.reshape(unit, per_row), ((0, 0), (0, 128 - per_row)))
    block_one = jnp.concatenate(
        [master_qkv[:, :CUT_ONE], vec_block, master_qkv[:, CUT_ONE:], jnp.zeros_like(vec_block)], axis=1
    )
    wait_one, wait_two, wait_three = {}, {}, {}

    def arrived(waits, stage):
        return waits.get((stage, "got"), ())

    def ready(waits, stage):
        return waits.get((stage, "ready"), ())

    one = gather(block_one.astype(LOW), wait_one)
    two = gather(jnp.concatenate([master_out, master_up], axis=1).astype(LOW), wait_two)
    if near:
        three = spread(master_down.astype(LOW), wait_three)
    else:
        whole = lax.all_gather(master_down.astype(LOW), AXES, axis=0, tiled=True)
        three = repeat(stack(rearrange(whole, owners, shards)), 4)
    next(one)
    next(one)
    wait_two[0, "start"] = arrived(wait_one, 1)
    next(two)
    wait_one[2, "end"] = arrived(wait_two, 0)
    next(one)
    wait_two[1, "start"] = arrived(wait_one, 2)
    one = next(one)

    vec_rows = jnp.concatenate([z[:HALF, CUT_ONE:] for z in one], axis=0)
    vec = nn(order, vec_rows)[:, :per_row].reshape(per_row, D)
    vec = jnp.pad(vec, ((0, 16 - per_row), (0, 0)))
    spans, far = tables(segments[0], tile_sides[0], valid_slots[0])
    slopes = LOG2E * jnp.exp2(-8.0 * (jnp.arange(HEADS, dtype=jnp.int32).astype(WIDE) + 1.0) / HEADS)
    x = tokens_in[0]
    dy = cotangent[0]
    act_one, qkv = project(x, vec, order, one)
    wait_two[1, "end"] = qkv
    next(two)
    wait_three[0, "start"] = arrived(wait_two, 0)
    wait_three[0, "end"] = qkv
    next(three)
    mixed_0, probs_0 = attend(0, qkv, far, spans, slopes, ready(wait_two, 1) + ready(wait_three, 0))
    wait_two[2, "end"] = mixed_0
    next(two)
    wait_three[1, "start"] = arrived(wait_two, 2)
    mixed_1, probs_1 = attend(3, qkv, far, spans, slopes, ready(wait_two, 2) + (mixed_0,))
    wait_three[1, "end"] = mixed_1
    next(three)
    two = next(two)
    mixed, hidden, act_two, gelu, gelu_slope = upward(
        x, (mixed_0, mixed_1), vec, order, two, ready(wait_three, 1)
    )
    wait_three[2, "end"] = mixed
    next(three)
    grad_three = down_grad(place_down, gelu, dy, arrived(wait_three, 2))
    three = next(three)
    if not near:
        back = jnp.sum(ids[:, None] * (owners[:, None] == ids[None, :]), axis=0)
        grad_three = stack(rearrange(unstack(grad_three), back, shards))
    wait_one, wait_two, wait_three = {}, {}, {}
    sum_three = scatter(grad_three, wait_three)
    block_out, dur, sums_up = downward(place_down, vec, gelu, gelu_slope, dy, hidden, three)
    wait_three[0, "end"] = dur
    next(sum_three)
    dh, dh_low, dmixed, sums = hidden_grad(vec, order, dur, dy, hidden, two, ready(wait_three, 0))
    wait_three[1, "end"] = dh_low
    next(sum_three)
    grad_two = two_grad(mixed, act_two, dh_low, dur, ready(wait_three, 1))
    wait_three[2, "end"] = grad_two
    next(sum_three)
    sum_two = scatter(grad_two, wait_two)
    d0 = attend_back(0, qkv, dmixed, probs_0, spans, ready(wait_three, 2) + tuple(grad_two))
    wait_three[3, "end"] = d0[0]
    next(sum_three)
    wait_two[0, "end"] = d0[0]
    next(sum_two)
    d1 = attend_back(3, qkv, dmixed, probs_1, spans, arrived(wait_three, 3) + ready(wait_two, 0) + (d0[0],))
    d = [z for pair in zip(d0, d1) for z in pair]
    grad_one = one_grad(act_one, d)
    wait_two[1, "end"] = grad_one
    next(sum_two)
    sum_one = scatter(grad_one, wait_one)
    next(sum_one)
    dact = input_back(order, d, one, ready(wait_two, 1) + ready(wait_one, 0))
    wait_two[2, "end"] = dact
    next(sum_two)
    tokens_grad, sums_one = input_grad(x, vec, dact, dh, ready(wait_two, 2))
    wait_one[1, "end"] = tokens_grad
    next(sum_one)
    next(sum_one)
    wait_two[3, "end"] = ready(wait_one, 2)
    next(sum_two)
    next(sum_one)
    vector_grad = jnp.concatenate([sums_one[:2], sums[:3], sums_up[:4], sums[3:4]], axis=0)
    blocks = jnp.take(vector_grad.reshape(shards, share), inverse, axis=0, mode="clip")
    if near:
        sum_vec = collect_vec(blocks, (arrived(wait_one, 1), arrived(wait_one, 2)))
    else:
        sum_vec = lax.psum_scatter(blocks.reshape(-1), AXES, scatter_dimension=0, tiled=True)
    sum_one, sum_two, sum_three = [list(z)[-1] for z in (sum_one, sum_two, sum_three)]
    upd_qkv = adamw(master_qkv, first_qkv, second_qkv, sum_one, RATE_MATRIX, DECAY_MATRIX)
    upd_out = adamw(master_out, first_out, second_out, sum_two[:, :D], RATE_MATRIX, DECAY_MATRIX)
    upd_up = adamw(master_up, first_up, second_up, sum_two[:, D:], RATE_MATRIX, DECAY_MATRIX)
    upd_down = adamw(master_down, first_down, second_down, sum_three, RATE_MATRIX, DECAY_MATRIX)
    upd_vec = adamw(master_vec, first_vec, second_vec, sum_vec, RATE_VECTOR, 0.0)
    return (
        (block_out[None], tokens_grad[None]) + upd_qkv + upd_out + upd_up + upd_down + upd_vec
    )


def solution(mesh):
    rows = P(AXES, None)
    flat = P(AXES)
    deep = P(AXES, None, None)
    stored = (rows,) * 4 + (flat,)
    in_specs = (deep,) * 2 + (rows,) * 3 + (P(),) + stored * 3
    out_specs = (deep,) * 2 + (rows,) * 12 + (flat,) * 3
    return jax.shard_map(local, mesh=mesh, in_specs=in_specs, out_specs=out_specs, check_vma=False)
```

time: 282 us -> 296 us (1.050)
  waiting for transfers between devices: 55.2 us -> 80.5 us
  Pallas kernels: 105 us -> 93.2 us
  between operations: 9.84 us -> 17.3 us
  local copies, waits for them, and re-layouts: 21.5 us -> 16.1 us
  other arithmetic: 21.3 us -> 17.4 us
  starting transfers between devices: 64.4 us -> 67.4 us
    pallas_call x4 -> x0, Pallas kernels: 36.1 us -> none  [the longest x2 20.6 us: attend_back(): pl.pallas_call(later(attend_back_kernel, 6, len(after)), grid_spec=pltpu....]
    ppermute x60 -> x55, waiting for transfers between devices: 55.2 us -> 80.5 us  [swap(): return lax.ppermute(value, AXES, pairs)]
    pallas_call x9 -> x31, Pallas kernels: 68.9 us -> 93.2 us  [whole_call(): pl.pallas_call(later(kernel, len(args), len(after)), in_specs=specs + [pl...]
    add x22 -> x3, other arithmetic: 5.5 us -> 0.1 us  [the longest x1 0.09 us: collect(): yield sum((z.astype(WIDE) for z in got), total)]
    ppermute x60 -> x55, starting transfers between devices: 64.4 us -> 67.4 us  [swap(): return lax.ppermute(value, AXES, pairs)]
    unnamed x76 -> x78, local copies, waits for them, and re-layouts: 9.06 us -> 10.6 us
  transfers between devices with their start and end apart: 60 -> 55, of which waited for: 24 -> 23; matrix products, arithmetic and copies ran while one was open for 8% -> 7% of each run, Pallas kernels for 38% -> 25%
where the time goes in v3:
time: 296 us; the launch traced here: 293 us
  Pallas kernels  93.2 us (31%)
  waiting for transfers between devices  80.5 us (27%)
  starting transfers between devices  67.4 us (23%)
  other arithmetic  17.4 us (6%)
  between operations  17.3 us (6%)
  local copies, waits for them, and re-layouts  16.1 us (5%)
    pallas_call x31, Pallas kernels, whole_call(): pl.pallas_call(later(kernel, len(args), len(after)), in_specs=specs + [pl...  93.2 us
    ppermute x55, waiting for transfers between devices, swap(): return lax.ppermute(value, AXES, pairs)  80.5 us
    ppermute x55, starting transfers between devices, swap(): return lax.ppermute(value, AXES, pairs)  67.4 us
    unnamed x78, local copies, waits for them, and re-layouts  10.6 us
  transfers between devices with their start and end apart: 55, of which 23 were waited for; matrix products, arithmetic and copies ran while one was open for 7% of the time, Pallas kernels for 25%

profile of v3, /device:TPU:0, one launch (start us, length us, event | category | flops | bytes accessed | tf_op | source)
XLA Modules:
  0.0 293.1 jit_solution(6370468874185125602)
XLA Ops:
  2.5 3.1 %collective-permute-start = (bf16[24,2560]{1,0:T(8,128)(2,1)S(1)}, bf16[24,2560]{1,0:T(8,128)(2,1)S(1)}, u32[]{:S(2)}, u32[]{:S(2)}) collective-permute-start(bf16[24,2560]{1,0:T(8,128)(2,1)S(1)} %fusion.11.refs_0_), channel_id=1, source_target_pairs={{0,8},{1,9},{2,10},{3,11},{4,12},{5,13},{6,14},{7,15},{8,0},{9,1},... | collective-permute-start | bytes 368648 | tf_op jit(solution)/shard_map/ppermute | solution.py:540
  5.6 2.6 collective-permute-start.1
  13.1 4.8 %collective-permute-done.1.refs_2_ = bf16[24,2560]{1,0:T(8,128)(2,1)S(1)} collective-permute-done((bf16[24,2560]{1,0:T(8,128)(2,1)S(1)}, bf16[24,2560]{1,0:T(8,128)(2,1)S(1)}, u32[]{:S(2)}, u32[]{:S(2)}) %collective-permute-start.1) | collective-permute-done | bytes 122912 | tf_op jit(solution)/shard_map/ppermute | solution.py:540
  17.9 1.6 collective-permute-start.3
  19.5 1.5 collective-permute-start.4
  22.3 1.9 collective-permute-done.3.refs_1_
  24.2 2.4 collective-permute-done.4.refs_3_
  26.6 1.6 collective-permute-start.5
  33.2 2.1 collective-permute-start.8
  35.3 1.6 collective-permute-start.9
  37.5 1.3 collective-permute-done.7.refs_1_
  39.5 7.5 %collective-permute-done.8.refs_2_ = bf16[24,3840]{1,0:T(8,128)(2,1)S(1)} collective-permute-done((bf16[24,3840]{1,0:T(8,128)(2,1)S(1)}, bf16[24,3840]{1,0:T(8,128)(2,1)S(1)}, u32[]{:S(2)}, u32[]{:S(2)}) %collective-permute-start.8) | collective-permute-done | bytes 184352 | tf_op jit(solution)/shard_map/ppermute | solution.py:540
  68.0 1.7 sqrt_select_fusion.refs_3_
  69.9 1.9 collective-permute-start.13
  71.9 1.8 collective-permute-start.14
  73.7 1.4 collective-permute-start.15
  78.7 1.5 collective-permute-start.11
  81.7 1.3 fusion.1
  83.0 1.3 reshape.214
  85.5 6.2 %project.1 = (bf16[576,768]{1,0:T(8,128)(2,1)S(1)}, bf16[576,2304]{1,0:T(8,128)(2,1)S(1)}) custom-call(bf16[576,768]{1,0:T(8,128)(2,1)S(1)} %bitcast.38, f32[16,768]{1,0:T(8,128)S(1)} %pad.15.refs_1_.refs_3_.refs_0_, bf16[768,768]{1,0:T(8,128)(2,1)S(1)} %fusion.refs_2_.refs_4_.refs_1_.refs_0_, bf16[768,1280]{1,0:T(8,128)(2,1)S(1)} %second.3.refs_3_.refs_7_, ...), custom_call_target="tpu_custom_call" | custom-call | flops 2717908992 | bytes 9584640 | tf_op jit(solution)/shard_map/project/pallas_call | solution.py:64
  91.7 1.4 first.4
  93.1 1.6 collective-permute-start.16
  96.4 4.6 %attend.2 = (bf16[576,384]{1,0:T(8,128)(2,1)S(1)}, bf16[4,6,240,256]{3,2,1,0:T(8,128)(2,1)S(1)}) custom-call(s32[5,5]{1,0:T(8,128)S(1)} %concatenate.20.refs_0_, f32[12]{0:T(128)S(1)} %exponential_multiply_fusion.refs_1_, bf16[576,2304]{1,0:T(8,128)(2,1)S(1)} %get-tuple-element.208.refs_2_.refs_1_, f32[4,240,256]{2,1,0:T(8,128)S(1)} %copy-done.4, ...), custom_call_target="tpu_custom_call" | custom-call | flops 8999999488 | bytes 7028884 | tf_op jit(solution)/shard_map/attend/pallas_call | solution.py:64
  101.0 10.0 %collective-permute-done.16.refs_1_ = bf16[192,1920]{1,0:T(8,128)(2,1)S(1)} collective-permute-done((bf16[192,1920]{1,0:T(8,128)(2,1)S(1)}, bf16[192,1920]{1,0:T(8,128)(2,1)S(1)}, u32[]{:S(2)}, u32[]{:S(2)}) %collective-permute-start.16) | collective-permute-done | bytes 737312 | tf_op jit(solution)/shard_map/ppermute | solution.py:540
  111.0 1.2 collective-permute-done.17.refs_3_
  113.7 4.6 %attend.3 = (bf16[576,384]{1,0:T(8,128)(2,1)S(1)}, bf16[4,6,240,256]{3,2,1,0:T(8,128)(2,1)S(1)}) custom-call(s32[5,5]{1,0:T(8,128)S(1)} %concatenate.20.refs_0_, f32[12]{0:T(128)S(1)} %exponential_multiply_fusion.refs_1_, bf16[576,2304]{1,0:T(8,128)(2,1)S(1)} %get-tuple-element.208.refs_2_.refs_1_, f32[4,240,256]{2,1,0:T(8,128)S(1)} %copy-done.4, ...), custom_call_target="tpu_custom_call" | custom-call | flops 8999999488 | bytes 7028884 | tf_op jit(solution)/shard_map/attend/pallas_call | solution.py:64
  118.3 3.7 %collective-permute-done.19.refs_1_ = bf16[384,384]{1,0:T(8,128)(2,1)S(1)} collective-permute-done((bf16[384,384]{1,0:T(8,128)(2,1)S(1)}, bf16[384,384]{1,0:T(8,128)(2,1)S(1)}, u32[]{:S(2)}, u32[]{:S(2)}) %collective-permute-start.19) | collective-permute-done | bytes 294944 | tf_op jit(solution)/shard_map/ppermute | solution.py:540
  122.9 1.5 collective-permute-start.22
  124.4 8.4 %upward.1 = (bf16[576,768]{1,0:T(8,128)(2,1)S(1)}, f32[576,768]{1,0:T(8,128)S(1)}, bf16[576,768]{1,0:T(8,128)(2,1)S(1)}, bf16[576,3072]{1,0:T(8,128)(2,1)S(1)}, bf16[576,3072]{1,0:T(8,128)(2,1)S(1)}) custom-call(bf16[576,768]{1,0:T(8,128)(2,1)S(1)} %bitcast.39, bf16[576,384]{1,0:T(8,128)(2,1)S(1)} %get-tuple-element.228.refs_5_.refs_1_, ...), custom_call_target="tpu_custom_call" | custom-call | flops 9512681472 | bytes 19513344 | tf_op jit(solution)/shard_map/upward/pallas_call | solution.py:64
  132.8 4.2 %collective-permute-done.21.refs_1_.refs_3_ = bf16[768,384]{1,0:T(8,128)(2,1)S(1)} collective-permute-done((bf16[768,384]{1,0:T(8,128)(2,1)S(1)}, bf16[768,384]{1,0:T(8,128)(2,1)S(1)}, u32[]{:S(2)}, u32[]{:S(2)}) %collective-permute-start.21) | collective-permute-done | bytes 589856 | tf_op jit(solution)/shard_map/ppermute | solution.py:540
  138.4 7.8 %down_grad.1 = (bf16[3072,384]{1,0:T(8,128)(2,1)S(1)}, bf16[3072,384]{1,0:T(8,128)(2,1)S(1)}) custom-call(s32[32]{0:T(128)S(1)} %get-tuple-element.377.refs_0_, bf16[576,3072]{1,0:T(8,128)(2,1)S(1)} %get-tuple-element.240.refs_2_.refs_1_, bf16[576,768]{1,0:T(8,128)(2,1)S(1)} %bitcast.35, bf16[768,384]{1,0:T(8,128)(2,1)S(1)} %collective-permute-done.21.refs_1_.refs_3_, ...), custom_call_target="tpu_custom_call" | custom-call | flops 2717908992 | bytes 9142400 | tf_op jit(solution)/shard_map/down_grad/pallas_call | solution.py:64
  146.3 12.6 %downward.1 = (bf16[576,768]{1,0:T(8,128)(2,1)}, bf16[576,3072]{1,0:T(8,128)(2,1)S(1)}, f32[8,768]{1,0:T(8,128)S(1)}) custom-call(s32[32]{0:T(128)S(1)} %get-tuple-element.377.refs_0_, f32[16,768]{1,0:T(8,128)S(1)} %pad.15.refs_1_.refs_3_.refs_0_, bf16[576,3072]{1,0:T(8,128)(2,1)S(1)} %get-tuple-element.240.refs_2_.refs_1_, ...), custom_call_target="tpu_custom_call" | custom-call | flops 5435817984 | bytes 18948224 | tf_op jit(solution)/shard_map/downward/pallas_call | solution.py:64
  159.4 1.6 collective-permute-start.25
  161.0 1.4 collective-permute-start.26
  162.4 8.7 %hidden_grad.1 = (f32[576,768]{1,0:T(8,128)S(1)}, bf16[576,768]{1,0:T(8,128)(2,1)S(1)}, bf16[576,768]{1,0:T(8,128)(2,1)S(1)}, f32[8,768]{1,0:T(8,128)S(1)}) custom-call(f32[16,768]{1,0:T(8,128)S(1)} %pad.15.refs_1_.refs_3_.refs_0_, bf16[768,768]{1,0:T(8,128)(2,1)S(1)} %fusion.refs_2_.refs_4_.refs_1_.refs_0_, ...), custom_call_target="tpu_custom_call" | custom-call | flops 4756340736 | bytes 16883712 | tf_op jit(solution)/shard_map/hidden_grad/pallas_call | solution.py:64
  171.2 4.0 %collective-permute-done.25.refs_1_ = bf16[768,384]{1,0:T(8,128)(2,1)S(1)} collective-permute-done((bf16[768,384]{1,0:T(8,128)(2,1)S(1)}, bf16[768,384]{1,0:T(8,128)(2,1)S(1)}, u32[]{:S(2)}, u32[]{:S(2)}) %collective-permute-start.25) | collective-permute-done | bytes 589856 | tf_op jit(solution)/shard_map/ppermute | solution.py:540
  175.2 1.2 collective-permute-done.26.refs_3_
  176.7 5.8 %two_grad.1 = (bf16[768,1920]{1,0:T(8,128)(2,1)S(1)}, bf16[768,1920]{1,0:T(8,128)(2,1)S(1)}) custom-call(bf16[576,768]{1,0:T(8,128)(2,1)S(1)} %get-tuple-element.245.refs_0_, bf16[576,768]{1,0:T(8,128)(2,1)S(1)} %get-tuple-element.269.refs_1_, bf16[576,768]{1,0:T(8,128)(2,1)S(1)} %get-tuple-element.261.refs_2_, ...), custom_call_target="tpu_custom_call" | custom-call | flops 3397386240 | bytes 12091392 | tf_op jit(solution)/shard_map/two_grad/pallas_call | solution.py:64
  182.6 1.5 collective-permute-start.27
  184.6 7.4 %collective-permute-done.27.refs_1_ = bf16[384,384]{1,0:T(8,128)(2,1)S(1)} collective-permute-done((bf16[384,384]{1,0:T(8,128)(2,1)S(1)}, bf16[384,384]{1,0:T(8,128)(2,1)S(1)}, u32[]{:S(2)}, u32[]{:S(2)}) %collective-permute-start.27) | collective-permute-done | bytes 294944 | tf_op jit(solution)/shard_map/ppermute | solution.py:540
  193.9 2.5 collective-permute-start.30
  196.3 1.4 collective-permute-start.31
  197.7 6.3 %attend_back.2 = (bf16[576,384]{1,0:T(8,128)(2,1)S(1)}, bf16[576,384]{1,0:T(8,128)(2,1)S(1)}, bf16[576,384]{1,0:T(8,128)(2,1)S(1)}) custom-call(s32[5,5]{1,0:T(8,128)S(1)} %concatenate.20.refs_0_, bf16[576,2304]{1,0:T(8,128)(2,1)S(1)} %get-tuple-element.208.refs_2_.refs_1_, bf16[576,768]{1,0:T(8,128)(2,1)S(1)} %get-tuple-element.257.refs_2_, ...), custom_call_target="tpu_custom_call" | custom-call | flops 12000000000 | bytes 7815268 | tf_op jit(solution)/shard_map/attend_back/pallas_call | solution.py:64
  204.7 2.9 collective-permute-done.30.refs_5_
  207.5 6.5 %attend_back.3 = (bf16[576,384]{1,0:T(8,128)(2,1)S(1)}, bf16[576,384]{1,0:T(8,128)(2,1)S(1)}, bf16[576,384]{1,0:T(8,128)(2,1)S(1)}) custom-call(s32[5,5]{1,0:T(8,128)S(1)} %concatenate.20.refs_0_, bf16[576,2304]{1,0:T(8,128)(2,1)S(1)} %get-tuple-element.208.refs_2_.refs_1_, bf16[576,768]{1,0:T(8,128)(2,1)S(1)} %get-tuple-element.257.refs_2_, ...), custom_call_target="tpu_custom_call" | custom-call | flops 12000000000 | bytes 7815268 | tf_op jit(solution)/shard_map/attend_back/pallas_call | solution.py:64
  214.1 3.6 %one_grad.1 = (bf16[768,1152]{1,0:T(8,128)(2,1)S(1)}, bf16[768,1152]{1,0:T(8,128)(2,1)S(1)}) custom-call(bf16[576,768]{1,0:T(8,128)(2,1)S(1)} %get-tuple-element.296.refs_0_, bf16[576,384]{1,0:T(8,128)(2,1)S(1)} %get-tuple-element.279.refs_11_.refs_1_, bf16[576,384]{1,0:T(8,128)(2,1)S(1)} %get-tuple-element.289.refs_2_, ...), custom_call_target="tpu_custom_call" | custom-call | flops 2038431744 | bytes 7077888 | tf_op jit(solution)/shard_map/one_grad/pallas_call | solution.py:64
  218.9 17.7 %collective-permute-done.33.refs_1_ = bf16[192,1920]{1,0:T(8,128)(2,1)S(1)} collective-permute-done((bf16[192,1920]{1,0:T(8,128)(2,1)S(1)}, bf16[192,1920]{1,0:T(8,128)(2,1)S(1)}, u32[]{:S(2)}, u32[]{:S(2)}) %collective-permute-start.33) | collective-permute-done | bytes 737312 | tf_op jit(solution)/shard_map/ppermute | solution.py:540
  237.9 1.5 collective-permute-start.37
  241.1 1.2 collective-permute-start.39
  242.3 5.9 %input_back.1.refs_2_ = f32[576,768]{1,0:T(8,128)S(1)} custom-call(bf16[768,768]{1,0:T(8,128)(2,1)S(1)} %fusion.refs_2_.refs_4_.refs_1_.refs_0_, bf16[576,384]{1,0:T(8,128)(2,1)S(1)} %get-tuple-element.279.refs_11_.refs_1_, bf16[576,384]{1,0:T(8,128)(2,1)S(1)} %get-tuple-element.289.refs_2_, bf16[576,384]{1,0:T(8,128)(2,1)S(1)} %get-tuple-element.290.refs_3_, ...), custom_call_target="tpu_custom_call" | custom-call | flops 2717908992 | bytes 9535488 | tf_op jit(solution)/shard_map/input_back/pallas_call | solution.py:64
  250.2 2.9 input_grad.1
  254.0 3.3 %collective-permute-start.45 = (bf16[24,3840]{1,0:T(8,128)(2,1)}, bf16[24,3840]{1,0:T(8,128)(2,1)S(1)}, u32[]{:S(2)}, u32[]{:S(2)}) collective-permute-start(bf16[24,3840]{1,0:T(8,128)(2,1)} %get-tuple-element.341.refs_5_), channel_id=1, source_target_pairs={{0,8},{1,9},{2,10},{3,11},{4,12},{5,13},{6,14},{7,15},{8,0},{9,1},... | collective-permute-start | bytes 552968 | tf_op jit(solution)/shard_map/ppermute | solution.py:540
  257.3 1.5 collective-permute-start.46
  258.7 2.3 collective-permute-start.47
  261.0 1.3 half_sum.5
  263.2 1.4 collective-permute-start.41
  264.6 1.8 collective-permute-done.45
  266.4 1.8 collective-permute-start.49
  268.7 1.3 collective-permute-start.50
  270.2 1.8 collective-permute-start.51
  272.0 2.2 multiply_subtract_fusion
  275.3 3.6 %collective-permute-start.43 = (bf16[24,2304]{1,0:T(8,128)(2,1)S(1)}, bf16[24,2304]{1,0:T(8,128)(2,1)S(1)}, u32[]{:S(2)}, u32[]{:S(2)}) collective-permute-start(bf16[24,2304]{1,0:T(8,128)(2,1)S(1)} %get-tuple-element.336), channel_id=1, source_target_pairs={{0,16},{1,17},{2,18},{3,19},{4,20},{5,21},{6,22},{7,23},{8,24},{9,... | collective-permute-start | bytes 331784 | tf_op jit(solution)/shard_map/ppermute | solution.py:540
  280.0 3.4 %collective-permute-start.52 = (f32[1,240]{1,0:T(1,128)S(1)}, f32[1,240]{1,0:T(1,128)S(1)}, u32[]{:S(2)}, u32[]{:S(2)}) collective-permute-start(f32[1,240]{1,0:T(1,128)S(1)} %get-tuple-element.397), channel_id=1, source_target_pairs={{0,8},{1,9},{2,10},{3,11},{4,12},{5,13},{6,14},{7,15},{8,0},{9,1},... | collective-permute-start | bytes 2888 | tf_op jit(solution)/shard_map/ppermute | solution.py:540
  287.0 4.9 %collective-permute-done.44 = bf16[24,2304]{1,0:T(8,128)(2,1)S(1)} collective-permute-done((bf16[24,2304]{1,0:T(8,128)(2,1)S(1)}, bf16[24,2304]{1,0:T(8,128)(2,1)S(1)}, u32[]{:S(2)}, u32[]{:S(2)}) %collective-permute-start.44) | collective-permute-done | bytes 110624 | tf_op jit(solution)/shard_map/ppermute | solution.py:540
  (229 shorter events, 50.7 us)
Async XLA Ops:
  0.7 29.2 %copy-start.35 = (s32[1,576]{1,0:T(1,128)S(1)}, s32[1,576]{1,0:T(1,128)}, u32[]{:S(2)}) copy-start(s32[1,576]{1,0:T(1,128)} %param.25) | copy-start | bytes 6916
  2.5 10.6 %collective-permute-start = (bf16[24,2560]{1,0:T(8,128)(2,1)S(1)}, bf16[24,2560]{1,0:T(8,128)(2,1)S(1)}, u32[]{:S(2)}, u32[]{:S(2)}) collective-permute-start(bf16[24,2560]{1,0:T(8,128)(2,1)S(1)} %fusion.11.refs_0_), channel_id=1, source_target_pairs={{0,8},{1,9},{2,10},{3,11},{4,12},{5,13},{6,14},{7,15},{8,0},{9,1},... | collective-permute-start | bytes 368648 | tf_op jit(solution)/shard_map/ppermute | solution.py:540
  5.6 12.3 %collective-permute-start.1 = (bf16[24,2560]{1,0:T(8,128)(2,1)S(1)}, bf16[24,2560]{1,0:T(8,128)(2,1)S(1)}, u32[]{:S(2)}, u32[]{:S(2)}) collective-permute-start(bf16[24,2560]{1,0:T(8,128)(2,1)S(1)} %fusion.11.refs_0_), channel_id=1, source_target_pairs={{0,16},{1,17},{2,18},{3,19},{4,20},{5,21},{6,22},{7,23},{8,24},{9,... | collective-permute-start | bytes 368648 | tf_op jit(solution)/shard_map/ppermute | solution.py:540
  8.2 9.7 %collective-permute-start.2 = (bf16[24,2560]{1,0:T(8,128)(2,1)S(1)}, bf16[24,2560]{1,0:T(8,128)(2,1)S(1)}, u32[]{:S(2)}, u32[]{:S(2)}) collective-permute-start(bf16[24,2560]{1,0:T(8,128)(2,1)S(1)} %fusion.11.refs_0_), channel_id=1, source_target_pairs={{0,24},{1,25},{2,26},{3,27},{4,28},{5,29},{6,30},{7,31},{8,16},{9,... | collective-permute-start | bytes 368648 | tf_op jit(solution)/shard_map/ppermute | solution.py:540
  17.9 6.3 %collective-permute-start.3 = (bf16[96,1280]{1,0:T(8,128)(2,1)S(1)}, bf16[96,1280]{1,0:T(8,128)(2,1)S(1)}, u32[]{:S(2)}, u32[]{:S(2)}) collective-permute-start(bf16[96,1280]{1,0:T(8,128)(2,1)S(1)} %get-tuple-element.193.refs_0_), channel_id=1, source_target_pairs={{0,2},{1,3},{2,0},{3,1},{4,6},{5,7},{6,4},{7,5},{8,10},{9,11},{10,... | collective-permute-start | bytes 737288 | tf_op jit(solution)/shard_map/ppermute | solution.py:540
  19.5 7.1 %collective-permute-start.4 = (bf16[96,1280]{1,0:T(8,128)(2,1)S(1)}, bf16[96,1280]{1,0:T(8,128)(2,1)S(1)}, u32[]{:S(2)}, u32[]{:S(2)}) collective-permute-start(bf16[96,1280]{1,0:T(8,128)(2,1)S(1)} %get-tuple-element.195), channel_id=1, source_target_pairs={{0,4},{1,5},{2,6},{3,7},{4,0},{5,1},{6,2},{7,3},{8,12},{9,13},{10,... | collective-permute-start | bytes 737288 | tf_op jit(solution)/shard_map/ppermute | solution.py:540
  26.6 21.7 %collective-permute-start.5 = (bf16[192,1280]{1,0:T(8,128)(2,1)S(1)}, bf16[192,1280]{1,0:T(8,128)(2,1)S(1)}, u32[]{:S(2)}, u32[]{:S(2)}) collective-permute-start(bf16[192,1280]{1,0:T(8,128)(2,1)S(1)} %get-tuple-element.199.refs_0_), channel_id=1, source_target_pairs={{0,4},{1,5},{2,6},{3,7},{4,0},{5,1},{6,2},{7,3},{8,12},{9,13},{10,... | collective-permute-start | bytes 1474568 | tf_op jit(solution)/shard_map/ppermute | solution.py:540
  28.2 20.9 %collective-permute-start.6 = (bf16[192,1280]{1,0:T(8,128)(2,1)S(1)}, bf16[192,1280]{1,0:T(8,128)(2,1)S(1)}, u32[]{:S(2)}, u32[]{:S(2)}) collective-permute-start(bf16[192,1280]{1,0:T(8,128)(2,1)S(1)} %get-tuple-element.201), channel_id=1, source_target_pairs={{0,2},{1,3},{2,0},{3,1},{4,6},{5,7},{6,4},{7,5},{8,10},{9,11},{10,... | collective-permute-start | bytes 1474568 | tf_op jit(solution)/shard_map/ppermute | solution.py:540
  32.5 6.3 %collective-permute-start.7 = (bf16[24,3840]{1,0:T(8,128)(2,1)S(1)}, bf16[24,3840]{1,0:T(8,128)(2,1)S(1)}, u32[]{:S(2)}, u32[]{:S(2)}) collective-permute-start(bf16[24,3840]{1,0:T(8,128)(2,1)S(1)} %pad_maximum_fusion.2.refs_0_), channel_id=1, source_target_pairs={{0,8},{1,9},{2,10},{3,11},{4,12},{5,13},{6,14},{7,15},{8,0},{9,1},... | collective-permute-start | bytes 552968 | tf_op jit(solution)/shard_map/ppermute | solution.py:540
  33.2 13.8 %collective-permute-start.8 = (bf16[24,3840]{1,0:T(8,128)(2,1)S(1)}, bf16[24,3840]{1,0:T(8,128)(2,1)S(1)}, u32[]{:S(2)}, u32[]{:S(2)}) collective-permute-start(bf16[24,3840]{1,0:T(8,128)(2,1)S(1)} %pad_maximum_fusion.2.refs_0_), channel_id=1, source_target_pairs={{0,16},{1,17},{2,18},{3,19},{4,20},{5,21},{6,22},{7,23},{8,24},{9,... | collective-permute-start | bytes 552968 | tf_op jit(solution)/shard_map/ppermute | solution.py:540
  35.3 12.4 %collective-permute-start.9 = (bf16[24,3840]{1,0:T(8,128)(2,1)S(1)}, bf16[24,3840]{1,0:T(8,128)(2,1)S(1)}, u32[]{:S(2)}, u32[]{:S(2)}) collective-permute-start(bf16[24,3840]{1,0:T(8,128)(2,1)S(1)} %pad_maximum_fusion.2.refs_0_), channel_id=1, source_target_pairs={{0,24},{1,25},{2,26},{3,27},{4,28},{5,29},{6,30},{7,31},{8,16},{9,... | collective-permute-start | bytes 552968 | tf_op jit(solution)/shard_map/ppermute | solution.py:540
  52.1 28.2 %collective-permute-start.10 = (bf16[768,1280]{1,0:T(8,128)(2,1)S(1)}, bf16[768,1280]{1,0:T(8,128)(2,1)}, u32[]{:S(2)}, u32[]{:S(2)}) collective-permute-start(bf16[768,1280]{1,0:T(8,128)(2,1)S(1)} %second.3.refs_3_.refs_7_), channel_id=1, source_target_pairs={{0,1},{1,0},{2,3},{3,2},{4,5},{5,4},{6,7},{7,6},{8,9},{9,8},{10,11... | collective-permute-start | bytes 5898248 | tf_op jit(solution)/shard_map/ppermute | solution.py:540
  69.9 21.8 %collective-permute-start.13 = (bf16[96,768]{1,0:T(8,128)(2,1)S(1)}, bf16[96,768]{1,0:T(8,128)(2,1)}, u32[]{:S(2)}, u32[]{:S(2)}) collective-permute-start(bf16[96,768]{1,0:T(8,128)(2,1)S(1)} %convert_element_type.67.refs_0_), channel_id=1, source_target_pairs={{0,8},{1,9},{2,10},{3,11},{4,12},{5,13},{6,14},{7,15},{8,0},{9,1},... | collective-permute-start | bytes 442376 | tf_op jit(solution)/shard_map/ppermute | solution.py:540
  71.9 19.8 %collective-permute-start.14 = (bf16[96,768]{1,0:T(8,128)(2,1)S(1)}, bf16[96,768]{1,0:T(8,128)(2,1)}, u32[]{:S(2)}, u32[]{:S(2)}) collective-permute-start(bf16[96,768]{1,0:T(8,128)(2,1)S(1)} %convert_element_type.67.refs_0_), channel_id=1, source_target_pairs={{0,16},{1,17},{2,18},{3,19},{4,20},{5,21},{6,22},{7,23},{8,24},{9,... | collective-permute-start | bytes 442376 | tf_op jit(solution)/shard_map/ppermute | solution.py:540
  73.7 18.1 %collective-permute-start.15 = (bf16[96,768]{1,0:T(8,128)(2,1)S(1)}, bf16[96,768]{1,0:T(8,128)(2,1)}, u32[]{:S(2)}, u32[]{:S(2)}) collective-permute-start(bf16[96,768]{1,0:T(8,128)(2,1)S(1)} %convert_element_type.67.refs_0_), channel_id=1, source_target_pairs={{0,24},{1,25},{2,26},{3,27},{4,28},{5,29},{6,30},{7,31},{8,16},{9,... | collective-permute-start | bytes 442376 | tf_op jit(solution)/shard_map/ppermute | solution.py:540
  78.7 12.9 %collective-permute-start.11 = (bf16[96,1920]{1,0:T(8,128)(2,1)}, bf16[96,1920]{1,0:T(8,128)(2,1)}, u32[]{:S(2)}, u32[]{:S(2)}) collective-permute-start(bf16[96,1920]{1,0:T(8,128)(2,1)} %get-tuple-element.214.refs_0_), channel_id=1, source_target_pairs={{0,2},{1,3},{2,0},{3,1},{4,6},{5,7},{6,4},{7,5},{8,10},{9,11},{10,... | collective-permute-start | bytes 1105928 | tf_op jit(solution)/shard_map/ppermute | solution.py:540
  80.3 11.4 %collective-permute-start.12 = (bf16[96,1920]{1,0:T(8,128)(2,1)}, bf16[96,1920]{1,0:T(8,128)(2,1)}, u32[]{:S(2)}, u32[]{:S(2)}) collective-permute-start(bf16[96,1920]{1,0:T(8,128)(2,1)} %get-tuple-element.215.refs_2_), channel_id=1, source_target_pairs={{0,4},{1,5},{2,6},{3,7},{4,0},{5,1},{6,2},{7,3},{8,12},{9,13},{10,... | collective-permute-start | bytes 1105928 | tf_op jit(solution)/shard_map/ppermute | solution.py:540
  93.1 17.8 %collective-permute-start.16 = (bf16[192,1920]{1,0:T(8,128)(2,1)S(1)}, bf16[192,1920]{1,0:T(8,128)(2,1)S(1)}, u32[]{:S(2)}, u32[]{:S(2)}) collective-permute-start(bf16[192,1920]{1,0:T(8,128)(2,1)S(1)} %get-tuple-element.218.refs_4_.refs_0_), channel_id=1, source_target_pairs={{0,4},{1,5},{2,6},{3,7},{4,0},{5,1},{6,2},{7,3},{8,12},{9,13},{10,... | collective-permute-start | bytes 2211848 | tf_op jit(solution)/shard_map/ppermute | solution.py:540
  94.7 17.5 %collective-permute-start.17 = (bf16[192,1920]{1,0:T(8,128)(2,1)S(1)}, bf16[192,1920]{1,0:T(8,128)(2,1)S(1)}, u32[]{:S(2)}, u32[]{:S(2)}) collective-permute-start(bf16[192,1920]{1,0:T(8,128)(2,1)S(1)} %get-tuple-element.219.refs_5_.refs_2_), channel_id=1, source_target_pairs={{0,2},{1,3},{2,0},{3,1},{4,6},{5,7},{6,4},{7,5},{8,10},{9,11},{10,... | collective-permute-start | bytes 2211848 | tf_op jit(solution)/shard_map/ppermute | solution.py:540
  112.5 11.9 %collective-permute-start.18 = (bf16[768,1920]{1,0:T(8,128)(2,1)S(1)}, bf16[768,1920]{1,0:T(8,128)(2,1)S(1)}, u32[]{:S(2)}, u32[]{:S(2)}) collective-permute-start(bf16[768,1920]{1,0:T(8,128)(2,1)S(1)} %second.4.refs_4_.refs_5_), channel_id=1, source_target_pairs={{0,1},{1,0},{2,3},{3,2},{4,5},{5,4},{6,7},{7,6},{8,9},{9,8},{10,11... | collective-permute-start | bytes 8847368 | tf_op jit(solution)/shard_map/ppermute | solution.py:540
  112.5 9.4 %collective-permute-start.19 = (bf16[384,384]{1,0:T(8,128)(2,1)S(1)}, bf16[384,384]{1,0:T(8,128)(2,1)S(1)}, u32[]{:S(2)}, u32[]{:S(2)}) collective-permute-start(bf16[384,384]{1,0:T(8,128)(2,1)S(1)} %get-tuple-element.234.refs_6_.refs_0_), channel_id=1, source_target_pairs={{0,2},{1,3},{2,0},{3,1},{4,6},{5,7},{6,4},{7,5},{8,10},{9,11},{10,... | collective-permute-start | bytes 884744 | tf_op jit(solution)/shard_map/ppermute | solution.py:540
  113.2 9.1 %collective-permute-start.20 = (bf16[384,384]{1,0:T(8,128)(2,1)S(1)}, bf16[384,384]{1,0:T(8,128)(2,1)S(1)}, u32[]{:S(2)}, u32[]{:S(2)}) collective-permute-start(bf16[384,384]{1,0:T(8,128)(2,1)S(1)} %get-tuple-element.235.refs_7_.refs_2_), channel_id=1, source_target_pairs={{0,4},{1,5},{2,6},{3,7},{4,0},{5,1},{6,2},{7,3},{8,12},{9,13},{10,... | collective-permute-start | bytes 884744 | tf_op jit(solution)/shard_map/ppermute | solution.py:540
  122.3 14.7 %collective-permute-start.21 = (bf16[768,384]{1,0:T(8,128)(2,1)S(1)}, bf16[768,384]{1,0:T(8,128)(2,1)S(1)}, u32[]{:S(2)}, u32[]{:S(2)}) collective-permute-start(bf16[768,384]{1,0:T(8,128)(2,1)S(1)} %get-tuple-element.238.refs_7_.refs_0_), channel_id=1, source_target_pairs={{0,4},{1,5},{2,6},{3,7},{4,0},{5,1},{6,2},{7,3},{8,12},{9,13},{10,... | collective-permute-start | bytes 1769480 | tf_op jit(solution)/shard_map/ppermute | solution.py:540
  122.9 14.3 %collective-permute-start.22 = (bf16[768,384]{1,0:T(8,128)(2,1)S(1)}, bf16[768,384]{1,0:T(8,128)(2,1)S(1)}, u32[]{:S(2)}, u32[]{:S(2)}) collective-permute-start(bf16[768,384]{1,0:T(8,128)(2,1)S(1)} %get-tuple-element.239.refs_8_.refs_2_), channel_id=1, source_target_pairs={{0,2},{1,3},{2,0},{3,1},{4,6},{5,7},{6,4},{7,5},{8,10},{9,11},{10,... | collective-permute-start | bytes 1769480 | tf_op jit(solution)/shard_map/ppermute | solution.py:540
  137.5 8.8 %collective-permute-start.23 = (bf16[3072,384]{1,0:T(8,128)(2,1)S(1)}, bf16[3072,384]{1,0:T(8,128)(2,1)S(1)}, u32[]{:S(2)}, u32[]{:S(2)}) collective-permute-start(bf16[3072,384]{1,0:T(8,128)(2,1)S(1)} %second.5.refs_6_), channel_id=1, source_target_pairs={{0,1},{1,0},{2,3},{3,2},{4,5},{5,4},{6,7},{7,6},{8,9},{9,8},{10,11... | collective-permute-start | bytes 7077896 | tf_op jit(solution)/shard_map/ppermute | solution.py:540
  146.2 12.7 %collective-permute-start.24 = (bf16[3072,384]{1,0:T(8,128)(2,1)S(1)}, bf16[3072,384]{1,0:T(8,128)(2,1)S(1)}, u32[]{:S(2)}, u32[]{:S(2)}) collective-permute-start(bf16[3072,384]{1,0:T(8,128)(2,1)S(1)} %get-tuple-element.251), channel_id=1, source_target_pairs={{0,1},{1,0},{2,3},{3,2},{4,5},{5,4},{6,7},{7,6},{8,9},{9,8},{10,11... | collective-permute-start | bytes 7077896 | tf_op jit(solution)/shard_map/ppermute | solution.py:540
  159.4 15.8 %collective-permute-start.25 = (bf16[768,384]{1,0:T(8,128)(2,1)S(1)}, bf16[768,384]{1,0:T(8,128)(2,1)S(1)}, u32[]{:S(2)}, u32[]{:S(2)}) collective-permute-start(bf16[768,384]{1,0:T(8,128)(2,1)S(1)} %get-tuple-element.259.refs_9_), channel_id=1, source_target_pairs={{0,4},{1,5},{2,6},{3,7},{4,0},{5,1},{6,2},{7,3},{8,12},{9,13},{10,... | collective-permute-start | bytes 1769480 | tf_op jit(solution)/shard_map/ppermute | solution.py:540
  161.0 15.4 %collective-permute-start.26 = (bf16[768,384]{1,0:T(8,128)(2,1)S(1)}, bf16[768,384]{1,0:T(8,128)(2,1)S(1)}, u32[]{:S(2)}, u32[]{:S(2)}) collective-permute-start(bf16[768,384]{1,0:T(8,128)(2,1)S(1)} %get-tuple-element.260.refs_10_), channel_id=1, source_target_pairs={{0,2},{1,3},{2,0},{3,1},{4,6},{5,7},{6,4},{7,5},{8,10},{9,11},{10,... | collective-permute-start | bytes 1769480 | tf_op jit(solution)/shard_map/ppermute | solution.py:540
  176.7 21.0 %copy-start.25 = (bf16[4,6,240,256]{3,2,1,0:T(8,128)(2,1)S(1)}, bf16[4,6,240,256]{3,2,1,0:T(8,128)(2,1)}, u32[]{:S(2)}) copy-start(bf16[4,6,240,256]{3,2,1,0:T(8,128)(2,1)} %copy-done.24) | copy-start | bytes 8847364
  182.5 21.5 %collective-permute-start.32 = (bf16[768,1920]{1,0:T(8,128)(2,1)S(1)}, bf16[768,1920]{1,0:T(8,128)(2,1)S(1)}, u32[]{:S(2)}, u32[]{:S(2)}) collective-permute-start(bf16[768,1920]{1,0:T(8,128)(2,1)S(1)} %get-tuple-element.272.refs_9_), channel_id=1, source_target_pairs={{0,1},{1,0},{2,3},{3,2},{4,5},{5,4},{6,7},{7,6},{8,9},{9,8},{10,11... | collective-permute-start | bytes 8847368 | tf_op jit(solution)/shard_map/ppermute | solution.py:540
  182.6 9.4 %collective-permute-start.27 = (bf16[384,384]{1,0:T(8,128)(2,1)S(1)}, bf16[384,384]{1,0:T(8,128)(2,1)S(1)}, u32[]{:S(2)}, u32[]{:S(2)}) collective-permute-start(bf16[384,384]{1,0:T(8,128)(2,1)S(1)} %get-tuple-element.267.refs_6_), channel_id=1, source_target_pairs={{0,2},{1,3},{2,0},{3,1},{4,6},{5,7},{6,4},{7,5},{8,10},{9,11},{10,... | collective-permute-start | bytes 884744 | tf_op jit(solution)/shard_map/ppermute | solution.py:540
  184.1 9.1 %collective-permute-start.28 = (bf16[384,384]{1,0:T(8,128)(2,1)S(1)}, bf16[384,384]{1,0:T(8,128)(2,1)S(1)}, u32[]{:S(2)}, u32[]{:S(2)}) collective-permute-start(bf16[384,384]{1,0:T(8,128)(2,1)S(1)} %get-tuple-element.268.refs_7_), channel_id=1, source_target_pairs={{0,4},{1,5},{2,6},{3,7},{4,0},{5,1},{6,2},{7,3},{8,12},{9,13},{10,... | collective-permute-start | bytes 884744 | tf_op jit(solution)/shard_map/ppermute | solution.py:540
  193.2 11.4 %collective-permute-start.29 = (bf16[96,768]{1,0:T(8,128)(2,1)S(1)}, bf16[96,768]{1,0:T(8,128)(2,1)S(1)}, u32[]{:S(2)}, u32[]{:S(2)}) collective-permute-start(bf16[96,768]{1,0:T(8,128)(2,1)S(1)} %get-tuple-element.281.refs_5_), channel_id=1, source_target_pairs={{0,8},{1,9},{2,10},{3,11},{4,12},{5,13},{6,14},{7,15},{8,0},{9,1},... | collective-permute-start | bytes 442376 | tf_op jit(solution)/shard_map/ppermute | solution.py:540
  193.9 13.7 %collective-permute-start.30 = (bf16[96,768]{1,0:T(8,128)(2,1)S(1)}, bf16[96,768]{1,0:T(8,128)(2,1)S(1)}, u32[]{:S(2)}, u32[]{:S(2)}) collective-permute-start(bf16[96,768]{1,0:T(8,128)(2,1)S(1)} %get-tuple-element.282.refs_6_), channel_id=1, source_target_pairs={{0,16},{1,17},{2,18},{3,19},{4,20},{5,21},{6,22},{7,23},{8,24},{9,... | collective-permute-start | bytes 442376 | tf_op jit(solution)/shard_map/ppermute | solution.py:540
  196.3 11.2 %collective-permute-start.31 = (bf16[96,768]{1,0:T(8,128)(2,1)S(1)}, bf16[96,768]{1,0:T(8,128)(2,1)S(1)}, u32[]{:S(2)}, u32[]{:S(2)}) collective-permute-start(bf16[96,768]{1,0:T(8,128)(2,1)S(1)} %get-tuple-element.283.refs_7_), channel_id=1, source_target_pairs={{0,24},{1,25},{2,26},{3,27},{4,28},{5,29},{6,30},{7,31},{8,16},{9,... | collective-permute-start | bytes 442376 | tf_op jit(solution)/shard_map/ppermute | solution.py:540
  217.7 21.9 %collective-permute-start.35 = (bf16[768,1152]{1,0:T(8,128)(2,1)S(1)}, bf16[768,1152]{1,0:T(8,128)(2,1)S(1)}, u32[]{:S(2)}, u32[]{:S(2)}) collective-permute-start(bf16[768,1152]{1,0:T(8,128)(2,1)S(1)} %get-tuple-element.298), channel_id=1, source_target_pairs={{0,1},{1,0},{2,3},{3,2},{4,5},{5,4},{6,7},{7,6},{8,9},{9,8},{10,11... | collective-permute-start | bytes 5308424 | tf_op jit(solution)/shard_map/ppermute | solution.py:540
  217.7 18.9 %collective-permute-start.33 = (bf16[192,1920]{1,0:T(8,128)(2,1)S(1)}, bf16[192,1920]{1,0:T(8,128)(2,1)S(1)}, u32[]{:S(2)}, u32[]{:S(2)}) collective-permute-start(bf16[192,1920]{1,0:T(8,128)(2,1)S(1)} %get-tuple-element.294.refs_9_), channel_id=1, source_target_pairs={{0,4},{1,5},{2,6},{3,7},{4,0},{5,1},{6,2},{7,3},{8,12},{9,13},{10,... | collective-permute-start | bytes 2211848 | tf_op jit(solution)/shard_map/ppermute | solution.py:540
  217.8 18.8 %collective-permute-start.34 = (bf16[192,1920]{1,0:T(8,128)(2,1)S(1)}, bf16[192,1920]{1,0:T(8,128)(2,1)S(1)}, u32[]{:S(2)}, u32[]{:S(2)}) collective-permute-start(bf16[192,1920]{1,0:T(8,128)(2,1)S(1)} %get-tuple-element.295.refs_10_), channel_id=1, source_target_pairs={{0,2},{1,3},{2,0},{3,1},{4,6},{5,7},{6,4},{7,5},{8,10},{9,11},{10,... | collective-permute-start | bytes 2211848 | tf_op jit(solution)/shard_map/ppermute | solution.py:540
  237.0 11.6 %collective-permute-start.36 = (bf16[96,1920]{1,0:T(8,128)(2,1)S(1)}, bf16[96,1920]{1,0:T(8,128)(2,1)S(1)}, u32[]{:S(2)}, u32[]{:S(2)}) collective-permute-start(bf16[96,1920]{1,0:T(8,128)(2,1)S(1)} %get-tuple-element.310.refs_11_), channel_id=1, source_target_pairs={{0,2},{1,3},{2,0},{3,1},{4,6},{5,7},{6,4},{7,5},{8,10},{9,11},{10,... | collective-permute-start | bytes 1105928 | tf_op jit(solution)/shard_map/ppermute | solution.py:540
  237.9 11.5 %collective-permute-start.37 = (bf16[96,1920]{1,0:T(8,128)(2,1)S(1)}, bf16[96,1920]{1,0:T(8,128)(2,1)S(1)}, u32[]{:S(2)}, u32[]{:S(2)}) collective-permute-start(bf16[96,1920]{1,0:T(8,128)(2,1)S(1)} %get-tuple-element.311.refs_12_), channel_id=1, source_target_pairs={{0,4},{1,5},{2,6},{3,7},{4,0},{5,1},{6,2},{7,3},{8,12},{9,13},{10,... | collective-permute-start | bytes 1105928 | tf_op jit(solution)/shard_map/ppermute | solution.py:540
  240.6 18.1 %collective-permute-start.38 = (bf16[192,1152]{1,0:T(8,128)(2,1)}, bf16[192,1152]{1,0:T(8,128)(2,1)}, u32[]{:S(2)}, u32[]{:S(2)}) collective-permute-start(bf16[192,1152]{1,0:T(8,128)(2,1)} %get-tuple-element.319.refs_15_), channel_id=1, source_target_pairs={{0,4},{1,5},{2,6},{3,7},{4,0},{5,1},{6,2},{7,3},{8,12},{9,13},{10,... | collective-permute-start | bytes 1327112 | tf_op jit(solution)/shard_map/ppermute | solution.py:540
  241.1 19.9 %collective-permute-start.39 = (bf16[192,1152]{1,0:T(8,128)(2,1)}, bf16[192,1152]{1,0:T(8,128)(2,1)}, u32[]{:S(2)}, u32[]{:S(2)}) collective-permute-start(bf16[192,1152]{1,0:T(8,128)(2,1)} %get-tuple-element.320.refs_16_), channel_id=1, source_target_pairs={{0,2},{1,3},{2,0},{3,1},{4,6},{5,7},{6,4},{7,5},{8,10},{9,11},{10,... | collective-permute-start | bytes 1327112 | tf_op jit(solution)/shard_map/ppermute | solution.py:540
  253.2 18.8 %copy-start.16 = (bf16[96,768]{1,0:T(8,128)(2,1)S(1)}, bf16[96,768]{1,0:T(8,128)(2,1)}, u32[]{:S(2)}) copy-start(bf16[96,768]{1,0:T(8,128)(2,1)} %copy-done.15) | copy-start | bytes 442372
  253.2 18.8 %copy-start.18 = (bf16[96,768]{1,0:T(8,128)(2,1)S(1)}, bf16[96,768]{1,0:T(8,128)(2,1)}, u32[]{:S(2)}) copy-start(bf16[96,768]{1,0:T(8,128)(2,1)} %copy-done.17) | copy-start | bytes 442372
  253.2 18.8 %copy-start.20 = (bf16[96,768]{1,0:T(8,128)(2,1)S(1)}, bf16[96,768]{1,0:T(8,128)(2,1)}, u32[]{:S(2)}) copy-start(bf16[96,768]{1,0:T(8,128)(2,1)} %copy-done.19) | copy-start | bytes 442372
  253.9 9.3 %collective-permute-start.48 = (f32[16,240]{1,0:T(8,128)S(1)}, f32[16,240]{1,0:T(8,128)S(1)}, u32[]{:S(2)}, u32[]{:S(2)}) collective-permute-start(f32[16,240]{1,0:T(8,128)S(1)} %slice.158), channel_id=1, source_target_pairs={{0,1},{1,0},{2,3},{3,2},{4,5},{5,4},{6,7},{7,6},{8,9},{9,8},{10,11... | collective-permute-start | bytes 46088 | tf_op jit(solution)/shard_map/ppermute | solution.py:540
  254.0 12.4 %collective-permute-start.45 = (bf16[24,3840]{1,0:T(8,128)(2,1)}, bf16[24,3840]{1,0:T(8,128)(2,1)S(1)}, u32[]{:S(2)}, u32[]{:S(2)}) collective-permute-start(bf16[24,3840]{1,0:T(8,128)(2,1)} %get-tuple-element.341.refs_5_), channel_id=1, source_target_pairs={{0,8},{1,9},{2,10},{3,11},{4,12},{5,13},{6,14},{7,15},{8,0},{9,1},... | collective-permute-start | bytes 552968 | tf_op jit(solution)/shard_map/ppermute | solution.py:540
  257.3 17.1 %collective-permute-start.46 = (bf16[24,3840]{1,0:T(8,128)(2,1)}, bf16[24,3840]{1,0:T(8,128)(2,1)S(1)}, u32[]{:S(2)}, u32[]{:S(2)}) collective-permute-start(bf16[24,3840]{1,0:T(8,128)(2,1)} %get-tuple-element.342.refs_6_), channel_id=1, source_target_pairs={{0,16},{1,17},{2,18},{3,19},{4,20},{5,21},{6,22},{7,23},{8,24},{9,... | collective-permute-start | bytes 552968 | tf_op jit(solution)/shard_map/ppermute | solution.py:540
  258.7 16.6 %collective-permute-start.47 = (bf16[24,3840]{1,0:T(8,128)(2,1)S(1)}, bf16[24,3840]{1,0:T(8,128)(2,1)S(1)}, u32[]{:S(2)}, u32[]{:S(2)}) collective-permute-start(bf16[24,3840]{1,0:T(8,128)(2,1)S(1)} %get-tuple-element.343.refs_7_), channel_id=1, source_target_pairs={{0,24},{1,25},{2,26},{3,27},{4,28},{5,29},{6,30},{7,31},{8,16},{9,... | collective-permute-start | bytes 552968 | tf_op jit(solution)/shard_map/ppermute | solution.py:540
  262.3 6.4 %collective-permute-start.40 = (bf16[96,1152]{1,0:T(8,128)(2,1)S(1)}, bf16[96,1152]{1,0:T(8,128)(2,1)S(1)}, u32[]{:S(2)}, u32[]{:S(2)}) collective-permute-start(bf16[96,1152]{1,0:T(8,128)(2,1)S(1)} %get-tuple-element.326), channel_id=1, source_target_pairs={{0,2},{1,3},{2,0},{3,1},{4,6},{5,7},{6,4},{7,5},{8,10},{9,11},{10,... | collective-permute-start | bytes 663560 | tf_op jit(solution)/shard_map/ppermute | solution.py:540
  263.2 6.9 %collective-permute-start.41 = (bf16[96,1152]{1,0:T(8,128)(2,1)S(1)}, bf16[96,1152]{1,0:T(8,128)(2,1)S(1)}, u32[]{:S(2)}, u32[]{:S(2)}) collective-permute-start(bf16[96,1152]{1,0:T(8,128)(2,1)S(1)} %get-tuple-element.327), channel_id=1, source_target_pairs={{0,4},{1,5},{2,6},{3,7},{4,0},{5,1},{6,2},{7,3},{8,12},{9,13},{10,... | collective-permute-start | bytes 663560 | tf_op jit(solution)/shard_map/ppermute | solution.py:540
  266.4 12.5 %collective-permute-start.49 = (f32[4,240]{1,0:T(4,128)S(1)}, f32[4,240]{1,0:T(4,128)S(1)}, u32[]{:S(2)}, u32[]{:S(2)}) collective-permute-start(f32[4,240]{1,0:T(4,128)S(1)} %get-tuple-element.382), channel_id=1, source_target_pairs={{0,2},{1,3},{2,0},{3,1},{4,6},{5,7},{6,4},{7,5},{8,10},{9,11},{10,... | collective-permute-start | bytes 11528 | tf_op jit(solution)/shard_map/ppermute | solution.py:540
  268.7 10.2 %collective-permute-start.50 = (f32[4,240]{1,0:T(4,128)S(1)}, f32[4,240]{1,0:T(4,128)S(1)}, u32[]{:S(2)}, u32[]{:S(2)}) collective-permute-start(f32[4,240]{1,0:T(4,128)S(1)} %get-tuple-element.381), channel_id=1, source_target_pairs={{0,4},{1,5},{2,6},{3,7},{4,0},{5,1},{6,2},{7,3},{8,12},{9,13},{10,... | collective-permute-start | bytes 11528 | tf_op jit(solution)/shard_map/ppermute | solution.py:540
  270.2 13.4 %copy-start.30 = (f32[24,3072]{1,0:T(8,128)S(1)}, f32[24,3072]{1,0:T(8,128)}, u32[]{:S(2)}) copy-start(f32[24,3072]{1,0:T(8,128)} %param.34) | copy-start | bytes 884740
  270.2 8.8 %collective-permute-start.51 = (f32[4,240]{1,0:T(4,128)S(1)}, f32[4,240]{1,0:T(4,128)S(1)}, u32[]{:S(2)}, u32[]{:S(2)}) collective-permute-start(f32[4,240]{1,0:T(4,128)S(1)} %get-tuple-element.380), channel_id=1, source_target_pairs={{0,6},{1,7},{2,4},{3,5},{4,2},{5,3},{6,0},{7,1},{8,14},{9,15},{10,... | collective-permute-start | bytes 11528 | tf_op jit(solution)/shard_map/ppermute | solution.py:540
  274.3 17.6 %copy-start.27 = (f32[24,2304]{1,0:T(8,128)S(1)}, f32[24,2304]{1,0:T(8,128)}, u32[]{:S(2)}) copy-start(f32[24,2304]{1,0:T(8,128)} %param.27) | copy-start | bytes 663556
  274.3 17.6 %copy-start.31 = (f32[24,2304]{1,0:T(8,128)S(1)}, f32[24,2304]{1,0:T(8,128)}, u32[]{:S(2)}) copy-start(f32[24,2304]{1,0:T(8,128)} %param.37) | copy-start | bytes 663556
  274.3 17.6 %copy-start.32 = (f32[24,2304]{1,0:T(8,128)S(1)}, f32[24,2304]{1,0:T(8,128)}, u32[]{:S(2)}) copy-start(f32[24,2304]{1,0:T(8,128)} %param.32) | copy-start | bytes 663556
  274.4 12.5 %collective-permute-start.42 = (bf16[24,2304]{1,0:T(8,128)(2,1)S(1)}, bf16[24,2304]{1,0:T(8,128)(2,1)S(1)}, u32[]{:S(2)}, u32[]{:S(2)}) collective-permute-start(bf16[24,2304]{1,0:T(8,128)(2,1)S(1)} %get-tuple-element.335), channel_id=1, source_target_pairs={{0,8},{1,9},{2,10},{3,11},{4,12},{5,13},{6,14},{7,15},{8,0},{9,1},... | collective-permute-start | bytes 331784 | tf_op jit(solution)/shard_map/ppermute | solution.py:540
  275.3 11.6 %collective-permute-start.43 = (bf16[24,2304]{1,0:T(8,128)(2,1)S(1)}, bf16[24,2304]{1,0:T(8,128)(2,1)S(1)}, u32[]{:S(2)}, u32[]{:S(2)}) collective-permute-start(bf16[24,2304]{1,0:T(8,128)(2,1)S(1)} %get-tuple-element.336), channel_id=1, source_target_pairs={{0,16},{1,17},{2,18},{3,19},{4,20},{5,21},{6,22},{7,23},{8,24},{9,... | collective-permute-start | bytes 331784 | tf_op jit(solution)/shard_map/ppermute | solution.py:540
  279.0 6.4 %collective-permute-start.54 = (f32[1,240]{1,0:T(1,128)S(1)}, f32[1,240]{1,0:T(1,128)S(1)}, u32[]{:S(2)}, u32[]{:S(2)}) collective-permute-start(f32[1,240]{1,0:T(1,128)S(1)} %get-tuple-element.398), channel_id=1, source_target_pairs={{0,24},{1,25},{2,26},{3,27},{4,28},{5,29},{6,30},{7,31},{8,16},{9,... | collective-permute-start | bytes 2888 | tf_op jit(solution)/shard_map/ppermute | solution.py:540
  280.0 6.3 %collective-permute-start.53 = (f32[1,240]{1,0:T(1,128)S(1)}, f32[1,240]{1,0:T(1,128)S(1)}, u32[]{:S(2)}, u32[]{:S(2)}) collective-permute-start(f32[1,240]{1,0:T(1,128)S(1)} %get-tuple-element.399), channel_id=1, source_target_pairs={{0,16},{1,17},{2,18},{3,19},{4,20},{5,21},{6,22},{7,23},{8,24},{9,... | collective-permute-start | bytes 2888 | tf_op jit(solution)/shard_map/ppermute | solution.py:540
  280.0 6.3 %collective-permute-start.52 = (f32[1,240]{1,0:T(1,128)S(1)}, f32[1,240]{1,0:T(1,128)S(1)}, u32[]{:S(2)}, u32[]{:S(2)}) collective-permute-start(f32[1,240]{1,0:T(1,128)S(1)} %get-tuple-element.397), channel_id=1, source_target_pairs={{0,8},{1,9},{2,10},{3,11},{4,12},{5,13},{6,14},{7,15},{8,0},{9,1},... | collective-permute-start | bytes 2888 | tf_op jit(solution)/shard_map/ppermute | solution.py:540
  285.3 6.5 %collective-permute-start.44 = (bf16[24,2304]{1,0:T(8,128)(2,1)S(1)}, bf16[24,2304]{1,0:T(8,128)(2,1)S(1)}, u32[]{:S(2)}, u32[]{:S(2)}) collective-permute-start(bf16[24,2304]{1,0:T(8,128)(2,1)S(1)} %get-tuple-element.337), channel_id=1, source_target_pairs={{0,24},{1,25},{2,26},{3,27},{4,28},{5,29},{6,30},{7,31},{8,16},{9,... | collective-permute-start | bytes 331784 | tf_op jit(solution)/shard_map/ppermute | solution.py:540
  (30 other events, 198.4 us)
